TPU v7x, 256 devices: a whole 4x4x8 slice. The times are simulated.
256 devices in a mesh: region: 16 (over x, y), shard: 16 (over z, core).
Axes of the slice: x: 4, y: 4, z: 8, core: 2. Of those that a mesh axis runs over, the one named last changes fastest.
Arguments:
- query_feats: bfloat16 [65536, 512], P(('region', 'shard')), may hold values from -6 to 6
- query_region: int32 [65536, 1], P(('region', 'shard')), may hold values from 0 to 15; in each aligned block of 256 rows (0 to 255, 256 to 511, ...) at most 32 rows name the same one
- neighbors: int32 [65536, 64], P(('region', 'shard')), may hold values from 0 to 1023
- latents: bfloat16 [16384, 512], P(('region', 'shard')), may hold values from -380 to 380
- w_query: bfloat16 [512, 512], replicated, may hold values from -0.25 to 0.25
- w_key: bfloat16 [512, 512], replicated, may hold values from -0.25 to 0.25
- w_value: bfloat16 [512, 512], replicated, may hold values from -0.25 to 0.25
- w_out: bfloat16 [512, 512], replicated, may hold values from -0.25 to 0.25
- norm_gain: float32 [512], replicated, may hold values from 0.1 to 1.9
- w_up: bfloat16 [512, 2048], replicated, may hold values from -0.25 to 0.25
- w_down: bfloat16 [2048, 512], replicated, may hold values from -0.125 to 0.125
Outputs:
- refined: bfloat16 [65536, 512], P(('region', 'shard'))
Inputs may be any that keep to these rules, and one draw needn't show every extreme that they name: `query_region`: among the queries of one device (aligned blocks of 256 rows) no region is named more than 32 times, a bound that some block reaches.
All inputs are finite; a program needn't handle non-finite values.
Results may differ from a plain program's by a relative error of at most 0.012.
The roundings to bfloat16 on the way count: a program that leaves them out, or rounds other values in their place, can miss the bound.
Values may be sent and summed in bfloat16 or wider, within the bound.
No kernel may reach another device: no remote copies, remote signals or barrier semaphores. Data moves between devices by JAX's collectives and lax.ppermute only.
A program may use at most 64 MiB of HBM per device.

v0:
```python
import jax
import jax.numpy as jnp
from jax import lax
from jax.sharding import PartitionSpec as P

HEADS = 4


def attend_block(query_proj, row_index, kv_table):
    slot_count, model_width = query_proj.shape
    table_rows = kv_table.shape[0]
    head_width = model_width // HEADS
    key_heads = kv_table[:, :model_width].reshape(table_rows, HEADS, head_width)
    value_heads = kv_table[:, model_width:].reshape(table_rows, HEADS, head_width)
    columns = jnp.arange(table_rows, dtype=jnp.int32)
    onehot = (row_index[:, :, None] == columns[None, None, :]).astype(jnp.bfloat16)
    counts = jnp.einsum(
        "skl,k->sl",
        onehot,
        jnp.ones((row_index.shape[1],), jnp.bfloat16),
        preferred_element_type=jnp.float32,
    )
    present = counts > 0.0
    scores = jnp.einsum(
        "shd,lhd->shl",
        query_proj.reshape(slot_count, HEADS, head_width),
        key_heads,
        preferred_element_type=jnp.float32,
    ) * head_width ** (-0.5)
    masked = jnp.where(present[:, None, :], scores, -jnp.inf)
    peak = jnp.max(masked, axis=2, keepdims=True)
    raised = jnp.where(present[:, None, :], jnp.exp(masked - peak), 0.0)
    total = jnp.sum(raised * counts[:, None, :], axis=2, keepdims=True)
    weights = (raised / total).astype(jnp.bfloat16)
    weighted = weights.astype(jnp.float32) * counts[:, None, :]
    mixed = jnp.einsum(
        "shl,lhd->shd", weighted, value_heads.astype(jnp.float32), precision=lax.Precision.HIGHEST
    )
    return mixed.reshape(slot_count, model_width).astype(jnp.bfloat16)


def refine_rows(features, row_index, kv_table, w_query, w_out, norm_gain, w_up, w_down):
    slot_count, model_width = features.shape
    neighbor_count = row_index.shape[1]
    query_proj = jnp.dot(features, w_query, preferred_element_type=jnp.float32).astype(jnp.bfloat16)
    block_rows = 128
    block_count = slot_count // block_rows

    def one_block(pair):
        return attend_block(pair[0], pair[1], kv_table)

    mixed = lax.map(
        one_block,
        (
            query_proj.reshape(block_count, block_rows, model_width),
            row_index.reshape(block_count, block_rows, neighbor_count),
        ),
    )
    mixed = mixed.reshape(slot_count, model_width)
    resid = features.astype(jnp.float32) + jnp.dot(mixed, w_out, preferred_element_type=jnp.float32)
    meansq = jnp.mean(resid * resid, axis=1, keepdims=True)
    normed = (resid * lax.rsqrt(meansq + 1e-05) * norm_gain).astype(jnp.bfloat16)
    hidden = jax.nn.gelu(
        jnp.dot(normed, w_up, preferred_element_type=jnp.float32), approximate=True
    ).astype(jnp.bfloat16)
    return (resid + jnp.dot(hidden, w_down, preferred_element_type=jnp.float32)).astype(
        jnp.bfloat16
    )


def project_both(token_rows, w_key, w_value):
    key_part = jnp.dot(token_rows, w_key, preferred_element_type=jnp.float32).astype(jnp.bfloat16)
    value_part = jnp.dot(token_rows, w_value, preferred_element_type=jnp.float32).astype(
        jnp.bfloat16
    )
    return jnp.concatenate([key_part, value_part], axis=1)


def on_device(
    query_feats,
    query_region,
    neighbors,
    latents,
    w_query,
    w_key,
    w_value,
    w_out,
    norm_gain,
    w_up,
    w_down,
):
    region_count = lax.axis_size("region")
    query_count, model_width = query_feats.shape
    neighbor_count = neighbors.shape[1]
    capacity = min(query_count, 2 * query_count // region_count)
    target = query_region[:, 0]
    onehot = (target[:, None] == jnp.arange(region_count, dtype=jnp.int32)[None, :]).astype(
        jnp.int32
    )
    earlier = jnp.cumsum(onehot, axis=0) - onehot
    position = jnp.sum(earlier * onehot, axis=1)
    slot_index = target * capacity + position
    send_feats = (
        jnp.zeros((region_count * capacity, model_width), jnp.bfloat16)
        .at[slot_index]
        .set(query_feats)
    )
    send_index = (
        jnp.zeros((region_count * capacity, neighbor_count), jnp.int32)
        .at[slot_index]
        .set(neighbors)
    )
    kv_table = project_both(lax.all_gather(latents, "shard", axis=0, tiled=True), w_key, w_value)
    recv_feats = lax.all_to_all(
        send_feats.reshape(region_count, capacity, model_width),
        "region",
        split_axis=0,
        concat_axis=0,
        tiled=True,
    )
    recv_index = lax.all_to_all(
        send_index.reshape(region_count, capacity, neighbor_count),
        "region",
        split_axis=0,
        concat_axis=0,
        tiled=True,
    )
    results = refine_rows(
        recv_feats.reshape(region_count * capacity, model_width),
        recv_index.reshape(region_count * capacity, neighbor_count),
        kv_table,
        w_query,
        w_out,
        norm_gain,
        w_up,
        w_down,
    )
    returned = lax.all_to_all(
        results.reshape(region_count, capacity, model_width),
        "region",
        split_axis=0,
        concat_axis=0,
        tiled=True,
    )
    return jnp.take(returned.reshape(region_count * capacity, model_width), slot_index, axis=0)


def solution(mesh):
    in_specs = (
        P(("region", "shard"), None),
        P(("region", "shard"), None),
        P(("region", "shard"), None),
        P(("region", "shard"), None),
        P(),
        P(),
        P(),
        P(),
        P(),
        P(),
        P(),
    )
    out_specs = P(("region", "shard"), None)
    return jax.shard_map(
        on_device, mesh=mesh, in_specs=in_specs, out_specs=out_specs, check_vma=False
    )
```

profile of v0, /device:TPU:1, one launch (start us, length us, event | category | flops | bytes accessed | tf_op | source)
XLA Modules:
  0.0 148.5 jit_solution(5529565379163913418)
XLA Ops:
  7.3 0.7 fusion.58
  8.8 0.9 copy.17
  9.7 0.8 fusion.57
  11.2 1.2 scatter_custom_fusion.1
  12.4 0.8 reshape.120
  13.3 7.6 %all-to-all-start.1 = ((s32[16,1,2048]{2,1,0:T(1,128)}), s32[16,1,2048]{2,1,0:T(1,128)S(1)}, u32[]{:S(2)}, u32[]{:S(2)}) async-start(s32[16,1,2048]{2,1,0:T(1,128)} %reshape.120), calls=%async_computation.1 | async-start | bytes 262144 | tf_op jit(solution)/shard_map/all_to_all | solution.py:121
  20.9 2.7 %scatter_custom_fusion = bf16[512,512]{1,0:T(8,128)(2,1)} fusion(s32[256]{0:T(256)S(1)} %bitcast.113, bf16[256,512]{1,0:T(8,128)(2,1)} %param.13, bf16[]{:T(256)} %constant.34.clone.1), kind=kCustom, calls=%fused_computation.59 | custom fusion | bytes 524800 | tf_op jit(solution)/shard_map/scatter | solution.py:106
  23.6 4.1 %all-to-all-done.1 = s32[16,1,2048]{2,1,0:T(1,128)S(1)} async-done(((s32[16,1,2048]{2,1,0:T(1,128)}), s32[16,1,2048]{2,1,0:T(1,128)S(1)}, u32[]{:S(2)}, u32[]{:S(2)}) %all-to-all-start.1) | async-done | bytes 131104 | tf_op jit(solution)/shard_map/all_to_all | solution.py:121
  27.7 3.6 %all-to-all-start = ((bf16[16,32,512]{2,1,0:T(8,128)(2,1)}), bf16[16,32,512]{2,1,0:T(8,128)(2,1)S(1)}, u32[]{:S(2)}, u32[]{:S(2)}) async-start(bf16[16,32,512]{2,1,0:T(8,128)(2,1)} %bitcast.12), calls=%async_computation | async-start | bytes 1048576 | tf_op jit(solution)/shard_map/all_to_all | solution.py:114
  31.8 0.9 reduce.4
  32.8 0.8 reshape.121
  33.6 6.9 %all-to-all-done = bf16[16,32,512]{2,1,0:T(8,128)(2,1)S(1)} async-done(((bf16[16,32,512]{2,1,0:T(8,128)(2,1)}), bf16[16,32,512]{2,1,0:T(8,128)(2,1)S(1)}, u32[]{:S(2)}, u32[]{:S(2)}) %all-to-all-start) | async-done | bytes 524320 | tf_op jit(solution)/shard_map/all_to_all | solution.py:114
  40.5 1.2 convolution_convert_fusion.2
  41.7 10.2 %all-gather.2.cloned.1.call-done = bf16[1024,512]{1,0:T(8,128)(2,1)} async-done(((bf16[64,512]{1,0:T(8,128)(2,1)}), bf16[1024,512]{1,0:T(8,128)(2,1)}) %all-gather.2.cloned.1.call-update) | async-done | bytes 1048592 | tf_op jit(solution)/shard_map/all_gather | solution.py:113
  51.9 3.0 %convolution_convert_fusion = bf16[1024,512]{1,0:T(8,128)(2,1)} fusion(bf16[1024,512]{1,0:T(8,128)(2,1)} %all-gather.2.cloned.1.call-done, bf16[512,512]{1,0:T(8,128)(2,1)} %param.19), kind=kOutput, calls=%fused_computation.48 | convolution fusion | flops 537395200 | bytes 2621440 | tf_op jit(solution)/shard_map/dot_general | solution.py:73
  55.0 1.5 copy.19
  56.5 3.1 %convolution_convert_fusion.1 = bf16[1024,512]{1,0:T(8,128)(2,1)} fusion(bf16[1024,512]{1,0:T(8,128)(2,1)} %all-gather.2.cloned.1.call-done, bf16[512,512]{1,0:T(8,128)(2,1)} %param.18), kind=kOutput, calls=%fused_computation.49 | convolution fusion | flops 537395200 | bytes 2621440 | tf_op jit(solution)/shard_map/dot_general | solution.py:72
  59.5 56.2 %while.10 = (s32[]{:T(128)}, bf16[4,128,512]{2,1,0:T(8,128)(2,1)}, s32[4,128,64]{2,1,0:T(8,128)}, bf16[4,128,512]{2,1,0:T(8,128)(2,1)}, bf16[1024,512]{1,0:T(8,1...) while((s32[]{:T(128)}, bf16[4,128,512]{2,1,0:T(8,128)(2,1)}, s32[4,128,64]{2,1,0:T(8,128)}, ...), condition=%wide.region_8.9_spmd, body=%wide.region_5.8_spmd.sunk | while | flops 970656768 | bytes 17400404 | solution.py:52
  59.5 0.9 constant_dynamic-slice_fusion.2
  60.6 1.7 %fusion.96 = f32[4,128,1024]{2,1,0:T(8,128)S(1)} fusion(bf16[128,4,128]{0,2,1:T(8,128)(2,1)S(1)} %bitcast.100, bf16[1024,512]{1,0:T(8,128)(2,1)} %get-tuple-element.121), kind=kOutput, calls=%fused_computation.21.clone.1 | convolution fusion | flops 134217728 | bytes 3276800 | tf_op jit(solution)/shard_map/while/body/eval_jaxpr/shd,lhd->shl/dot_general | solution.py:24
  62.3 0.9 dynamic-slice_bitcast_fusion.2
  63.1 6.9 %fusion.97 = f32[1,128,1024]{2,0,1:T(1,128)S(1)} fusion(s32[128,64]{1,0:T(8,128)S(1)} %dynamic-slice_bitcast_fusion.2), kind=kOutput, calls=%fused_computation.6.clone.1 | convolution fusion | flops 25165824 | bytes 557056 | tf_op jit(solution)/shard_map/while/body/eval_jaxpr/skl,k->sl/dot_general | solution.py:17
  70.2 0.9 fusion.98
  71.5 1.3 fusion.99
  73.6 0.9 constant_dynamic-slice_fusion.2
  74.6 1.7 %fusion.96 = f32[4,128,1024]{2,1,0:T(8,128)S(1)} fusion(bf16[128,4,128]{0,2,1:T(8,128)(2,1)S(1)} %bitcast.100, bf16[1024,512]{1,0:T(8,128)(2,1)} %get-tuple-element.121), kind=kOutput, calls=%fused_computation.21.clone.1 | convolution fusion | flops 134217728 | bytes 3276800 | tf_op jit(solution)/shard_map/while/body/eval_jaxpr/shd,lhd->shl/dot_general | solution.py:24
  76.3 0.9 dynamic-slice_bitcast_fusion.2
  77.2 6.9 %fusion.97 = f32[1,128,1024]{2,0,1:T(1,128)S(1)} fusion(s32[128,64]{1,0:T(8,128)S(1)} %dynamic-slice_bitcast_fusion.2), kind=kOutput, calls=%fused_computation.6.clone.1 | convolution fusion | flops 25165824 | bytes 557056 | tf_op jit(solution)/shard_map/while/body/eval_jaxpr/skl,k->sl/dot_general | solution.py:17
  84.2 0.9 fusion.98
  85.5 1.3 fusion.99
  87.6 0.9 constant_dynamic-slice_fusion.2
  88.7 1.7 %fusion.96 = f32[4,128,1024]{2,1,0:T(8,128)S(1)} fusion(bf16[128,4,128]{0,2,1:T(8,128)(2,1)S(1)} %bitcast.100, bf16[1024,512]{1,0:T(8,128)(2,1)} %get-tuple-element.121), kind=kOutput, calls=%fused_computation.21.clone.1 | convolution fusion | flops 134217728 | bytes 3276800 | tf_op jit(solution)/shard_map/while/body/eval_jaxpr/shd,lhd->shl/dot_general | solution.py:24
  90.4 0.9 dynamic-slice_bitcast_fusion.2
  91.2 6.9 %fusion.97 = f32[1,128,1024]{2,0,1:T(1,128)S(1)} fusion(s32[128,64]{1,0:T(8,128)S(1)} %dynamic-slice_bitcast_fusion.2), kind=kOutput, calls=%fused_computation.6.clone.1 | convolution fusion | flops 25165824 | bytes 557056 | tf_op jit(solution)/shard_map/while/body/eval_jaxpr/skl,k->sl/dot_general | solution.py:17
  98.3 0.9 fusion.98
  99.6 1.3 fusion.99
  101.7 0.9 constant_dynamic-slice_fusion.2
  102.7 1.7 %fusion.96 = f32[4,128,1024]{2,1,0:T(8,128)S(1)} fusion(bf16[128,4,128]{0,2,1:T(8,128)(2,1)S(1)} %bitcast.100, bf16[1024,512]{1,0:T(8,128)(2,1)} %get-tuple-element.121), kind=kOutput, calls=%fused_computation.21.clone.1 | convolution fusion | flops 134217728 | bytes 3276800 | tf_op jit(solution)/shard_map/while/body/eval_jaxpr/shd,lhd->shl/dot_general | solution.py:24
  104.4 0.9 dynamic-slice_bitcast_fusion.2
  105.3 6.9 %fusion.97 = f32[1,128,1024]{2,0,1:T(1,128)S(1)} fusion(s32[128,64]{1,0:T(8,128)S(1)} %dynamic-slice_bitcast_fusion.2), kind=kOutput, calls=%fused_computation.6.clone.1 | convolution fusion | flops 25165824 | bytes 557056 | tf_op jit(solution)/shard_map/while/body/eval_jaxpr/skl,k->sl/dot_general | solution.py:17
  112.3 0.9 fusion.98
  113.6 1.3 fusion.99
  115.7 1.9 %multiply_reduce_fusion.1 = (f32[512]{0:T(512)S(1)}, f32[512,512]{1,0:T(8,128)S(1)}) fusion(bf16[512,512]{1,0:T(8,128)(2,1)} %bitcast.109, bf16[512,512]{1,0:T(8,128)(2,1)} %param.20, bf16[512,512]{1,0:T(8,128)(2,1)} %bitcast.104), kind=kOutput, calls=%fused_computation.55 | convolution fusion | flops 269483520 | bytes 2623488 | tf_op jit(solution)/shard_map/dot_general | solution.py:60
  117.6 5.1 %fusion.43 = bf16[512,512]{1,0:T(8,128)(2,1)} fusion(f32[512,512]{1,0:T(8,128)S(1)} %get-tuple-element.65, bf16[2048,512]{1,0:T(8,128)(2,1)S(1)} %copy-done, bf16[512,2048]{1,0:T(8,128)(2,1)} %param.22, f32[512]{0:T(512)S(1)} %copy-done.3, f32[512]{0:T(512)S(1)} %add_rsqrt_fusion), kind=kOutput, calls=%fused_computation.52 | convolution fusion | flops 2158231552 | bytes 5771264 | tf_op jit(solution)/shard_map/dot_general | solution.py:66
  122.7 6.7 %all-to-all-start.2 = ((bf16[16,32,512]{2,1,0:T(8,128)(2,1)}), bf16[16,32,512]{2,1,0:T(8,128)(2,1)S(1)}, u32[]{:S(2)}, u32[]{:S(2)}) async-start(bf16[16,32,512]{2,1,0:T(8,128)(2,1)} %bitcast.108), calls=%async_computation.2 | async-start | bytes 1048576 | tf_op jit(solution)/shard_map/all_to_all | solution.py:138
  129.4 10.3 %all-to-all-done.2 = bf16[16,32,512]{2,1,0:T(8,128)(2,1)S(1)} async-done(((bf16[16,32,512]{2,1,0:T(8,128)(2,1)}), bf16[16,32,512]{2,1,0:T(8,128)(2,1)S(1)}, u32[]{:S(2)}, u32[]{:S(2)}) %all-to-all-start.2) | async-done | bytes 524320 | tf_op jit(solution)/shard_map/all_to_all | solution.py:138
  139.7 1.2 gather_fusion
  140.8 0.8 broadcast_select_fusion
  (43 shorter events, 8.5 us)
Async XLA Ops:
  6.5 111.1 %copy-start = (bf16[2048,512]{1,0:T(8,128)(2,1)S(1)}, bf16[2048,512]{1,0:T(8,128)(2,1)}, u32[]{:S(2)}) copy-start(bf16[2048,512]{1,0:T(8,128)(2,1)} %param.23) | copy-start | bytes 6291460
  6.5 33.9 %copy-start.2 = (bf16[512,512]{1,0:T(8,128)(2,1)S(1)}, bf16[512,512]{1,0:T(8,128)(2,1)}, u32[]{:S(2)}) copy-start(bf16[512,512]{1,0:T(8,128)(2,1)} %param.17) | copy-start | bytes 1572868
  6.5 45.4 %all-gather.2.cloned.1.call-start = ((), (), s32[]{:S(2)}) async-start(), calls=%async_computation.3 | async-start | bytes 1114112 | tf_op jit(solution)/shard_map/all_gather | solution.py:113
  13.3 14.5 %all-to-all-start.1 = ((s32[16,1,2048]{2,1,0:T(1,128)}), s32[16,1,2048]{2,1,0:T(1,128)S(1)}, u32[]{:S(2)}, u32[]{:S(2)}) async-start(s32[16,1,2048]{2,1,0:T(1,128)} %reshape.120), calls=%async_computation.1 | async-start | bytes 262144 | tf_op jit(solution)/shard_map/all_to_all | solution.py:121
  27.7 12.7 %all-to-all-start = ((bf16[16,32,512]{2,1,0:T(8,128)(2,1)}), bf16[16,32,512]{2,1,0:T(8,128)(2,1)S(1)}, u32[]{:S(2)}, u32[]{:S(2)}) async-start(bf16[16,32,512]{2,1,0:T(8,128)(2,1)} %bitcast.12), calls=%async_computation | async-start | bytes 1048576 | tf_op jit(solution)/shard_map/all_to_all | solution.py:114
  40.5 11.5 %copy-start.1 = (bf16[16,32,512]{2,1,0:T(8,128)(2,1)}, bf16[16,32,512]{2,1,0:T(8,128)(2,1)S(1)}, u32[]{:S(2)}) copy-start(bf16[16,32,512]{2,1,0:T(8,128)(2,1)S(1)} %all-to-all-done) | copy-start | bytes 1572868
  115.7 1.9 %copy-start.3 = (f32[512]{0:T(512)S(1)}, f32[512]{0:T(512)}, u32[]{:S(2)}) copy-start(f32[512]{0:T(512)} %param.21) | copy-start | bytes 6148
  122.7 17.0 %all-to-all-start.2 = ((bf16[16,32,512]{2,1,0:T(8,128)(2,1)}), bf16[16,32,512]{2,1,0:T(8,128)(2,1)S(1)}, u32[]{:S(2)}, u32[]{:S(2)}) async-start(bf16[16,32,512]{2,1,0:T(8,128)(2,1)} %bitcast.108), calls=%async_computation.2 | async-start | bytes 1048576 | tf_op jit(solution)/shard_map/all_to_all | solution.py:138
Sparse Core Ops, SparseCore 0:
  9.2 42.6 all-gather.1
where the time goes:
time: 150 us; the launch traced here: 148 us
  matrix products  53.9 us (36%)
  waiting for transfers between devices  32.2 us (21%)
  local copies, waits for them, and re-layouts  20.9 us (14%)
  starting transfers between devices  17.8 us (12%)
  between operations  13.5 us (9%)
  other arithmetic  9.96 us (7%)
    dot_general x4, matrix products, attend_block(): jnp.einsum('skl,k->sl', onehot, jnp.ones((row_index.shape[1],), jnp.bfloa...  27.5 us
    all_to_all x1, waiting for transfers between devices, on_device(): lax.all_to_all(results.reshape(region_count, capacity, model_width), 'reg...  10.3 us
    all_gather x1, waiting for transfers between devices, on_device(): lax.all_gather(latents, 'shard', axis=0, tiled=True)  10.2 us
    all_to_all x1, starting transfers between devices, on_device(): lax.all_to_all(send_index.reshape(region_count, capacity, neighbor_count)...  7.58 us
    all_to_all x1, waiting for transfers between devices, on_device(): lax.all_to_all(send_feats.reshape(region_count, capacity, model_width), '...  6.86 us
    dot_general x4, matrix products, attend_block(): jnp.einsum('shd,lhd->shl', query_proj.reshape(slot_count, HEADS, head_wid...  6.85 us
    all_to_all x1, starting transfers between devices, on_device(): lax.all_to_all(results.reshape(region_count, capacity, model_width), 'reg...  6.69 us
    dot_general x4, matrix products, attend_block(): jnp.einsum('shl,lhd->shd', weighted, value_heads.astype(jnp.float32), pre...  5.19 us
  transfers between devices with their start and end apart: 4, of which 4 were waited for; matrix products, arithmetic and copies ran while one was open for 8% of the time, Pallas kernels for 0%

commit v1 on v0

v1 whole, which is shorter than its diff:
```python
import functools
import math

import jax
import jax.numpy as jnp
from jax import lax
from jax.experimental import pallas as pl
from jax.experimental.pallas import tpu as pltpu
from jax.sharding import PartitionSpec as P

HEADS = 4
LANES = 128
ABSENT = -1e30
F32 = jnp.float32
BF16 = jnp.bfloat16
VMEM = pl.BlockSpec(memory_space=pltpu.VMEM)
NT = (((1,), (1,)), ((), ()))


def slots_of(region_row, region_count, capacity):
    rows = region_row.shape[1]
    onehot = (lax.broadcasted_iota(jnp.int32, (region_count, rows), 0) == region_row).astype(F32)
    earlier_than = lax.broadcasted_iota(jnp.int32, (rows, rows), 0) < lax.broadcasted_iota(
        jnp.int32, (rows, rows), 1
    )
    earlier = jnp.dot(onehot.astype(BF16), earlier_than.astype(BF16), preferred_element_type=F32)
    rank = jnp.sum(earlier * onehot, axis=0, keepdims=True)
    return region_row.astype(F32) * float(capacity) + rank


def pack_kernel(region_count, capacity, feats_ref, region_ref, neighbors_ref, w_query_ref, send_ref):
    slot_count = region_count * capacity
    rows, width = feats_ref.shape
    neighbor_count = neighbors_ref.shape[0]
    slot_row = slots_of(region_ref[...], region_count, capacity)
    place = (
        lax.broadcasted_iota(jnp.int32, (slot_count, rows), 0).astype(F32) == slot_row
    ).astype(BF16)
    query = jnp.dot(feats_ref[...], w_query_ref[...], preferred_element_type=F32).astype(BF16)
    send_ref[:, :width] = jnp.dot(place, query, preferred_element_type=F32).astype(BF16)
    number = neighbors_ref[...]
    coded = ((number & 127) + 128) << (number >> 7)
    coded = coded.astype(F32).astype(BF16)
    spread = lax.dot_general(place, coded, NT, preferred_element_type=F32).astype(BF16)
    filler = jnp.zeros((slot_count, send_ref.shape[1] - width - neighbor_count), BF16)
    send_ref[:, width:] = jnp.concatenate([spread, filler], axis=1)


def count_kernel(neighbor_count, received_ref, logcount_ref, low_ref, digit_ref):
    slot_count = logcount_ref.shape[1]
    coded = received_ref[...].astype(F32)
    for block in range(slot_count // LANES):
        part = jnp.transpose(coded[block * LANES : (block + 1) * LANES])[:neighbor_count]
        high = jnp.zeros(part.shape, jnp.int32)
        for power in range(1, 8):
            high += (part >= float(128 << power)).astype(jnp.int32)
        value = part.astype(jnp.int32)
        low_ref[block] = (value >> high) - 128
        digit_ref[block] = jnp.int32(1) << (4 * high)

    def one(step, carry):
        block, half = step // 2, step % 2
        base = half * 64
        lanes = pl.ds(pl.multiple_of(block * LANES, LANES), LANES)
        rows = lax.broadcasted_iota(jnp.int32, (64, LANES), 0) + base
        even = jnp.zeros((64, LANES), jnp.int32)
        odd = jnp.zeros((64, LANES), jnp.int32)
        for first in range(0, neighbor_count, 13):
            total = jnp.zeros((64, LANES), jnp.int32)
            for k in range(first, min(first + 13, neighbor_count)):
                same = low_ref[block, k : k + 1, :] == rows
                total = total + jnp.where(same, digit_ref[block, k : k + 1, :], 0)
            even = even + (total & 0x0F0F0F0F)
            odd = odd + ((total >> 4) & 0x0F0F0F0F)
        for high in range(8):
            field = ((odd if high % 2 else even) >> (8 * (high // 2))) & 0xFF
            logs = jnp.where(field > 0, jnp.log2(field.astype(F32)), ABSENT)
            target = pl.ds(pl.multiple_of(high * LANES + base, 64), 64)
            logcount_ref[target, lanes] = logs
        return carry

    lax.fori_loop(0, slot_count // LANES * 2, one, 0)


def attend_kernel(
    query_ref, logcount_ref, near_ref, far_ref, w_key_ref, w_value_ref, mixed_ref, token_ref, key_ref, value_ref
):
    slot_count, width = query_ref.shape
    head_width = width // HEADS
    half_rows = near_ref.shape[0]
    chips = half_rows // 64
    place = lax.axis_index("shard")
    chip, core = place // 2, place % 2
    for step in range(chips):
        origin = lax.rem(chip - step + chips, chips) * 2
        piece = slice(step * 64, step * 64 + 64)
        token_ref[pl.ds(pl.multiple_of((origin + core) * 64, 64), 64), :] = near_ref[piece, :]
        token_ref[pl.ds(pl.multiple_of((origin + 1 - core) * 64, 64), 64), :] = far_ref[piece, :]
    tokens = token_ref[...]
    key_ref[...] = jnp.dot(tokens, w_key_ref[...], preferred_element_type=F32).astype(BF16)
    value_ref[...] = lax.dot_general(
        w_value_ref[...], tokens, (((0,), (1,)), ((), ())), preferred_element_type=F32
    ).astype(BF16)
    factor = head_width ** (-0.5) * math.log2(math.e)
    size = 256
    for block in range(slot_count // size):
        rows = slice(block * size, (block + 1) * size)
        for head in range(HEADS):
            columns = slice(head * head_width, (head + 1) * head_width)
            scores = lax.dot_general(
                key_ref[:, columns], query_ref[rows, columns], NT, preferred_element_type=F32
            )
            scores = scores * factor + logcount_ref[:, rows]
            peak = jnp.max(scores, axis=0, keepdims=True)
            raised = jnp.exp2(scores - peak)
            total = jnp.sum(raised, axis=0, keepdims=True)
            mixed = jnp.dot(value_ref[columns, :], raised.astype(BF16), preferred_element_type=F32)
            mixed_ref[rows, columns] = jnp.transpose(mixed / total).astype(BF16)


def finish_kernel(
    region_count,
    capacity,
    feats_ref,
    region_ref,
    returned_ref,
    w_out_ref,
    gain_ref,
    w_up_ref,
    w_down_ref,
    refined_ref,
):
    rows = feats_ref.shape[0]
    slot_count = region_count * capacity
    slot_row = slots_of(region_ref[...], region_count, capacity)
    slot_column = jnp.transpose(jnp.broadcast_to(slot_row, (LANES, rows)))
    pick = jnp.concatenate(
        [
            (lax.broadcasted_iota(jnp.int32, (rows, LANES), 1) + first).astype(F32) == slot_column
            for first in range(0, slot_count, LANES)
        ],
        axis=1,
    ).astype(BF16)
    mixed = jnp.dot(pick, returned_ref[...], preferred_element_type=F32).astype(BF16)
    resid = feats_ref[...].astype(F32) + jnp.dot(
        mixed, w_out_ref[...], preferred_element_type=F32
    )
    meansq = jnp.mean(resid * resid, axis=1, keepdims=True)
    normed = (resid * lax.rsqrt(meansq + 1e-05) * gain_ref[...]).astype(BF16)
    hidden = jax.nn.gelu(
        jnp.dot(normed, w_up_ref[...], preferred_element_type=F32), approximate=True
    ).astype(BF16)
    refined_ref[...] = (
        resid + jnp.dot(hidden, w_down_ref[...], preferred_element_type=F32)
    ).astype(BF16)


def params(mebibytes):
    return pltpu.CompilerParams(vmem_limit_bytes=mebibytes << 20)


def on_device(
    query_feats,
    query_region,
    neighbors,
    latents,
    w_query,
    w_key,
    w_value,
    w_out,
    norm_gain,
    w_up,
    w_down,
):
    region_count = lax.axis_size("region")
    shard_count = lax.axis_size("shard")
    chips = shard_count // 2
    query_count, width = query_feats.shape
    neighbor_count = neighbors.shape[1]
    capacity = min(query_count, 2 * query_count // region_count)
    slot_count = region_count * capacity
    wide = width + LANES
    table_rows = latents.shape[0] * shard_count
    region_row = query_region.reshape(1, query_count)

    def ring(step):
        return [
            (chip * 2 + core, (chip + step) % chips * 2 + core)
            for chip in range(chips)
            for core in range(2)
        ]

    pieces = [latents] + [lax.ppermute(latents, "shard", ring(step)) for step in range(1, chips)]
    send = pl.pallas_call(
        functools.partial(pack_kernel, region_count, capacity),
        out_shape=jax.ShapeDtypeStruct((slot_count, wide), BF16),
        in_specs=[VMEM] * 4,
        out_specs=VMEM,
        compiler_params=params(12),
        name="pack",
    )(query_feats, region_row, neighbors.T, w_query)
    received = lax.all_to_all(
        send.reshape(region_count, capacity, wide), "region", split_axis=0, concat_axis=0, tiled=True
    ).reshape(slot_count, wide)
    near = jnp.concatenate(pieces, axis=0)
    far = lax.ppermute(
        near, "shard", [(place, place + 1 - 2 * (place % 2)) for place in range(shard_count)]
    )
    logcount = pl.pallas_call(
        functools.partial(count_kernel, neighbor_count),
        grid=(1,),
        out_shape=jax.ShapeDtypeStruct((table_rows, slot_count), F32),
        in_specs=[pl.BlockSpec((slot_count, LANES), lambda i: (0, width // LANES))],
        out_specs=pl.BlockSpec((table_rows, slot_count), lambda i: (0, 0)),
        scratch_shapes=[
            pltpu.VMEM((slot_count // LANES, neighbor_count, LANES), jnp.int32),
            pltpu.VMEM((slot_count // LANES, neighbor_count, LANES), jnp.int32),
        ],
        compiler_params=params(12),
        name="count",
    )(received)
    mixed = pl.pallas_call(
        attend_kernel,
        grid=(1,),
        out_shape=jax.ShapeDtypeStruct((slot_count, width), BF16),
        in_specs=[
            pl.BlockSpec((slot_count, width), lambda i: (0, 0)),
            pl.BlockSpec((table_rows, slot_count), lambda i: (0, 0)),
            pl.BlockSpec(near.shape, lambda i: (0, 0)),
            pl.BlockSpec(near.shape, lambda i: (0, 0)),
            pl.BlockSpec(w_key.shape, lambda i: (0, 0)),
            pl.BlockSpec(w_value.shape, lambda i: (0, 0)),
        ],
        out_specs=pl.BlockSpec((slot_count, width), lambda i: (0, 0)),
        scratch_shapes=[
            pltpu.VMEM((table_rows, width), BF16),
            pltpu.VMEM((table_rows, width), BF16),
            pltpu.VMEM((width, table_rows), BF16),
        ],
        compiler_params=params(32),
        name="attend",
    )(received, logcount, near, far, w_key, w_value)
    returned = lax.all_to_all(
        mixed.reshape(region_count, capacity, width), "region", split_axis=0, concat_axis=0, tiled=True
    ).reshape(slot_count, width)
    return pl.pallas_call(
        functools.partial(finish_kernel, region_count, capacity),
        out_shape=jax.ShapeDtypeStruct((query_count, width), BF16),
        in_specs=[VMEM] * 7,
        out_specs=VMEM,
        compiler_params=params(24),
        name="finish",
    )(query_feats, region_row, returned, w_out, norm_gain.reshape(1, width), w_up, w_down)


def solution(mesh):
    in_specs = (P(("region", "shard"), None),) * 4 + (P(),) * 7
    out_specs = P(("region", "shard"), None)
    return jax.shard_map(
        on_device, mesh=mesh, in_specs=in_specs, out_specs=out_specs, check_vma=False
    )
```

time: 150 us -> 69.8 us (0.47)
  matrix products: 53.9 us -> 0 us
  waiting for transfers between devices: 32.2 us -> 7.17 us
  local copies, waits for them, and re-layouts: 20.9 us -> 3.61 us
  blocking collectives: 0 us -> 16.9 us
  Pallas kernels: 0 us -> 14.5 us
  between operations: 13.5 us -> 0.23 us
  other arithmetic: 9.96 us -> 0 us
  starting transfers between devices: 17.8 us -> 26.1 us
    dot_general x17 -> x0, matrix products: 53.9 us -> none  [the longest x4 27.5 us: attend_block(): jnp.einsum('skl,k->sl', onehot, jnp.ones((row_index.shape[1],), jnp.bfloa...]
    all_to_all x3 -> x1, waiting for transfers between devices: 21.3 us -> 0.01 us  [on_device(): lax.all_to_all(send.reshape(region_count, capacity, wide), 'region', spli...]
    ppermute x0 -> x8, starting transfers between devices: none -> 19.3 us  [the longest x7 15.5 us: on_device(): lax.ppermute(latents, 'shard', ring(step))]
    all_to_all x0 -> x1, blocking collectives: none -> 16.9 us  [on_device(): lax.all_to_all(mixed.reshape(region_count, capacity, width), 'region', sp...]
    pallas_call x0 -> x4, Pallas kernels: none -> 14.5 us  [the longest x1 7.21 us: on_device(): pl.pallas_call(attend_kernel, grid=(1,), out_shape=jax.ShapeDtypeStruct((...]
    all_to_all x3 -> x1, starting transfers between devices: 17.8 us -> 6.76 us  [on_device(): lax.all_to_all(send.reshape(region_count, capacity, wide), 'region', spli...]
    all_gather x1 -> x0, waiting for transfers between devices: 10.2 us -> none  [on_device(): lax.all_gather(latents, 'shard', axis=0, tiled=True)]
    ppermute x0 -> x8, waiting for transfers between devices: none -> 7.17 us  [the longest x7 7.17 us: on_device(): lax.ppermute(latents, 'shard', ring(step))]
  transfers between devices with their start and end apart: 4 -> 9, of which waited for: 4 -> 2; matrix products, arithmetic and copies ran while one was open for 8% -> 0% of each run, Pallas kernels for 0% -> 6%
where the time goes in v1:
time: 69.8 us; the launch traced here: 68.5 us
  starting transfers between devices  26.1 us (37%)
  blocking collectives  16.9 us (24%)
  Pallas kernels  14.5 us (21%)
  waiting for transfers between devices  7.17 us (10%)
  local copies, waits for them, and re-layouts  3.61 us (5%)
    all_to_all x1, blocking collectives, on_device(): lax.all_to_all(mixed.reshape(region_count, capacity, width), 'region', sp...  16.9 us
    ppermute x7, starting transfers between devices, on_device(): lax.ppermute(latents, 'shard', ring(step))  15.5 us
    pallas_call x1, Pallas kernels, on_device(): pl.pallas_call(attend_kernel, grid=(1,), out_shape=jax.ShapeDtypeStruct((...  7.21 us
    ppermute x7, waiting for transfers between devices, on_device(): lax.ppermute(latents, 'shard', ring(step))  7.17 us
    all_to_all x1, starting transfers between devices, on_device(): lax.all_to_all(send.reshape(region_count, capacity, wide), 'region', spli...  6.76 us
    ppermute x1, starting transfers between devices, on_device(): lax.ppermute(near, 'shard', [(place, place + 1 - 2 * (place % 2)) for pla...  3.81 us
    unnamed x33, local copies, waits for them, and re-layouts  3.61 us
    pallas_call x1, Pallas kernels, on_device(): pl.pallas_call(functools.partial(finish_kernel, region_count, capacity),...  2.96 us
  transfers between devices with their start and end apart: 9, of which 2 were waited for; matrix products, arithmetic and copies ran while one was open for 0% of the time, Pallas kernels for 6%

profile of v1, /device:TPU:1, one launch (start us, length us, event | category | flops | bytes accessed | tf_op | source)
XLA Modules:
  0.0 68.5 jit_solution(8683842560085100748)
XLA Ops:
  0.0 6.8 %collective-permute-start.5 = (bf16[64,512]{1,0:T(8,128)(2,1)}, bf16[64,512]{1,0:T(8,128)(2,1)S(1)}, u32[]{:S(2)}, u32[]{:S(2)}) collective-permute-start(bf16[64,512]{1,0:T(8,128)(2,1)} %param.14), channel_id=1, source_target_pairs={{0,12},{1,13},{2,14},{3,15},{4,0},{5,1},{6,2},{7,3},{8,4},{9,5},{1... | collective-permute-start | bytes 196616 | tf_op jit(solution)/shard_map/ppermute | solution.py:193
  6.9 0.7 %collective-permute-start.4 = (bf16[64,512]{1,0:T(8,128)(2,1)}, bf16[64,512]{1,0:T(8,128)(2,1)S(1)}, u32[]{:S(2)}, u32[]{:S(2)}) collective-permute-start(bf16[64,512]{1,0:T(8,128)(2,1)} %param.14), channel_id=1, source_target_pairs={{0,10},{1,11},{2,12},{3,13},{4,14},{5,15},{6,0},{7,1},{8,2},{9,3},... | collective-permute-start | bytes 196616 | tf_op jit(solution)/shard_map/ppermute | solution.py:193
  7.6 4.2 %collective-permute-start.3 = (bf16[64,512]{1,0:T(8,128)(2,1)}, bf16[64,512]{1,0:T(8,128)(2,1)S(1)}, u32[]{:S(2)}, u32[]{:S(2)}) collective-permute-start(bf16[64,512]{1,0:T(8,128)(2,1)} %param.14), channel_id=1, source_target_pairs={{0,8},{1,9},{2,10},{3,11},{4,12},{5,13},{6,14},{7,15},{8,0},{9,1},... | collective-permute-start | bytes 196616 | tf_op jit(solution)/shard_map/ppermute | solution.py:193
  11.8 0.0 collective-permute-start.2
  11.8 1.4 %collective-permute-start = (bf16[64,512]{1,0:T(8,128)(2,1)}, bf16[64,512]{1,0:T(8,128)(2,1)S(1)}, u32[]{:S(2)}, u32[]{:S(2)}) collective-permute-start(bf16[64,512]{1,0:T(8,128)(2,1)} %param.14), channel_id=1, source_target_pairs={{0,2},{1,3},{2,4},{3,5},{4,6},{5,7},{6,8},{7,9},{8,10},{9,11},{10,... | collective-permute-start | bytes 196616 | tf_op jit(solution)/shard_map/ppermute | solution.py:193
  13.2 0.0 copy-start.2
  13.2 0.9 %copy-done.2 = bf16[256,512]{1,0:T(8,128)(2,1)S(1)} copy-done((bf16[256,512]{1,0:T(8,128)(2,1)S(1)}, bf16[256,512]{1,0:T(8,128)(2,1)}, u32[]{:S(2)}) %copy-start.2) | copy-done | bytes 262168
  14.2 0.0 copy-start.5
  14.2 1.0 %copy-done.5 = bf16[512,512]{1,0:T(8,128)(2,1)S(1)} copy-done((bf16[512,512]{1,0:T(8,128)(2,1)S(1)}, bf16[512,512]{1,0:T(8,128)(2,1)}, u32[]{:S(2)}) %copy-start.5) | copy-done | bytes 524312
  15.2 0.0 copy-start.8
  15.2 0.8 %copy-done.8 = s32[256,64]{0,1:T(8,128)S(1)} copy-done((s32[256,64]{0,1:T(8,128)S(1)}, s32[256,64]{0,1:T(8,128)}, u32[]{:S(2)}) %copy-start.8) | copy-done | bytes 65560
  16.1 0.0 copy-start.9
  16.1 0.7 copy-done.9
  16.7 1.5 %pack.1 = bf16[512,640]{1,0:T(8,128)(2,1)} custom-call(bf16[256,512]{1,0:T(8,128)(2,1)S(1)} %copy-done.2, s32[1,256]{1,0:T(1,128)S(1)} %bitcast.12, s32[64,256]{1,0:T(8,128)S(1)} %bitcast.11, bf16[512,512]{1,0:T(8,128)(2,1)S(1)} %copy-done.5), custom_call_target="tpu_custom_call" | custom-call | tf_op jit(solution)/shard_map/pack/pallas_call | solution.py:194
  18.3 6.8 %all-to-all-start = ((bf16[16,32,640]{2,1,0:T(8,128)(2,1)}), bf16[16,32,640]{2,1,0:T(8,128)(2,1)S(1)}, u32[]{:S(2)}, u32[]{:S(2)}) async-start(bf16[16,32,640]{2,1,0:T(8,128)(2,1)} %bitcast.2), calls=%async_computation | async-start | bytes 1310720 | tf_op jit(solution)/shard_map/all_to_all | solution.py:202
  25.0 0.0 copy-done.12
  25.0 0.0 copy-start.6
  25.1 0.0 copy-start.7
  25.1 0.0 collective-permute-done
  25.1 2.2 %collective-permute-start.1 = (bf16[64,512]{1,0:T(8,128)(2,1)S(1)}, bf16[64,512]{1,0:T(8,128)(2,1)S(1)}, u32[]{:S(2)}, u32[]{:S(2)}) collective-permute-start(bf16[64,512]{1,0:T(8,128)(2,1)S(1)} %copy-done.12), channel_id=1, source_target_pairs={{0,4},{1,5},{2,6},{3,7},{4,8},{5,9},{6,10},{7,11},{8,12},{9,13},{1... | collective-permute-start | bytes 196616 | tf_op jit(solution)/shard_map/ppermute | solution.py:193
  27.3 3.7 %collective-permute-done.1 = bf16[64,512]{1,0:T(8,128)(2,1)S(1)} collective-permute-done((bf16[64,512]{1,0:T(8,128)(2,1)S(1)}, bf16[64,512]{1,0:T(8,128)(2,1)S(1)}, u32[]{:S(2)}, u32[]{:S(2)}) %collective-permute-start.1) | collective-permute-done | bytes 65568 | tf_op jit(solution)/shard_map/ppermute | solution.py:193
  30.9 0.1 collective-permute-start.6
  31.1 0.0 collective-permute-done.2
  31.1 0.0 collective-permute-done.3
  31.1 0.0 collective-permute-done.4
  31.1 0.0 collective-permute-done.5
  31.2 3.5 %collective-permute-done.6 = bf16[64,512]{1,0:T(8,128)(2,1)S(1)} collective-permute-done((bf16[64,512]{1,0:T(8,128)(2,1)S(1)}, bf16[64,512]{1,0:T(8,128)(2,1)S(1)}, u32[]{:S(2)}, u32[]{:S(2)}) %collective-permute-start.6) | collective-permute-done | bytes 65568 | tf_op jit(solution)/shard_map/ppermute | solution.py:193
  34.7 3.8 %collective-permute-start.7 = (bf16[512,512]{1,0:T(8,128)(2,1)S(1)}, bf16[512,512]{1,0:T(8,128)(2,1)S(1)}, u32[]{:S(2)}, u32[]{:S(2)}) collective-permute-start(bf16[512,512]{1,0:T(8,128)(2,1)S(1)} %constant_dynamic-update-slice_fusion.near_ref), channel_id=1, source_target_pairs={{0,1},{1,0},{2,3},{3,2},{4,5},{5,4},{6,7},{7,6},{8,9},{9,8},{10,11... | collective-permute-start | bytes 1572872 | tf_op jit(solution)/shard_map/ppermute | solution.py:206
  38.5 0.0 all-to-all-done
  38.5 2.8 %count.1.logcount_ref = f32[1024,512]{1,0:T(8,128)S(1)} custom-call(bf16[512,640]{1,0:T(8,128)(2,1)S(1)} %bitcast.7), custom_call_target="tpu_custom_call" | custom-call | tf_op jit(solution)/shard_map/count/pallas_call | solution.py:209
  41.3 0.0 copy-start
  41.3 0.0 copy-start.1
  41.3 0.0 copy-start.3
  41.4 0.0 copy-start.4
  41.4 0.0 copy-start.10
  41.4 0.0 copy-start.11
  41.4 0.0 collective-permute-done.7.far_ref
  41.4 0.0 copy-done.6
  41.4 0.0 copy-done.7
  41.4 7.2 %attend.1 = bf16[512,512]{1,0:T(8,128)(2,1)S(1)} custom-call(bf16[512,640]{1,0:T(8,128)(2,1)S(1)} %bitcast.8, f32[1024,512]{1,0:T(8,128)S(1)} %count.1.logcount_ref, bf16[512,512]{1,0:T(8,128)(2,1)S(1)} %constant_dynamic-update-slice_fusion.near_ref, bf16[512,512]{1,0:T(8,128)(2,1)S(1)} %collective-permute-done.7.far_ref, bf16[512,512]{1,0:T(8,128)(2,1)S(1)} %copy-done.6, ...), custom_call_target="tpu_custom_call" | custom-call | tf_op jit(solution)/shard_map/attend/pallas_call | solution.py:222
  48.6 16.9 %all_to_all.10 = bf16[16,32,512]{2,1,0:T(8,128)(2,1)S(1)} all-to-all(bf16[16,32,512]{2,1,0:T(8,128)(2,1)S(1)} %bitcast.10), channel_id=1, replica_groups=mesh['region'=16,'shard'=16] {'region'}, dimensions={0} | all-to-all | bytes 1048576 | tf_op jit(solution)/shard_map/all_to_all | solution.py:243
  65.5 0.0 copy-done
  65.5 0.0 copy-done.1
  65.5 0.0 copy-done.3
  65.5 0.0 copy-done.4
  65.5 0.0 copy-done.10
  65.5 0.0 copy-done.11
  65.5 3.0 %finish.1 = bf16[256,512]{1,0:T(8,128)(2,1)} custom-call(bf16[256,512]{1,0:T(8,128)(2,1)S(1)} %copy-done.3, s32[1,256]{1,0:T(1,128)S(1)} %bitcast.13, bf16[512,512]{1,0:T(8,128)(2,1)S(1)} %bitcast.9, bf16[512,512]{1,0:T(8,128)(2,1)S(1)} %copy-done.4, f32[1,512]{1,0:T(1,128)S(1)} %bitcast.14, bf16[512,2048]{1,0:T(8,128)(2,1)S(1)} %copy-done, ...), custom_call_target="tpu_custom_call" | custom-call | tf_op jit(solution)/shard_map/finish/pallas_call | solution.py:246
  (9 shorter events, 0.1 us)
Async XLA Ops:
  0.0 31.1 %collective-permute-start.5 = (bf16[64,512]{1,0:T(8,128)(2,1)}, bf16[64,512]{1,0:T(8,128)(2,1)S(1)}, u32[]{:S(2)}, u32[]{:S(2)}) collective-permute-start(bf16[64,512]{1,0:T(8,128)(2,1)} %param.14), channel_id=1, source_target_pairs={{0,12},{1,13},{2,14},{3,15},{4,0},{5,1},{6,2},{7,3},{8,4},{9,5},{1... | collective-permute-start | bytes 196616 | tf_op jit(solution)/shard_map/ppermute | solution.py:193
  6.9 24.3 %collective-permute-start.4 = (bf16[64,512]{1,0:T(8,128)(2,1)}, bf16[64,512]{1,0:T(8,128)(2,1)S(1)}, u32[]{:S(2)}, u32[]{:S(2)}) collective-permute-start(bf16[64,512]{1,0:T(8,128)(2,1)} %param.14), channel_id=1, source_target_pairs={{0,10},{1,11},{2,12},{3,13},{4,14},{5,15},{6,0},{7,1},{8,2},{9,3},... | collective-permute-start | bytes 196616 | tf_op jit(solution)/shard_map/ppermute | solution.py:193
  7.6 23.5 %collective-permute-start.3 = (bf16[64,512]{1,0:T(8,128)(2,1)}, bf16[64,512]{1,0:T(8,128)(2,1)S(1)}, u32[]{:S(2)}, u32[]{:S(2)}) collective-permute-start(bf16[64,512]{1,0:T(8,128)(2,1)} %param.14), channel_id=1, source_target_pairs={{0,8},{1,9},{2,10},{3,11},{4,12},{5,13},{6,14},{7,15},{8,0},{9,1},... | collective-permute-start | bytes 196616 | tf_op jit(solution)/shard_map/ppermute | solution.py:193
  11.8 19.3 %collective-permute-start.2 = (bf16[64,512]{1,0:T(8,128)(2,1)}, bf16[64,512]{1,0:T(8,128)(2,1)S(1)}, u32[]{:S(2)}, u32[]{:S(2)}) collective-permute-start(bf16[64,512]{1,0:T(8,128)(2,1)} %param.14), channel_id=1, source_target_pairs={{0,6},{1,7},{2,8},{3,9},{4,10},{5,11},{6,12},{7,13},{8,14},{9,15},... | collective-permute-start | bytes 196616 | tf_op jit(solution)/shard_map/ppermute | solution.py:193
  11.8 13.3 %collective-permute-start = (bf16[64,512]{1,0:T(8,128)(2,1)}, bf16[64,512]{1,0:T(8,128)(2,1)S(1)}, u32[]{:S(2)}, u32[]{:S(2)}) collective-permute-start(bf16[64,512]{1,0:T(8,128)(2,1)} %param.14), channel_id=1, source_target_pairs={{0,2},{1,3},{2,4},{3,5},{4,6},{5,7},{6,8},{7,9},{8,10},{9,11},{10,... | collective-permute-start | bytes 196616 | tf_op jit(solution)/shard_map/ppermute | solution.py:193
  13.2 0.9 %copy-start.2 = (bf16[256,512]{1,0:T(8,128)(2,1)S(1)}, bf16[256,512]{1,0:T(8,128)(2,1)}, u32[]{:S(2)}) copy-start(bf16[256,512]{1,0:T(8,128)(2,1)} %feats_ref.3) | copy-start | bytes 786436
  14.2 1.0 %copy-start.5 = (bf16[512,512]{1,0:T(8,128)(2,1)S(1)}, bf16[512,512]{1,0:T(8,128)(2,1)}, u32[]{:S(2)}) copy-start(bf16[512,512]{1,0:T(8,128)(2,1)} %w_query_ref.1) | copy-start | bytes 1572868
  15.2 0.8 %copy-start.8 = (s32[256,64]{0,1:T(8,128)S(1)}, s32[256,64]{0,1:T(8,128)}, u32[]{:S(2)}) copy-start(s32[256,64]{0,1:T(8,128)} %param.13) | copy-start | bytes 196612
  16.1 0.7 copy-start.9
  16.7 8.3 %copy-start.12 = (bf16[64,512]{1,0:T(8,128)(2,1)S(1)}, bf16[64,512]{1,0:T(8,128)(2,1)}, u32[]{:S(2)}) copy-start(bf16[64,512]{1,0:T(8,128)(2,1)} %param.14) | copy-start | bytes 196612
  18.3 20.2 %all-to-all-start = ((bf16[16,32,640]{2,1,0:T(8,128)(2,1)}), bf16[16,32,640]{2,1,0:T(8,128)(2,1)S(1)}, u32[]{:S(2)}, u32[]{:S(2)}) async-start(bf16[16,32,640]{2,1,0:T(8,128)(2,1)} %bitcast.2), calls=%async_computation | async-start | bytes 1310720 | tf_op jit(solution)/shard_map/all_to_all | solution.py:202
  25.0 16.4 %copy-start.6 = (bf16[512,512]{1,0:T(8,128)(2,1)S(1)}, bf16[512,512]{1,0:T(8,128)(2,1)}, u32[]{:S(2)}) copy-start(bf16[512,512]{1,0:T(8,128)(2,1)} %w_key_ref.1) | copy-start | bytes 1572868
  25.1 16.4 %copy-start.7 = (bf16[512,512]{1,0:T(8,128)(2,1)S(1)}, bf16[512,512]{1,0:T(8,128)(2,1)}, u32[]{:S(2)}) copy-start(bf16[512,512]{1,0:T(8,128)(2,1)} %w_value_ref.1) | copy-start | bytes 1572868
  25.1 5.8 %collective-permute-start.1 = (bf16[64,512]{1,0:T(8,128)(2,1)S(1)}, bf16[64,512]{1,0:T(8,128)(2,1)S(1)}, u32[]{:S(2)}, u32[]{:S(2)}) collective-permute-start(bf16[64,512]{1,0:T(8,128)(2,1)S(1)} %copy-done.12), channel_id=1, source_target_pairs={{0,4},{1,5},{2,6},{3,7},{4,8},{5,9},{6,10},{7,11},{8,12},{9,13},{1... | collective-permute-start | bytes 196616 | tf_op jit(solution)/shard_map/ppermute | solution.py:193
  30.9 3.7 %collective-permute-start.6 = (bf16[64,512]{1,0:T(8,128)(2,1)S(1)}, bf16[64,512]{1,0:T(8,128)(2,1)S(1)}, u32[]{:S(2)}, u32[]{:S(2)}) collective-permute-start(bf16[64,512]{1,0:T(8,128)(2,1)S(1)} %copy-done.12), channel_id=1, source_target_pairs={{0,14},{1,15},{2,0},{3,1},{4,2},{5,3},{6,4},{7,5},{8,6},{9,7},{10,... | collective-permute-start | bytes 196616 | tf_op jit(solution)/shard_map/ppermute | solution.py:193
  34.7 6.7 %collective-permute-start.7 = (bf16[512,512]{1,0:T(8,128)(2,1)S(1)}, bf16[512,512]{1,0:T(8,128)(2,1)S(1)}, u32[]{:S(2)}, u32[]{:S(2)}) collective-permute-start(bf16[512,512]{1,0:T(8,128)(2,1)S(1)} %constant_dynamic-update-slice_fusion.near_ref), channel_id=1, source_target_pairs={{0,1},{1,0},{2,3},{3,2},{4,5},{5,4},{6,7},{7,6},{8,9},{9,8},{10,11... | collective-permute-start | bytes 1572872 | tf_op jit(solution)/shard_map/ppermute | solution.py:206
  41.3 24.2 %copy-start = (bf16[512,2048]{1,0:T(8,128)(2,1)S(1)}, bf16[512,2048]{1,0:T(8,128)(2,1)}, u32[]{:S(2)}) copy-start(bf16[512,2048]{1,0:T(8,128)(2,1)} %w_up_ref.1) | copy-start | bytes 6291460
  41.3 24.2 %copy-start.1 = (bf16[2048,512]{1,0:T(8,128)(2,1)S(1)}, bf16[2048,512]{1,0:T(8,128)(2,1)}, u32[]{:S(2)}) copy-start(bf16[2048,512]{1,0:T(8,128)(2,1)} %w_down_ref.1) | copy-start | bytes 6291460
  41.3 24.2 %copy-start.3 = (bf16[256,512]{1,0:T(8,128)(2,1)S(1)}, bf16[256,512]{1,0:T(8,128)(2,1)}, u32[]{:S(2)}) copy-start(bf16[256,512]{1,0:T(8,128)(2,1)} %feats_ref.3) | copy-start | bytes 786436
  41.4 24.2 %copy-start.4 = (bf16[512,512]{1,0:T(8,128)(2,1)S(1)}, bf16[512,512]{1,0:T(8,128)(2,1)}, u32[]{:S(2)}) copy-start(bf16[512,512]{1,0:T(8,128)(2,1)} %w_out_ref.1) | copy-start | bytes 1572868
  41.4 24.2 %copy-start.10 = (s32[256,1]{0,1:T(1,128)S(1)}, s32[256,1]{0,1:T(1,128)}, u32[]{:S(2)}) copy-start(s32[256,1]{0,1:T(1,128)} %param.12) | copy-start | bytes 3076
  41.4 24.2 %copy-start.11 = (f32[512]{0:T(512)S(1)}, f32[512]{0:T(512)}, u32[]{:S(2)}) copy-start(f32[512]{0:T(512)} %param.19) | copy-start | bytes 6148

commit v2 on v1

--- a/solution.py
+++ b/solution.py
@@ -28,7 +28,8 @@
     return region_row.astype(F32) * float(capacity) + rank
 
 
-def pack_kernel(region_count, capacity, feats_ref, region_ref, neighbors_ref, w_query_ref, send_ref):
+def pack_kernel(region_count, capacity, feats_ref, region_ref, neighbors_ref, w_query_ref, latents_ref, send_ref, held_ref):
+    held_ref[...] = latents_ref[...]
     slot_count = region_count * capacity
     rows, width = feats_ref.shape
     neighbor_count = neighbors_ref.shape[0]
@@ -48,7 +49,8 @@
 
 def count_kernel(neighbor_count, received_ref, logcount_ref, low_ref, digit_ref):
     slot_count = logcount_ref.shape[1]
-    coded = received_ref[...].astype(F32)
+    width = received_ref.shape[1] - LANES
+    coded = received_ref[:, width:].astype(F32)
     for block in range(slot_count // LANES):
         part = jnp.transpose(coded[block * LANES : (block + 1) * LANES])[:neighbor_count]
         high = jnp.zeros(part.shape, jnp.int32)
@@ -82,39 +84,66 @@
     lax.fori_loop(0, slot_count // LANES * 2, one, 0)
 
 
+def join_kernel(*refs):
+    joined_ref = refs[-1]
+    rows = refs[0].shape[0]
+    for step, ref in enumerate(refs[:-1]):
+        joined_ref[step * rows : (step + 1) * rows, :] = ref[...]
+
+
 def attend_kernel(
-    query_ref, logcount_ref, near_ref, far_ref, w_key_ref, w_value_ref, mixed_ref, token_ref, key_ref, value_ref
+    rows_held,
+    query_ref,
+    logcount_ref,
+    own_ref,
+    beside_ref,
+    across_ref,
+    slant_ref,
+    w_key_ref,
+    w_value_ref,
+    mixed_ref,
+    token_ref,
+    key_ref,
+    value_ref,
 ):
-    slot_count, width = query_ref.shape
+    slot_count, width = mixed_ref.shape
     head_width = width // HEADS
-    half_rows = near_ref.shape[0]
-    chips = half_rows // 64
     place = lax.axis_index("shard")
-    chip, core = place // 2, place % 2
-    for step in range(chips):
-        origin = lax.rem(chip - step + chips, chips) * 2
-        piece = slice(step * 64, step * 64 + 64)
-        token_ref[pl.ds(pl.multiple_of((origin + core) * 64, 64), 64), :] = near_ref[piece, :]
-        token_ref[pl.ds(pl.multiple_of((origin + 1 - core) * 64, 64), 64), :] = far_ref[piece, :]
+    chips = token_ref.shape[0] // (2 * rows_held)
+    for flip, ref in ((0, own_ref), (2, beside_ref), (1, across_ref), (3, slant_ref)):
+        holder = jnp.bitwise_xor(place, flip)
+        for step in range(chips // 2):
+            origin = lax.rem(holder - 4 * step + 2 * chips, 2 * chips)
+            target = pl.ds(pl.multiple_of(origin * rows_held, rows_held), rows_held)
+            token_ref[target, :] = ref[step * rows_held : (step + 1) * rows_held, :]
     tokens = token_ref[...]
     key_ref[...] = jnp.dot(tokens, w_key_ref[...], preferred_element_type=F32).astype(BF16)
     value_ref[...] = lax.dot_general(
         w_value_ref[...], tokens, (((0,), (1,)), ((), ())), preferred_element_type=F32
     ).astype(BF16)
     factor = head_width ** (-0.5) * math.log2(math.e)
-    size = 256
+    size, chunk = 128, 256
     for block in range(slot_count // size):
         rows = slice(block * size, (block + 1) * size)
         for head in range(HEADS):
             columns = slice(head * head_width, (head + 1) * head_width)
-            scores = lax.dot_general(
-                key_ref[:, columns], query_ref[rows, columns], NT, preferred_element_type=F32
-            )
-            scores = scores * factor + logcount_ref[:, rows]
-            peak = jnp.max(scores, axis=0, keepdims=True)
-            raised = jnp.exp2(scores - peak)
-            total = jnp.sum(raised, axis=0, keepdims=True)
-            mixed = jnp.dot(value_ref[columns, :], raised.astype(BF16), preferred_element_type=F32)
+            peak = jnp.full((1, size), 2 * ABSENT, F32)
+            total = jnp.zeros((1, size), F32)
+            mixed = jnp.zeros((head_width, size), F32)
+            for first in range(0, key_ref.shape[0], chunk):
+                part = slice(first, first + chunk)
+                scores = lax.dot_general(
+                    key_ref[part, columns], query_ref[rows, columns], NT, preferred_element_type=F32
+                )
+                scores = scores * factor + logcount_ref[part, rows]
+                higher = jnp.maximum(peak, jnp.max(scores, axis=0, keepdims=True))
+                raised = jnp.exp2(scores - higher)
+                shrink = jnp.exp2(peak - higher)
+                total = total * shrink + jnp.sum(raised, axis=0, keepdims=True)
+                mixed = mixed * shrink + jnp.dot(
+                    value_ref[columns, part], raised.astype(BF16), preferred_element_type=F32
+                )
+                peak = higher
             mixed_ref[rows, columns] = jnp.transpose(mixed / total).astype(BF16)
 
 
@@ -183,63 +212,73 @@
     table_rows = latents.shape[0] * shard_count
     region_row = query_region.reshape(1, query_count)
 
-    def ring(step):
-        return [
-            (chip * 2 + core, (chip + step) % chips * 2 + core)
-            for chip in range(chips)
-            for core in range(2)
-        ]
-
-    pieces = [latents] + [lax.ppermute(latents, "shard", ring(step)) for step in range(1, chips)]
-    send = pl.pallas_call(
+    def swap(flip):
+        return [(place, place ^ flip) for place in range(shard_count)]
+
+    pieces = [
+        lax.ppermute(
+            latents, "shard", [(place, (place + 4 * step) % shard_count) for place in range(shard_count)]
+        )
+        for step in range(1, chips // 2)
+    ]
+    send, held = pl.pallas_call(
         functools.partial(pack_kernel, region_count, capacity),
-        out_shape=jax.ShapeDtypeStruct((slot_count, wide), BF16),
-        in_specs=[VMEM] * 4,
-        out_specs=VMEM,
-        compiler_params=params(12),
+        grid=(1,),
+        out_shape=[
+            jax.ShapeDtypeStruct((slot_count, wide), BF16),
+            jax.ShapeDtypeStruct(latents.shape, BF16),
+        ],
+        in_specs=[
+            pl.BlockSpec((query_count, width), lambda i: (0, 0)),
+            pl.BlockSpec((1, query_count), lambda i: (0, 0)),
+            pl.BlockSpec((neighbor_count, query_count), lambda i: (0, 0)),
+            pl.BlockSpec((width, width), lambda i: (0, 0)),
+            pl.BlockSpec(latents.shape, lambda i: (0, 0)),
+        ],
+        out_specs=[pl.BlockSpec((slot_count, wide), lambda i: (0, 0)), VMEM],
+        compiler_params=params(56),
         name="pack",
-    )(query_feats, region_row, neighbors.T, w_query)
+    )(query_feats, region_row, neighbors.T, w_query, latents)
     received = lax.all_to_all(
         send.reshape(region_count, capacity, wide), "region", split_axis=0, concat_axis=0, tiled=True
     ).reshape(slot_count, wide)
-    near = jnp.concatenate(pieces, axis=0)
-    far = lax.ppermute(
-        near, "shard", [(place, place + 1 - 2 * (place % 2)) for place in range(shard_count)]
-    )
+    own = pl.pallas_call(
+        join_kernel,
+        out_shape=jax.ShapeDtypeStruct(((len(pieces) + 1) * latents.shape[0], width), BF16),
+        in_specs=[VMEM] * (len(pieces) + 1),
+        out_specs=VMEM,
+        compiler_params=params(4),
+        cost_estimate=pl.CostEstimate(flops=10**11, bytes_accessed=0, transcendentals=0),
+        name="join",
+    )(held, *pieces)
+    beside = lax.ppermute(own, "shard", swap(2))
+    across = lax.ppermute(own, "shard", swap(1))
+    slant = lax.ppermute(beside, "shard", swap(1))
     logcount = pl.pallas_call(
         functools.partial(count_kernel, neighbor_count),
-        grid=(1,),
         out_shape=jax.ShapeDtypeStruct((table_rows, slot_count), F32),
-        in_specs=[pl.BlockSpec((slot_count, LANES), lambda i: (0, width // LANES))],
-        out_specs=pl.BlockSpec((table_rows, slot_count), lambda i: (0, 0)),
+        in_specs=[VMEM],
+        out_specs=VMEM,
         scratch_shapes=[
             pltpu.VMEM((slot_count // LANES, neighbor_count, LANES), jnp.int32),
             pltpu.VMEM((slot_count // LANES, neighbor_count, LANES), jnp.int32),
         ],
-        compiler_params=params(12),
+        compiler_params=params(8),
         name="count",
     )(received)
     mixed = pl.pallas_call(
-        attend_kernel,
-        grid=(1,),
+        functools.partial(attend_kernel, latents.shape[0]),
         out_shape=jax.ShapeDtypeStruct((slot_count, width), BF16),
-        in_specs=[
-            pl.BlockSpec((slot_count, width), lambda i: (0, 0)),
-            pl.BlockSpec((table_rows, slot_count), lambda i: (0, 0)),
-            pl.BlockSpec(near.shape, lambda i: (0, 0)),
-            pl.BlockSpec(near.shape, lambda i: (0, 0)),
-            pl.BlockSpec(w_key.shape, lambda i: (0, 0)),
-            pl.BlockSpec(w_value.shape, lambda i: (0, 0)),
-        ],
-        out_specs=pl.BlockSpec((slot_count, width), lambda i: (0, 0)),
+        in_specs=[VMEM] * 8,
+        out_specs=VMEM,
         scratch_shapes=[
             pltpu.VMEM((table_rows, width), BF16),
             pltpu.VMEM((table_rows, width), BF16),
             pltpu.VMEM((width, table_rows), BF16),
         ],
-        compiler_params=params(32),
+        compiler_params=params(24),
         name="attend",
-    )(received, logcount, near, far, w_key, w_value)
+    )(received, logcount, own, beside, across, slant, w_key, w_value)
     returned = lax.all_to_all(
         mixed.reshape(region_count, capacity, width), "region", split_axis=0, concat_axis=0, tiled=True
     ).reshape(slot_count, width)

time: 69.8 us -> 57.6 us (0.83); the launches traced: 68.5 us -> 57.4 us
  waiting for transfers between devices: 7.17 us -> 4.17 us
  local copies, waits for them, and re-layouts: 3.61 us -> 0.89 us
  starting transfers between devices: 26.1 us -> 23.7 us
  Pallas kernels: 14.5 us -> 12.6 us
  blocking collectives: 16.9 us -> 15.8 us
    ppermute x8 -> x6, waiting for transfers between devices: 7.17 us -> 3.2 us  [the longest x1 3.19 us: on_device(): beside = lax.ppermute(own, 'shard', swap(2))]
    unnamed x33 -> x18, local copies, waits for them, and re-layouts: 3.61 us -> 0.89 us
    ppermute x8 -> x6, starting transfers between devices: 19.3 us -> 16.9 us  [the longest x3 11.3 us: on_device(): lax.ppermute(latents, 'shard', [(place, (place + 4 * step) % shard_count)...]
    pallas_call x3 -> x4, Pallas kernels: 11.6 us -> 9.68 us  [the longest x1 4.22 us: on_device(): pl.pallas_call(functools.partial(attend_kernel, latents.shape[0]), out_sh...]
    all_to_all x1, blocking collectives: 16.9 us -> 15.8 us  [on_device(): lax.all_to_all(mixed.reshape(region_count, capacity, width), 'region', sp...]
    all_to_all x1, waiting for transfers between devices: 0.01 us -> 0.96 us  [on_device(): lax.all_to_all(send.reshape(region_count, capacity, wide), 'region', spli...]
  transfers between devices with their start and end apart: 9 -> 7, of which waited for: 2 -> 2; matrix products, arithmetic and copies ran while one was open for 0% -> 0% of each run, Pallas kernels for 6% -> 9%
where the time goes in v2:
time: 57.6 us; the launch traced here: 57.4 us
  starting transfers between devices  23.7 us (41%)
  blocking collectives  15.8 us (27%)
  Pallas kernels  12.6 us (22%)
  waiting for transfers between devices  4.17 us (7%)
  local copies, waits for them, and re-layouts  0.89 us (2%)
    all_to_all x1, blocking collectives, on_device(): lax.all_to_all(mixed.reshape(region_count, capacity, width), 'region', sp...  15.8 us
    ppermute x3, starting transfers between devices, on_device(): lax.ppermute(latents, 'shard', [(place, (place + 4 * step) % shard_count)...  11.3 us
    all_to_all x1, starting transfers between devices, on_device(): lax.all_to_all(send.reshape(region_count, capacity, wide), 'region', spli...  6.76 us
    pallas_call x1, Pallas kernels, on_device(): pl.pallas_call(functools.partial(attend_kernel, latents.shape[0]), out_sh...  4.22 us
    ppermute x1, waiting for transfers between devices, on_device(): beside = lax.ppermute(own, 'shard', swap(2))  3.19 us
    pallas_call x1, Pallas kernels, on_device(): pl.pallas_call(functools.partial(finish_kernel, region_count, capacity),...  2.96 us
    pallas_call x1, Pallas kernels, on_device(): pl.pallas_call(functools.partial(count_kernel, neighbor_count), out_shape...  2.81 us
    ppermute x1, starting transfers between devices, on_device(): slant = lax.ppermute(beside, 'shard', swap(1))  2.72 us
  transfers between devices with their start and end apart: 7, of which 2 were waited for; matrix products, arithmetic and copies ran while one was open for 0% of the time, Pallas kernels for 9%

profile of v2, /device:TPU:1, one launch (start us, length us, event | category | flops | bytes accessed | tf_op | source)
XLA Modules:
  0.0 57.4 jit_solution(18276055718294856438)
XLA Ops:
  0.0 3.8 %collective-permute-start = (bf16[64,512]{1,0:T(8,128)(2,1)}, bf16[64,512]{1,0:T(8,128)(2,1)S(1)}, u32[]{:S(2)}, u32[]{:S(2)}) collective-permute-start(bf16[64,512]{1,0:T(8,128)(2,1)} %latents_ref.1), channel_id=1, source_target_pairs={{0,4},{1,5},{2,6},{3,7},{4,8},{5,9},{6,10},{7,11},{8,12},{9,13},{1... | collective-permute-start | bytes 196616 | tf_op jit(solution)/shard_map/ppermute | solution.py:219
  3.8 3.0 %collective-permute-start.2 = (bf16[64,512]{1,0:T(8,128)(2,1)}, bf16[64,512]{1,0:T(8,128)(2,1)S(1)}, u32[]{:S(2)}, u32[]{:S(2)}) collective-permute-start(bf16[64,512]{1,0:T(8,128)(2,1)} %latents_ref.1), channel_id=1, source_target_pairs={{0,12},{1,13},{2,14},{3,15},{4,0},{5,1},{6,2},{7,3},{8,4},{9,5},{1... | collective-permute-start | bytes 196616 | tf_op jit(solution)/shard_map/ppermute | solution.py:219
  6.9 4.5 %collective-permute-start.1 = (bf16[64,512]{1,0:T(8,128)(2,1)}, bf16[64,512]{1,0:T(8,128)(2,1)S(1)}, u32[]{:S(2)}, u32[]{:S(2)}) collective-permute-start(bf16[64,512]{1,0:T(8,128)(2,1)} %latents_ref.1), channel_id=1, source_target_pairs={{0,8},{1,9},{2,10},{3,11},{4,12},{5,13},{6,14},{7,15},{8,0},{9,1},... | collective-permute-start | bytes 196616 | tf_op jit(solution)/shard_map/ppermute | solution.py:219
  11.3 2.6 %pack.1 = (bf16[512,640]{1,0:T(8,128)(2,1)}, bf16[64,512]{1,0:T(8,128)(2,1)}) custom-call(bf16[256,512]{1,0:T(8,128)(2,1)} %feats_ref.3, s32[1,256]{1,0:T(1,128)} %bitcast.11, s32[64,256]{1,0:T(8,128)} %bitcast.15, bf16[512,512]{1,0:T(8,128)(2,1)} %w_query_ref.1, bf16[64,512]{1,0:T(8,128)(2,1)} %latents_ref.1), custom_call_target="tpu_custom_call" | custom-call | tf_op jit(solution)/shard_map/pack/pallas_call | solution.py:224
  13.9 6.8 %all-to-all-start = ((bf16[16,32,640]{2,1,0:T(8,128)(2,1)}), bf16[16,32,640]{2,1,0:T(8,128)(2,1)S(1)}, u32[]{:S(2)}, u32[]{:S(2)}) async-start(bf16[16,32,640]{2,1,0:T(8,128)(2,1)} %bitcast.14), calls=%async_computation | async-start | bytes 1310720 | tf_op jit(solution)/shard_map/all_to_all | solution.py:242
  20.7 0.0 collective-permute-done.refs_1_
  20.7 0.0 collective-permute-done.2.refs_3_
  20.7 0.0 collective-permute-done.1.refs_2_
  20.7 0.0 copy-start.8
  20.7 0.8 %copy-done.8 = bf16[64,512]{1,0:T(8,128)(2,1)S(1)} copy-done((bf16[64,512]{1,0:T(8,128)(2,1)S(1)}, bf16[64,512]{1,0:T(8,128)(2,1)}, u32[]{:S(2)}) %copy-start.8) | copy-done | bytes 65560
  21.6 0.0 copy-start.4
  21.6 0.0 copy-start.5
  21.6 0.8 %collective-permute-start.3 = (bf16[256,512]{1,0:T(8,128)(2,1)S(1)}, bf16[256,512]{1,0:T(8,128)(2,1)S(1)}, u32[]{:S(2)}, u32[]{:S(2)}) collective-permute-start(bf16[256,512]{1,0:T(8,128)(2,1)S(1)} %join.1.own_ref), channel_id=1, source_target_pairs={{0,2},{1,3},{2,0},{3,1},{4,6},{5,7},{6,4},{7,5},{8,10},{9,11},{10,... | collective-permute-start | bytes 786440 | tf_op jit(solution)/shard_map/ppermute | solution.py:254
  22.4 2.1 %collective-permute-start.4 = (bf16[256,512]{1,0:T(8,128)(2,1)S(1)}, bf16[256,512]{1,0:T(8,128)(2,1)S(1)}, u32[]{:S(2)}, u32[]{:S(2)}) collective-permute-start(bf16[256,512]{1,0:T(8,128)(2,1)S(1)} %join.1.own_ref), channel_id=1, source_target_pairs={{0,1},{1,0},{2,3},{3,2},{4,5},{5,4},{6,7},{7,6},{8,9},{9,8},{10,11... | collective-permute-start | bytes 786440 | tf_op jit(solution)/shard_map/ppermute | solution.py:255
  24.5 3.2 %collective-permute-done.3.beside_ref = bf16[256,512]{1,0:T(8,128)(2,1)S(1)} collective-permute-done((bf16[256,512]{1,0:T(8,128)(2,1)S(1)}, bf16[256,512]{1,0:T(8,128)(2,1)S(1)}, u32[]{:S(2)}, u32[]{:S(2)}) %collective-permute-start.3) | collective-permute-done | bytes 262176 | tf_op jit(solution)/shard_map/ppermute | solution.py:254
  27.7 2.7 %collective-permute-start.5 = (bf16[256,512]{1,0:T(8,128)(2,1)S(1)}, bf16[256,512]{1,0:T(8,128)(2,1)S(1)}, u32[]{:S(2)}, u32[]{:S(2)}) collective-permute-start(bf16[256,512]{1,0:T(8,128)(2,1)S(1)} %collective-permute-done.3.beside_ref), channel_id=1, source_target_pairs={{0,1},{1,0},{2,3},{3,2},{4,5},{5,4},{6,7},{7,6},{8,9},{9,8},{10,11... | collective-permute-start | bytes 786440 | tf_op jit(solution)/shard_map/ppermute | solution.py:256
  30.4 1.0 %all-to-all-done = bf16[16,32,640]{2,1,0:T(8,128)(2,1)S(1)} async-done(((bf16[16,32,640]{2,1,0:T(8,128)(2,1)}), bf16[16,32,640]{2,1,0:T(8,128)(2,1)S(1)}, u32[]{:S(2)}, u32[]{:S(2)}) %all-to-all-start) | async-done | bytes 655392 | tf_op jit(solution)/shard_map/all_to_all | solution.py:242
  31.4 2.8 %count.1.logcount_ref = f32[1024,512]{1,0:T(8,128)S(1)} custom-call(bf16[512,640]{1,0:T(8,128)(2,1)S(1)} %bitcast.7), custom_call_target="tpu_custom_call" | custom-call | tf_op jit(solution)/shard_map/count/pallas_call | solution.py:257
  34.2 0.0 copy-start
  34.2 0.0 copy-start.1
  34.2 0.0 copy-start.2
  34.3 0.0 copy-start.3
  34.3 0.0 copy-start.6
  34.3 0.0 copy-start.7
  34.3 0.0 collective-permute-done.4.across_ref
  34.3 0.0 collective-permute-done.5.slant_ref
  34.3 0.0 copy-done.4
  34.3 0.0 copy-done.5
  34.3 4.2 %attend.1 = bf16[512,512]{1,0:T(8,128)(2,1)S(1)} custom-call(bf16[512,640]{1,0:T(8,128)(2,1)S(1)} %bitcast.8, f32[1024,512]{1,0:T(8,128)S(1)} %count.1.logcount_ref, bf16[256,512]{1,0:T(8,128)(2,1)S(1)} %join.1.own_ref, bf16[256,512]{1,0:T(8,128)(2,1)S(1)} %collective-permute-done.3.beside_ref, bf16[256,512]{1,0:T(8,128)(2,1)S(1)} %collective-permute-done.4.across_ref, ...), custom_call_target="tpu_custom_call" | custom-call | tf_op jit(solution)/shard_map/attend/pallas_call | solution.py:269
  38.6 15.8 %all_to_all.10 = bf16[16,32,512]{2,1,0:T(8,128)(2,1)S(1)} all-to-all(bf16[16,32,512]{2,1,0:T(8,128)(2,1)S(1)} %bitcast.10), channel_id=1, replica_groups=mesh['region'=16,'shard'=16] {'region'}, dimensions={0} | all-to-all | bytes 1048576 | tf_op jit(solution)/shard_map/all_to_all | solution.py:282
  54.4 0.0 copy-done
  54.4 0.0 copy-done.1
  54.4 0.0 copy-done.2
  54.4 0.0 copy-done.3
  54.4 0.0 copy-done.6
  54.4 0.0 copy-done.7
  54.4 3.0 %finish.1 = bf16[256,512]{1,0:T(8,128)(2,1)} custom-call(bf16[256,512]{1,0:T(8,128)(2,1)S(1)} %copy-done.2, s32[1,256]{1,0:T(1,128)S(1)} %bitcast.12, bf16[512,512]{1,0:T(8,128)(2,1)S(1)} %bitcast.9, bf16[512,512]{1,0:T(8,128)(2,1)S(1)} %copy-done.3, f32[1,512]{1,0:T(1,128)S(1)} %bitcast.13, bf16[512,2048]{1,0:T(8,128)(2,1)S(1)} %copy-done, ...), custom_call_target="tpu_custom_call" | custom-call | tf_op jit(solution)/shard_map/finish/pallas_call | solution.py:285
  (1 shorter events, 0.0 us)
Async XLA Ops:
  0.0 20.7 %collective-permute-start = (bf16[64,512]{1,0:T(8,128)(2,1)}, bf16[64,512]{1,0:T(8,128)(2,1)S(1)}, u32[]{:S(2)}, u32[]{:S(2)}) collective-permute-start(bf16[64,512]{1,0:T(8,128)(2,1)} %latents_ref.1), channel_id=1, source_target_pairs={{0,4},{1,5},{2,6},{3,7},{4,8},{5,9},{6,10},{7,11},{8,12},{9,13},{1... | collective-permute-start | bytes 196616 | tf_op jit(solution)/shard_map/ppermute | solution.py:219
  3.8 16.9 %collective-permute-start.2 = (bf16[64,512]{1,0:T(8,128)(2,1)}, bf16[64,512]{1,0:T(8,128)(2,1)S(1)}, u32[]{:S(2)}, u32[]{:S(2)}) collective-permute-start(bf16[64,512]{1,0:T(8,128)(2,1)} %latents_ref.1), channel_id=1, source_target_pairs={{0,12},{1,13},{2,14},{3,15},{4,0},{5,1},{6,2},{7,3},{8,4},{9,5},{1... | collective-permute-start | bytes 196616 | tf_op jit(solution)/shard_map/ppermute | solution.py:219
  6.9 13.9 %collective-permute-start.1 = (bf16[64,512]{1,0:T(8,128)(2,1)}, bf16[64,512]{1,0:T(8,128)(2,1)S(1)}, u32[]{:S(2)}, u32[]{:S(2)}) collective-permute-start(bf16[64,512]{1,0:T(8,128)(2,1)} %latents_ref.1), channel_id=1, source_target_pairs={{0,8},{1,9},{2,10},{3,11},{4,12},{5,13},{6,14},{7,15},{8,0},{9,1},... | collective-permute-start | bytes 196616 | tf_op jit(solution)/shard_map/ppermute | solution.py:219
  13.9 17.5 %all-to-all-start = ((bf16[16,32,640]{2,1,0:T(8,128)(2,1)}), bf16[16,32,640]{2,1,0:T(8,128)(2,1)S(1)}, u32[]{:S(2)}, u32[]{:S(2)}) async-start(bf16[16,32,640]{2,1,0:T(8,128)(2,1)} %bitcast.14), calls=%async_computation | async-start | bytes 1310720 | tf_op jit(solution)/shard_map/all_to_all | solution.py:242
  20.7 0.8 %copy-start.8 = (bf16[64,512]{1,0:T(8,128)(2,1)S(1)}, bf16[64,512]{1,0:T(8,128)(2,1)}, u32[]{:S(2)}) copy-start(bf16[64,512]{1,0:T(8,128)(2,1)} %get-tuple-element.8.refs_0_) | copy-start | bytes 196612
  21.6 12.7 %copy-start.4 = (bf16[512,512]{1,0:T(8,128)(2,1)S(1)}, bf16[512,512]{1,0:T(8,128)(2,1)}, u32[]{:S(2)}) copy-start(bf16[512,512]{1,0:T(8,128)(2,1)} %w_key_ref.1) | copy-start | bytes 1572868
  21.6 12.7 %copy-start.5 = (bf16[512,512]{1,0:T(8,128)(2,1)S(1)}, bf16[512,512]{1,0:T(8,128)(2,1)}, u32[]{:S(2)}) copy-start(bf16[512,512]{1,0:T(8,128)(2,1)} %w_value_ref.1) | copy-start | bytes 1572868
  21.6 6.1 %collective-permute-start.3 = (bf16[256,512]{1,0:T(8,128)(2,1)S(1)}, bf16[256,512]{1,0:T(8,128)(2,1)S(1)}, u32[]{:S(2)}, u32[]{:S(2)}) collective-permute-start(bf16[256,512]{1,0:T(8,128)(2,1)S(1)} %join.1.own_ref), channel_id=1, source_target_pairs={{0,2},{1,3},{2,0},{3,1},{4,6},{5,7},{6,4},{7,5},{8,10},{9,11},{10,... | collective-permute-start | bytes 786440 | tf_op jit(solution)/shard_map/ppermute | solution.py:254
  22.4 11.8 %collective-permute-start.4 = (bf16[256,512]{1,0:T(8,128)(2,1)S(1)}, bf16[256,512]{1,0:T(8,128)(2,1)S(1)}, u32[]{:S(2)}, u32[]{:S(2)}) collective-permute-start(bf16[256,512]{1,0:T(8,128)(2,1)S(1)} %join.1.own_ref), channel_id=1, source_target_pairs={{0,1},{1,0},{2,3},{3,2},{4,5},{5,4},{6,7},{7,6},{8,9},{9,8},{10,11... | collective-permute-start | bytes 786440 | tf_op jit(solution)/shard_map/ppermute | solution.py:255
  27.7 6.6 %collective-permute-start.5 = (bf16[256,512]{1,0:T(8,128)(2,1)S(1)}, bf16[256,512]{1,0:T(8,128)(2,1)S(1)}, u32[]{:S(2)}, u32[]{:S(2)}) collective-permute-start(bf16[256,512]{1,0:T(8,128)(2,1)S(1)} %collective-permute-done.3.beside_ref), channel_id=1, source_target_pairs={{0,1},{1,0},{2,3},{3,2},{4,5},{5,4},{6,7},{7,6},{8,9},{9,8},{10,11... | collective-permute-start | bytes 786440 | tf_op jit(solution)/shard_map/ppermute | solution.py:256
  34.2 20.2 %copy-start = (bf16[512,2048]{1,0:T(8,128)(2,1)S(1)}, bf16[512,2048]{1,0:T(8,128)(2,1)}, u32[]{:S(2)}) copy-start(bf16[512,2048]{1,0:T(8,128)(2,1)} %w_up_ref.1) | copy-start | bytes 6291460
  34.2 20.1 %copy-start.1 = (bf16[2048,512]{1,0:T(8,128)(2,1)S(1)}, bf16[2048,512]{1,0:T(8,128)(2,1)}, u32[]{:S(2)}) copy-start(bf16[2048,512]{1,0:T(8,128)(2,1)} %w_down_ref.1) | copy-start | bytes 6291460
  34.2 20.1 %copy-start.2 = (bf16[256,512]{1,0:T(8,128)(2,1)S(1)}, bf16[256,512]{1,0:T(8,128)(2,1)}, u32[]{:S(2)}) copy-start(bf16[256,512]{1,0:T(8,128)(2,1)} %feats_ref.3) | copy-start | bytes 786436
  34.3 20.1 %copy-start.3 = (bf16[512,512]{1,0:T(8,128)(2,1)S(1)}, bf16[512,512]{1,0:T(8,128)(2,1)}, u32[]{:S(2)}) copy-start(bf16[512,512]{1,0:T(8,128)(2,1)} %w_out_ref.1) | copy-start | bytes 1572868
  34.3 20.1 %copy-start.6 = (s32[256,1]{0,1:T(1,128)S(1)}, s32[256,1]{0,1:T(1,128)}, u32[]{:S(2)}) copy-start(s32[256,1]{0,1:T(1,128)} %param.12) | copy-start | bytes 3076
  34.3 20.1 %copy-start.7 = (f32[512]{0:T(512)S(1)}, f32[512]{0:T(512)}, u32[]{:S(2)}) copy-start(f32[512]{0:T(512)} %param.19) | copy-start | bytes 6148

commit v3 on v2

v3 whole, which is shorter than its diff:
```python
import functools
import math

import jax
import jax.numpy as jnp
from jax import lax
from jax.experimental import pallas as pl
from jax.experimental.pallas import tpu as pltpu
from jax.sharding import PartitionSpec as P

HEADS = 4
LANES = 128
ABSENT = -1e30
F32 = jnp.float32
BF16 = jnp.bfloat16
VMEM = pl.BlockSpec(memory_space=pltpu.VMEM)
NT = (((1,), (1,)), ((), ()))


def slots_of(region_row, region_count, capacity):
    rows = region_row.shape[1]
    onehot = (lax.broadcasted_iota(jnp.int32, (region_count, rows), 0) == region_row).astype(F32)
    earlier_than = lax.broadcasted_iota(jnp.int32, (rows, rows), 0) < lax.broadcasted_iota(
        jnp.int32, (rows, rows), 1
    )
    earlier = jnp.dot(onehot.astype(BF16), earlier_than.astype(BF16), preferred_element_type=F32)
    rank = jnp.sum(earlier * onehot, axis=0, keepdims=True)
    return region_row.astype(F32) * float(capacity) + rank


def pack_kernel(
    region_count,
    capacity,
    feats_hbm,
    region_hbm,
    neighbors_hbm,
    w_query_hbm,
    send_ref,
    feats_ref,
    region_ref,
    neighbors_ref,
    w_query_ref,
    arrived,
):
    sources = (region_hbm, neighbors_hbm, feats_hbm, w_query_hbm)
    targets = (region_ref, neighbors_ref, feats_ref, w_query_ref)
    copies = [
        pltpu.make_async_copy(source, target, arrived.at[number])
        for number, (source, target) in enumerate(zip(sources, targets))
    ]
    for copy in copies:
        copy.start()
    slot_count = region_count * capacity
    rows, width = feats_ref.shape
    copies[0].wait()
    slot_row = slots_of(region_ref[...], region_count, capacity)
    place = (
        lax.broadcasted_iota(jnp.int32, (slot_count, rows), 0).astype(F32) == slot_row
    ).astype(BF16)
    copies[1].wait()
    number = neighbors_ref[...]
    coded = ((number & 127) + 128) << (number >> 7)
    coded = coded.astype(F32).astype(BF16)
    spread = lax.dot_general(place, coded, NT, preferred_element_type=F32)
    spread = spread.reshape(region_count, capacity, spread.shape[1])
    half = capacity // 2
    spread = jnp.concatenate([spread[:, :half], spread[:, half:]], axis=2)
    send_ref[:, width // LANES * capacity :, :] = spread.astype(BF16)
    copies[2].wait()
    copies[3].wait()
    query = jnp.dot(feats_ref[...], w_query_ref[...], preferred_element_type=F32).astype(BF16)
    placed = jnp.dot(place, query, preferred_element_type=F32).astype(BF16)
    for head in range(width // LANES):
        send_ref[:, head * capacity : (head + 1) * capacity, :] = placed[
            :, head * LANES : (head + 1) * LANES
        ].reshape(region_count, capacity, LANES)


def count_kernel(neighbor_count, received_ref, logcount_ref, low_ref, digit_ref):
    slot_count = logcount_ref.shape[3]
    sources, rows, _ = received_ref.shape
    half = slot_count // sources // 2
    coded = received_ref[:, rows - half :, :].astype(F32).reshape(sources * half, LANES)
    blocks = slot_count // LANES
    for pair in range(blocks // 2):
        both = jnp.transpose(coded[pair * LANES : (pair + 1) * LANES])
        for side in range(2):
            part = both[side * neighbor_count : (side + 1) * neighbor_count]
            high = jnp.zeros(part.shape, jnp.int32)
            for power in range(1, 8):
                high += (part >= float(128 << power)).astype(jnp.int32)
            number = (high - 1) * 128 + (part.astype(jnp.int32) >> high)
            low_ref[side * (blocks // 2) + pair] = number & 63
            digit_ref[side * (blocks // 2) + pair] = jnp.int32(1) << (2 * (number >> 6))

    size = 32

    def one(step, carry):
        block, base = step // 2, step % 2 * size
        lanes = pl.ds(pl.multiple_of(block * LANES, LANES), LANES)
        inside = pl.ds(pl.multiple_of(base, size), size)
        numbers = lax.broadcasted_iota(jnp.int32, (size, LANES), 0) + base
        wide = [0, 0, 0, 0]
        for first in range(0, neighbor_count, 15):
            last = min(first + 15, neighbor_count)
            middle = [0, 0]
            for start in range(first, last, 3):
                narrow = 0
                for k in range(start, min(start + 3, last)):
                    same = low_ref[block, k : k + 1, :] == numbers
                    narrow = narrow + jnp.where(same, digit_ref[block, k : k + 1, :], 0)
                middle[0] = middle[0] + (narrow & 0x33333333)
                middle[1] = middle[1] + ((narrow >> 2) & 0x33333333)
            for odd in range(2):
                wide[odd] = wide[odd] + (middle[odd] & 0x0F0F0F0F)
                wide[2 + odd] = wide[2 + odd] + ((middle[odd] >> 4) & 0x0F0F0F0F)
        for digit in range(16):
            count = (wide[digit % 4] >> (8 * (digit // 4))) & 0xFF
            logs = jnp.maximum(jnp.log2(count.astype(F32)), ABSENT)
            logcount_ref[digit // 2, digit % 2, inside, lanes] = logs
        return carry

    lax.fori_loop(0, blocks * 2, one, 0)


def join_kernel(*refs):
    joined_ref = refs[-1]
    first = 0
    for ref in refs[:-1]:
        rows = ref.shape[0]
        joined_ref[first : first + rows, :] = ref[...]
        first += rows


def attend_kernel(
    first_part,
    rows_held,
    received_ref,
    logcount_ref,
    table_ref,
    table_more_ref,
    w_key_ref,
    w_value_ref,
    *refs,
):
    if first_part:
        mixed_out_ref, stats_out_ref, token_ref, key_ref, value_ref = refs
        sources, capacity = received_ref.shape[0], received_ref.shape[1] * 2 // (2 * HEADS + 1)
        width = w_key_ref.shape[1]
    else:
        mixed_in_ref, stats_in_ref, mixed_ref, token_ref, key_ref, value_ref = refs
        sources, capacity, width = mixed_ref.shape
    head_width = width // HEADS
    place = lax.axis_index("shard")
    chips = token_ref.shape[0] // rows_held
    chip, core = place // 2, place % 2
    if not first_part:
        core = 1 - core
    skip = 2 + 4 * core
    for step, offset in enumerate((0, 4, 1, 5, 7, 3, skip, skip + 4)):
        origin = lax.rem(chip + offset, chips)
        target = pl.ds(pl.multiple_of(origin * rows_held, rows_held), rows_held)
        ref, row = (table_ref, step) if step < 2 else (table_more_ref, step - 2)
        token_ref[target, :] = ref[row * rows_held : (row + 1) * rows_held, :]
    tokens = token_ref[...]
    key_ref[...] = jnp.dot(tokens, w_key_ref[...], preferred_element_type=F32).astype(BF16)
    value_ref[...] = lax.dot_general(
        w_value_ref[...], tokens, (((0,), (1,)), ((), ())), preferred_element_type=F32
    ).astype(BF16)
    factor = head_width ** (-0.5) * math.log2(math.e)
    half, chunk = capacity // 2, 256
    group = LANES // half
    for block in range(sources * capacity // LANES):
        side, first_source = divmod(block * group, sources)
        senders = slice(first_source, first_source + group)
        lanes = slice(block * LANES, (block + 1) * LANES)
        for head in range(HEADS):
            columns = slice(head * head_width, (head + 1) * head_width)
            top = head * capacity + side * half
            query = received_ref[senders, top : top + half, :].reshape(LANES, head_width)
            number = block * HEADS + head
            if first_part:
                peak = jnp.full((1, LANES), 2 * ABSENT, F32)
                total = jnp.zeros((1, LANES), F32)
                mixed = jnp.zeros((head_width, LANES), F32)
            else:
                peak = stats_in_ref[number, 0:1, :]
                total = stats_in_ref[number, 1:2, :]
                mixed = mixed_in_ref[number]
            for first in range(0, key_ref.shape[0], chunk):
                part = slice(first, first + chunk)
                holders = slice(first // rows_held, (first + chunk) // rows_held)
                scores = lax.dot_general(
                    key_ref[part, columns], query, NT, preferred_element_type=F32
                )
                logcount = logcount_ref[holders, core, :, lanes].reshape(chunk, LANES)
                scores = scores * factor + logcount
                higher = jnp.maximum(peak, jnp.max(scores, axis=0, keepdims=True))
                raised = jnp.exp2(scores - higher)
                shrink = jnp.exp2(peak - higher)
                total = total * shrink + jnp.sum(raised, axis=0, keepdims=True)
                mixed = mixed * shrink + jnp.dot(
                    value_ref[columns, part], raised.astype(BF16), preferred_element_type=F32
                )
                peak = higher
            if first_part:
                mixed_out_ref[number] = mixed
                stats_out_ref[number, 0:1, :] = peak
                stats_out_ref[number, 1:2, :] = total
            else:
                mixed_ref[senders, side * half : (side + 1) * half, columns] = (
                    jnp.transpose(mixed / total).astype(BF16).reshape(group, half, head_width)
                )


def pick_kernel(region_count, capacity, region_ref, after_ref, pick_ref):
    rows, slot_count = pick_ref.shape
    slot_row = slots_of(region_ref[...], region_count, capacity)
    slot_column = jnp.transpose(jnp.broadcast_to(slot_row, (LANES, rows)))
    pick_ref[...] = jnp.concatenate(
        [
            (lax.broadcasted_iota(jnp.int32, (rows, LANES), 1) + first).astype(F32) == slot_column
            for first in range(0, slot_count, LANES)
        ],
        axis=1,
    ).astype(BF16)


def finish_kernel(
    feats_ref,
    pick_ref,
    returned_ref,
    w_out_ref,
    gain_ref,
    w_up_ref,
    w_down_ref,
    refined_ref,
):
    mixed = jnp.dot(pick_ref[...], returned_ref[...], preferred_element_type=F32).astype(BF16)
    resid = feats_ref[...].astype(F32) + jnp.dot(
        mixed, w_out_ref[...], preferred_element_type=F32
    )
    meansq = jnp.mean(resid * resid, axis=1, keepdims=True)
    normed = (resid * lax.rsqrt(meansq + 1e-05) * gain_ref[...]).astype(BF16)
    hidden = jax.nn.gelu(
        jnp.dot(normed, w_up_ref[...], preferred_element_type=F32), approximate=True
    ).astype(BF16)
    refined_ref[...] = (
        resid + jnp.dot(hidden, w_down_ref[...], preferred_element_type=F32)
    ).astype(BF16)


def params(mebibytes):
    return pltpu.CompilerParams(vmem_limit_bytes=mebibytes << 20)


def on_device(
    query_feats,
    query_region,
    neighbors,
    latents,
    w_query,
    w_key,
    w_value,
    w_out,
    norm_gain,
    w_up,
    w_down,
):
    region_count = lax.axis_size("region")
    shard_count = lax.axis_size("shard")
    chips = shard_count // 2
    query_count, width = query_feats.shape
    neighbor_count = neighbors.shape[1]
    capacity = min(query_count, 2 * query_count // region_count)
    slot_count = region_count * capacity
    table_rows = latents.shape[0] * chips
    region_row = query_region.reshape(1, query_count)
    payload = (region_count, width // LANES * capacity + capacity // 2, LANES)

    def fetch(table, chip_offset, other_offset=None):
        steps = (chip_offset, chip_offset if other_offset is None else other_offset)
        pairs = [
            ((chip + steps[core]) % chips * 2 + core, chip * 2 + core)
            for chip in range(chips)
            for core in range(2)
        ]
        return lax.ppermute(table, "shard", pairs)

    def swap(table):
        return lax.ppermute(table, "shard", [(place, place ^ 1) for place in range(shard_count)])

    def join(pieces, flops, name):
        rows = sum(piece.shape[0] for piece in pieces)
        return pl.pallas_call(
            join_kernel,
            out_shape=jax.ShapeDtypeStruct((rows, width), BF16),
            in_specs=[VMEM] * len(pieces),
            out_specs=VMEM,
            compiler_params=params(4),
            cost_estimate=pl.CostEstimate(flops=flops, bytes_accessed=0, transcendentals=0),
            name=name,
        )(*pieces)

    opposite = fetch(latents, 4)
    send = pl.pallas_call(
        functools.partial(pack_kernel, region_count, capacity),
        out_shape=jax.ShapeDtypeStruct(payload, BF16),
        in_specs=[pl.BlockSpec(memory_space=pl.ANY)] * 4,
        out_specs=VMEM,
        scratch_shapes=[
            pltpu.VMEM((query_count, width), BF16),
            pltpu.VMEM((1, query_count), jnp.int32),
            pltpu.VMEM((neighbor_count, query_count), jnp.int32),
            pltpu.VMEM((width, width), BF16),
            pltpu.SemaphoreType.DMA((4,)),
        ],
        compiler_params=params(56),
        name="pack",
    )(query_feats, region_row, neighbors.T, w_query)
    received = lax.all_to_all(send, "region", split_axis=0, concat_axis=0, tiled=True)
    near = join([latents, opposite], 10**11, "join_near")
    pick = pl.pallas_call(
        functools.partial(pick_kernel, region_count, capacity),
        out_shape=jax.ShapeDtypeStruct((query_count, slot_count), BF16),
        in_specs=[VMEM] * 2,
        out_specs=VMEM,
        compiler_params=params(4),
        cost_estimate=pl.CostEstimate(flops=10**10, bytes_accessed=0, transcendentals=0),
        name="pick",
    )(region_row, near)
    received, pick = lax.optimization_barrier((received, pick))
    logcount = pl.pallas_call(
        functools.partial(count_kernel, neighbor_count),
        out_shape=jax.ShapeDtypeStruct((chips, 2, latents.shape[0], slot_count), F32),
        in_specs=[VMEM],
        out_specs=VMEM,
        scratch_shapes=[
            pltpu.VMEM((slot_count // LANES, neighbor_count, LANES), jnp.int32),
            pltpu.VMEM((slot_count // LANES, neighbor_count, LANES), jnp.int32),
        ],
        compiler_params=params(8),
        name="count",
    )(received)
    arrivals = [fetch(near, 1), fetch(near, -1), fetch(near, 2, -2)]
    arrivals, logcount = lax.optimization_barrier((arrivals, logcount))
    near_more = join(arrivals, 0, "join_more")
    far = swap(near)
    far_more = swap(near_more)
    scratch = [
        pltpu.VMEM((table_rows, width), BF16),
        pltpu.VMEM((table_rows, width), BF16),
        pltpu.VMEM((width, table_rows), BF16),
    ]
    groups = slot_count // LANES * HEADS
    sums = pl.pallas_call(
        functools.partial(attend_kernel, True, latents.shape[0]),
        out_shape=[
            jax.ShapeDtypeStruct((groups, width // HEADS, LANES), F32),
            jax.ShapeDtypeStruct((groups, 8, LANES), F32),
        ],
        in_specs=[VMEM] * 6,
        out_specs=[VMEM] * 2,
        scratch_shapes=scratch,
        compiler_params=params(16),
        cost_estimate=pl.CostEstimate(flops=10**10, bytes_accessed=0, transcendentals=0),
        name="attend_near",
    )(received, logcount, near, near_more, w_key, w_value)
    mixed = pl.pallas_call(
        functools.partial(attend_kernel, False, latents.shape[0]),
        out_shape=jax.ShapeDtypeStruct((region_count, capacity, width), BF16),
        in_specs=[VMEM] * 8,
        out_specs=VMEM,
        scratch_shapes=scratch,
        compiler_params=params(16),
        name="attend_far",
    )(received, logcount, far, far_more, w_key, w_value, *sums)
    returned = lax.all_to_all(
        mixed, "region", split_axis=0, concat_axis=0, tiled=True
    ).reshape(slot_count, width)
    return pl.pallas_call(
        finish_kernel,
        out_shape=jax.ShapeDtypeStruct((query_count, width), BF16),
        in_specs=[VMEM] * 7,
        out_specs=VMEM,
        compiler_params=params(24),
        name="finish",
    )(query_feats, pick, returned, w_out, norm_gain.reshape(1, width), w_up, w_down)


def solution(mesh):
    in_specs = (P(("region", "shard"), None),) * 4 + (P(),) * 7
    out_specs = P(("region", "shard"), None)
    return jax.shard_map(
        on_device, mesh=mesh, in_specs=in_specs, out_specs=out_specs, check_vma=False
    )
```

time: 57.6 us -> 53.3 us (0.925)
  blocking collectives: 15.8 us -> 13.2 us
  starting transfers between devices: 23.7 us -> 21.9 us
  waiting for transfers between devices: 4.17 us -> 5.45 us
  local copies, waits for them, and re-layouts: 0.89 us -> 0.05 us
    all_to_all x1, waiting for transfers between devices: 0.96 us -> 5.44 us  [on_device(): lax.all_to_all(send, 'region', split_axis=0, concat_axis=0, tiled=True)]
    ppermute x6, waiting for transfers between devices: 3.2 us -> 0.02 us  [the longest x4 0.01 us: fetch(): return lax.ppermute(table, 'shard', pairs)]
    all_to_all x1, blocking collectives: 15.8 us -> 13.2 us  [on_device(): lax.all_to_all(mixed, 'region', split_axis=0, concat_axis=0, tiled=True)]
    ppermute x6, starting transfers between devices: 16.9 us -> 15.2 us  [the longest x4 11.6 us: fetch(): return lax.ppermute(table, 'shard', pairs)]
    unnamed x18, local copies, waits for them, and re-layouts: 0.89 us -> 0.05 us
    pallas_call x1, Pallas kernels: 2.81 us -> 2.02 us  [on_device(): pl.pallas_call(functools.partial(count_kernel, neighbor_count), out_shape...]
    pallas_call x4 -> x7, Pallas kernels: 9.83 us -> 10.2 us  [the longest x1 2.76 us: on_device(): pl.pallas_call(finish_kernel, out_shape=jax.ShapeDtypeStruct((query_count...]
  transfers between devices with their start and end apart: 7 -> 7, of which waited for: 2 -> 1; matrix products, arithmetic and copies ran while one was open for 0% -> 0% of each run, Pallas kernels for 9% -> 13%
where the time goes in v3:
time: 53.3 us; the launch traced here: 53 us
  starting transfers between devices  21.9 us (41%)
  blocking collectives  13.2 us (25%)
  Pallas kernels  12.2 us (23%)
  waiting for transfers between devices  5.45 us (10%)
    all_to_all x1, blocking collectives, on_device(): lax.all_to_all(mixed, 'region', split_axis=0, concat_axis=0, tiled=True)  13.2 us
    ppermute x4, starting transfers between devices, fetch(): return lax.ppermute(table, 'shard', pairs)  11.6 us
    all_to_all x1, starting transfers between devices, on_device(): lax.all_to_all(send, 'region', split_axis=0, concat_axis=0, tiled=True)  6.77 us
    all_to_all x1, waiting for transfers between devices, on_device(): lax.all_to_all(send, 'region', split_axis=0, concat_axis=0, tiled=True)  5.44 us
    ppermute x2, starting transfers between devices, swap(): lax.ppermute(table, 'shard', [(place, place ^ 1) for place in range(shard...  3.58 us
    pallas_call x1, Pallas kernels, on_device(): pl.pallas_call(finish_kernel, out_shape=jax.ShapeDtypeStruct((query_count...  2.76 us
    pallas_call x1, Pallas kernels, on_device(): pl.pallas_call(functools.partial(pack_kernel, region_count, capacity), ou...  2.59 us
    pallas_call x1, Pallas kernels, on_device(): pl.pallas_call(functools.partial(attend_kernel, False, latents.shape[0]),...  2.35 us
  transfers between devices with their start and end apart: 7, of which 1 were waited for; matrix products, arithmetic and copies ran while one was open for 0% of the time, Pallas kernels for 13%

profile of v3, /device:TPU:1, one launch (start us, length us, event | category | flops | bytes accessed | tf_op | source)
XLA Modules:
  0.0 53.0 jit_solution(12259566402523887503)
XLA Ops:
  0.0 0.0 copy-start.8
  0.0 7.7 %collective-permute-start = (bf16[64,512]{1,0:T(8,128)(2,1)}, bf16[64,512]{1,0:T(8,128)(2,1)S(1)}, u32[]{:S(2)}, u32[]{:S(2)}) collective-permute-start(bf16[64,512]{1,0:T(8,128)(2,1)} %refs_0_.1), channel_id=1, source_target_pairs={{8,0},{9,1},{10,2},{11,3},{12,4},{13,5},{14,6},{15,7},{0,8},{1,9},... | collective-permute-start | bytes 196616 | tf_op jit(solution)/shard_map/ppermute | solution.py:288
  7.7 2.6 %pack.1 = bf16[16,144,128]{2,1,0:T(8,128)(2,1)} custom-call(bf16[256,512]{1,0:T(8,128)(2,1)} %feats_ref.1, s32[1,256]{1,0:T(1,128)} %bitcast.6, s32[64,256]{1,0:T(8,128)} %bitcast.8, bf16[512,512]{1,0:T(8,128)(2,1)} %w_query_hbm.1), custom_call_target="tpu_custom_call" | custom-call | tf_op jit(solution)/shard_map/pack/pallas_call | solution.py:306
  10.3 6.8 %all-to-all-start = ((bf16[16,144,128]{2,1,0:T(8,128)(2,1)}), bf16[16,144,128]{2,1,0:T(8,128)(2,1)S(1)}, u32[]{:S(2)}, u32[]{:S(2)}) async-start(bf16[16,144,128]{2,1,0:T(8,128)(2,1)} %pack.1), calls=%async_computation | async-start | bytes 1179648 | tf_op jit(solution)/shard_map/all_to_all | solution.py:321
  17.1 0.0 copy-start.7
  17.1 0.0 collective-permute-done.refs_1_
  17.1 0.0 copy-done.8
  17.2 1.3 %collective-permute-start.4 = (bf16[128,512]{1,0:T(8,128)(2,1)S(1)}, bf16[128,512]{1,0:T(8,128)(2,1)S(1)}, u32[]{:S(2)}, u32[]{:S(2)}) collective-permute-start(bf16[128,512]{1,0:T(8,128)(2,1)S(1)} %join_near.1.after_ref.table_ref), channel_id=1, source_target_pairs={{0,1},{1,0},{2,3},{3,2},{4,5},{5,4},{6,7},{7,6},{8,9},{9,8},{10,11... | collective-permute-start | bytes 393224 | tf_op jit(solution)/shard_map/ppermute | solution.py:291
  18.5 1.2 %collective-permute-start.3 = (bf16[128,512]{1,0:T(8,128)(2,1)S(1)}, bf16[128,512]{1,0:T(8,128)(2,1)S(1)}, u32[]{:S(2)}, u32[]{:S(2)}) collective-permute-start(bf16[128,512]{1,0:T(8,128)(2,1)S(1)} %join_near.1.after_ref.table_ref), channel_id=1, source_target_pairs={{4,0},{13,1},{6,2},{15,3},{8,4},{1,5},{10,6},{3,7},{12,8},{5,9},{1... | collective-permute-start | bytes 393224 | tf_op jit(solution)/shard_map/ppermute | solution.py:288
  19.7 0.7 %collective-permute-start.2 = (bf16[128,512]{1,0:T(8,128)(2,1)S(1)}, bf16[128,512]{1,0:T(8,128)(2,1)S(1)}, u32[]{:S(2)}, u32[]{:S(2)}) collective-permute-start(bf16[128,512]{1,0:T(8,128)(2,1)S(1)} %join_near.1.after_ref.table_ref), channel_id=1, source_target_pairs={{14,0},{15,1},{0,2},{1,3},{2,4},{3,5},{4,6},{5,7},{6,8},{7,9},{8,1... | collective-permute-start | bytes 393224 | tf_op jit(solution)/shard_map/ppermute | solution.py:288
  20.4 1.9 %collective-permute-start.1 = (bf16[128,512]{1,0:T(8,128)(2,1)S(1)}, bf16[128,512]{1,0:T(8,128)(2,1)S(1)}, u32[]{:S(2)}, u32[]{:S(2)}) collective-permute-start(bf16[128,512]{1,0:T(8,128)(2,1)S(1)} %join_near.1.after_ref.table_ref), channel_id=1, source_target_pairs={{2,0},{3,1},{4,2},{5,3},{6,4},{7,5},{8,6},{9,7},{10,8},{11,9},{12,... | collective-permute-start | bytes 393224 | tf_op jit(solution)/shard_map/ppermute | solution.py:288
  22.4 0.0 copy-done.7
  22.4 0.3 pick.1.pick_ref
  22.6 0.0 copy-start.3
  22.7 0.0 copy-start.4
  22.7 5.4 %all-to-all-done.received_ref = bf16[16,144,128]{2,1,0:T(8,128)(2,1)S(1)} async-done(((bf16[16,144,128]{2,1,0:T(8,128)(2,1)}), bf16[16,144,128]{2,1,0:T(8,128)(2,1)S(1)}, u32[]{:S(2)}, u32[]{:S(2)}) %all-to-all-start) | async-done | bytes 589856 | tf_op jit(solution)/shard_map/all_to_all | solution.py:321
  28.1 2.0 %count.1.logcount_ref = f32[8,2,64,512]{3,2,1,0:T(8,128)S(1)} custom-call(bf16[16,144,128]{2,1,0:T(8,128)(2,1)S(1)} %all-to-all-done.received_ref), custom_call_target="tpu_custom_call" | custom-call | tf_op jit(solution)/shard_map/count/pallas_call | solution.py:333
  30.1 0.0 collective-permute-done.3.refs_2_
  30.1 0.0 collective-permute-done.2.refs_1_
  30.2 0.0 collective-permute-done.1.refs_0_
  30.2 2.2 %collective-permute-start.5 = (bf16[384,512]{1,0:T(8,128)(2,1)S(1)}, bf16[384,512]{1,0:T(8,128)(2,1)S(1)}, u32[]{:S(2)}, u32[]{:S(2)}) collective-permute-start(bf16[384,512]{1,0:T(8,128)(2,1)S(1)} %join_more.1.table_more_ref), channel_id=1, source_target_pairs={{0,1},{1,0},{2,3},{3,2},{4,5},{5,4},{6,7},{7,6},{8,9},{9,8},{10,11... | collective-permute-start | bytes 1179656 | tf_op jit(solution)/shard_map/ppermute | solution.py:291
  32.5 0.0 copy-done.3
  32.5 0.0 copy-done.4
  32.5 2.2 %attend_near.1 = (f32[16,128,128]{2,1,0:T(8,128)S(1)}, f32[16,8,128]{2,1,0:T(8,128)S(1)}) custom-call(bf16[16,144,128]{2,1,0:T(8,128)(2,1)S(1)} %all-to-all-done.received_ref, f32[8,2,64,512]{3,2,1,0:T(8,128)S(1)} %count.1.logcount_ref, bf16[128,512]{1,0:T(8,128)(2,1)S(1)} %join_near.1.after_ref.table_ref, bf16[384,512]{1,0:T(8,128)(2,1)S(1)} %join_more.1.table_more_ref, ...), custom_call_target="tpu_custom_call" | custom-call | flops 10000000000 | tf_op jit(solution)/shard_map/attend_near/pallas_call | solution.py:356
  34.6 0.0 collective-permute-done.4.table_ref
  34.6 0.0 collective-permute-done.5.table_more_ref
  34.7 0.0 copy-start
  34.7 0.0 copy-start.1
  34.7 0.0 copy-start.2
  34.7 0.0 copy-start.5
  34.7 0.0 copy-start.6
  34.7 2.4 %attend_far.1 = bf16[16,32,512]{2,1,0:T(8,128)(2,1)S(1)} custom-call(bf16[16,144,128]{2,1,0:T(8,128)(2,1)S(1)} %all-to-all-done.received_ref, f32[8,2,64,512]{3,2,1,0:T(8,128)S(1)} %count.1.logcount_ref, bf16[128,512]{1,0:T(8,128)(2,1)S(1)} %collective-permute-done.4.table_ref, bf16[384,512]{1,0:T(8,128)(2,1)S(1)} %collective-permute-done.5.table_more_ref, ...), custom_call_target="tpu_custom_call" | custom-call | tf_op jit(solution)/shard_map/attend_far/pallas_call | solution.py:369
  37.1 13.2 %all_to_all.10 = bf16[16,32,512]{2,1,0:T(8,128)(2,1)S(1)} all-to-all(bf16[16,32,512]{2,1,0:T(8,128)(2,1)S(1)} %attend_far.1), channel_id=1, replica_groups=mesh['region'=16,'shard'=16] {'region'}, dimensions={0} | all-to-all | bytes 1048576 | tf_op jit(solution)/shard_map/all_to_all | solution.py:378
  50.2 0.0 copy-done
  50.2 0.0 copy-done.1
  50.2 0.0 copy-done.2
  50.2 0.0 copy-done.5
  50.3 0.0 copy-done.6
  50.3 2.8 %finish.1 = bf16[256,512]{1,0:T(8,128)(2,1)} custom-call(bf16[256,512]{1,0:T(8,128)(2,1)S(1)} %copy-done.2, bf16[256,512]{1,0:T(8,128)(2,1)S(1)} %pick.1.pick_ref, bf16[512,512]{1,0:T(8,128)(2,1)S(1)} %bitcast.4, bf16[512,512]{1,0:T(8,128)(2,1)S(1)} %copy-done.5, f32[1,512]{1,0:T(1,128)S(1)} %bitcast.5, bf16[512,2048]{1,0:T(8,128)(2,1)S(1)} %copy-done, ...), custom_call_target="tpu_custom_call" | custom-call | tf_op jit(solution)/shard_map/finish/pallas_call | solution.py:381
  (2 shorter events, 0.0 us)
Async XLA Ops:
  0.0 17.1 %copy-start.8 = (bf16[64,512]{1,0:T(8,128)(2,1)S(1)}, bf16[64,512]{1,0:T(8,128)(2,1)}, u32[]{:S(2)}) copy-start(bf16[64,512]{1,0:T(8,128)(2,1)} %refs_0_.1) | copy-start | bytes 196612
  0.0 17.1 %collective-permute-start = (bf16[64,512]{1,0:T(8,128)(2,1)}, bf16[64,512]{1,0:T(8,128)(2,1)S(1)}, u32[]{:S(2)}, u32[]{:S(2)}) collective-permute-start(bf16[64,512]{1,0:T(8,128)(2,1)} %refs_0_.1), channel_id=1, source_target_pairs={{8,0},{9,1},{10,2},{11,3},{12,4},{13,5},{14,6},{15,7},{0,8},{1,9},... | collective-permute-start | bytes 196616 | tf_op jit(solution)/shard_map/ppermute | solution.py:288
  10.3 17.8 %all-to-all-start = ((bf16[16,144,128]{2,1,0:T(8,128)(2,1)}), bf16[16,144,128]{2,1,0:T(8,128)(2,1)S(1)}, u32[]{:S(2)}, u32[]{:S(2)}) async-start(bf16[16,144,128]{2,1,0:T(8,128)(2,1)} %pack.1), calls=%async_computation | async-start | bytes 1179648 | tf_op jit(solution)/shard_map/all_to_all | solution.py:321
  17.1 5.2 %copy-start.7 = (s32[256,1]{0,1:T(1,128)S(1)}, s32[256,1]{0,1:T(1,128)}, u32[]{:S(2)}) copy-start(s32[256,1]{0,1:T(1,128)} %param.12) | copy-start | bytes 3076
  17.2 17.5 %collective-permute-start.4 = (bf16[128,512]{1,0:T(8,128)(2,1)S(1)}, bf16[128,512]{1,0:T(8,128)(2,1)S(1)}, u32[]{:S(2)}, u32[]{:S(2)}) collective-permute-start(bf16[128,512]{1,0:T(8,128)(2,1)S(1)} %join_near.1.after_ref.table_ref), channel_id=1, source_target_pairs={{0,1},{1,0},{2,3},{3,2},{4,5},{5,4},{6,7},{7,6},{8,9},{9,8},{10,11... | collective-permute-start | bytes 393224 | tf_op jit(solution)/shard_map/ppermute | solution.py:291
  18.5 11.6 %collective-permute-start.3 = (bf16[128,512]{1,0:T(8,128)(2,1)S(1)}, bf16[128,512]{1,0:T(8,128)(2,1)S(1)}, u32[]{:S(2)}, u32[]{:S(2)}) collective-permute-start(bf16[128,512]{1,0:T(8,128)(2,1)S(1)} %join_near.1.after_ref.table_ref), channel_id=1, source_target_pairs={{4,0},{13,1},{6,2},{15,3},{8,4},{1,5},{10,6},{3,7},{12,8},{5,9},{1... | collective-permute-start | bytes 393224 | tf_op jit(solution)/shard_map/ppermute | solution.py:288
  19.7 10.5 %collective-permute-start.2 = (bf16[128,512]{1,0:T(8,128)(2,1)S(1)}, bf16[128,512]{1,0:T(8,128)(2,1)S(1)}, u32[]{:S(2)}, u32[]{:S(2)}) collective-permute-start(bf16[128,512]{1,0:T(8,128)(2,1)S(1)} %join_near.1.after_ref.table_ref), channel_id=1, source_target_pairs={{14,0},{15,1},{0,2},{1,3},{2,4},{3,5},{4,6},{5,7},{6,8},{7,9},{8,1... | collective-permute-start | bytes 393224 | tf_op jit(solution)/shard_map/ppermute | solution.py:288
  20.4 9.7 %collective-permute-start.1 = (bf16[128,512]{1,0:T(8,128)(2,1)S(1)}, bf16[128,512]{1,0:T(8,128)(2,1)S(1)}, u32[]{:S(2)}, u32[]{:S(2)}) collective-permute-start(bf16[128,512]{1,0:T(8,128)(2,1)S(1)} %join_near.1.after_ref.table_ref), channel_id=1, source_target_pairs={{2,0},{3,1},{4,2},{5,3},{6,4},{7,5},{8,6},{9,7},{10,8},{11,9},{12,... | collective-permute-start | bytes 393224 | tf_op jit(solution)/shard_map/ppermute | solution.py:288
  22.6 9.8 %copy-start.3 = (bf16[512,512]{1,0:T(8,128)(2,1)S(1)}, bf16[512,512]{1,0:T(8,128)(2,1)}, u32[]{:S(2)}) copy-start(bf16[512,512]{1,0:T(8,128)(2,1)} %w_key_ref.3) | copy-start | bytes 1572868
  22.7 9.8 %copy-start.4 = (bf16[512,512]{1,0:T(8,128)(2,1)S(1)}, bf16[512,512]{1,0:T(8,128)(2,1)}, u32[]{:S(2)}) copy-start(bf16[512,512]{1,0:T(8,128)(2,1)} %w_value_ref.3) | copy-start | bytes 1572868
  30.2 4.4 %collective-permute-start.5 = (bf16[384,512]{1,0:T(8,128)(2,1)S(1)}, bf16[384,512]{1,0:T(8,128)(2,1)S(1)}, u32[]{:S(2)}, u32[]{:S(2)}) collective-permute-start(bf16[384,512]{1,0:T(8,128)(2,1)S(1)} %join_more.1.table_more_ref), channel_id=1, source_target_pairs={{0,1},{1,0},{2,3},{3,2},{4,5},{5,4},{6,7},{7,6},{8,9},{9,8},{10,11... | collective-permute-start | bytes 1179656 | tf_op jit(solution)/shard_map/ppermute | solution.py:291
  34.7 15.6 %copy-start = (bf16[512,2048]{1,0:T(8,128)(2,1)S(1)}, bf16[512,2048]{1,0:T(8,128)(2,1)}, u32[]{:S(2)}) copy-start(bf16[512,2048]{1,0:T(8,128)(2,1)} %w_up_ref.1) | copy-start | bytes 6291460
  34.7 15.6 %copy-start.1 = (bf16[2048,512]{1,0:T(8,128)(2,1)S(1)}, bf16[2048,512]{1,0:T(8,128)(2,1)}, u32[]{:S(2)}) copy-start(bf16[2048,512]{1,0:T(8,128)(2,1)} %w_down_ref.1) | copy-start | bytes 6291460
  34.7 15.6 %copy-start.2 = (bf16[256,512]{1,0:T(8,128)(2,1)S(1)}, bf16[256,512]{1,0:T(8,128)(2,1)}, u32[]{:S(2)}) copy-start(bf16[256,512]{1,0:T(8,128)(2,1)} %feats_ref.1) | copy-start | bytes 786436
  34.7 15.6 %copy-start.5 = (bf16[512,512]{1,0:T(8,128)(2,1)S(1)}, bf16[512,512]{1,0:T(8,128)(2,1)}, u32[]{:S(2)}) copy-start(bf16[512,512]{1,0:T(8,128)(2,1)} %w_out_ref.1) | copy-start | bytes 1572868
  34.7 15.6 %copy-start.6 = (f32[512]{0:T(512)S(1)}, f32[512]{0:T(512)}, u32[]{:S(2)}) copy-start(f32[512]{0:T(512)} %param.19) | copy-start | bytes 6148

commit v4 on v3

--- a/solution.py
+++ b/solution.py
@@ -28,52 +28,48 @@
     return region_row.astype(F32) * float(capacity) + rank
 
 
-def pack_kernel(
-    region_count,
-    capacity,
-    feats_hbm,
-    region_hbm,
-    neighbors_hbm,
-    w_query_hbm,
-    send_ref,
-    feats_ref,
-    region_ref,
-    neighbors_ref,
-    w_query_ref,
-    arrived,
-):
-    sources = (region_hbm, neighbors_hbm, feats_hbm, w_query_hbm)
-    targets = (region_ref, neighbors_ref, feats_ref, w_query_ref)
-    copies = [
-        pltpu.make_async_copy(source, target, arrived.at[number])
-        for number, (source, target) in enumerate(zip(sources, targets))
-    ]
-    for copy in copies:
-        copy.start()
-    slot_count = region_count * capacity
-    rows, width = feats_ref.shape
-    copies[0].wait()
-    slot_row = slots_of(region_ref[...], region_count, capacity)
-    place = (
-        lax.broadcasted_iota(jnp.int32, (slot_count, rows), 0).astype(F32) == slot_row
-    ).astype(BF16)
-    copies[1].wait()
-    number = neighbors_ref[...]
-    coded = ((number & 127) + 128) << (number >> 7)
-    coded = coded.astype(F32).astype(BF16)
-    spread = lax.dot_general(place, coded, NT, preferred_element_type=F32)
-    spread = spread.reshape(region_count, capacity, spread.shape[1])
-    half = capacity // 2
-    spread = jnp.concatenate([spread[:, :half], spread[:, half:]], axis=2)
-    send_ref[:, width // LANES * capacity :, :] = spread.astype(BF16)
-    copies[2].wait()
-    copies[3].wait()
-    query = jnp.dot(feats_ref[...], w_query_ref[...], preferred_element_type=F32).astype(BF16)
-    placed = jnp.dot(place, query, preferred_element_type=F32).astype(BF16)
-    for head in range(width // LANES):
-        send_ref[:, head * capacity : (head + 1) * capacity, :] = placed[
-            :, head * LANES : (head + 1) * LANES
-        ].reshape(region_count, capacity, LANES)
+def pack_kernel(region_count, capacity, early_turn, *refs):
+    feats_hbm, region_hbm, neighbors_hbm, w_query_hbm = refs[:4]
+    send_hbm, feats_ref, region_ref, neighbors_ref, w_query_ref, send_ref, arrived, left = refs[-8:]
+    early = lax.axis_index("shard") < lax.axis_size("shard") * 3 // 8
+
+    @pl.when(early if early_turn else jnp.logical_not(early))
+    def _():
+        sources = (region_hbm, neighbors_hbm, feats_hbm, w_query_hbm)
+        targets = (region_ref, neighbors_ref, feats_ref, w_query_ref)
+        copies = [
+            pltpu.make_async_copy(source, target, arrived.at[number])
+            for number, (source, target) in enumerate(zip(sources, targets))
+        ]
+        for copy in copies:
+            copy.start()
+        slot_count = region_count * capacity
+        rows, width = feats_ref.shape
+        copies[0].wait()
+        slot_row = slots_of(region_ref[...], region_count, capacity)
+        place = (
+            lax.broadcasted_iota(jnp.int32, (slot_count, rows), 0).astype(F32) == slot_row
+        ).astype(BF16)
+        copies[1].wait()
+        number = neighbors_ref[...]
+        coded = ((number & 127) + 128) << (number >> 7)
+        coded = coded.astype(F32).astype(BF16)
+        spread = lax.dot_general(place, coded, NT, preferred_element_type=F32)
+        spread = spread.reshape(region_count, capacity, spread.shape[1])
+        half = capacity // 2
+        spread = jnp.concatenate([spread[:, :half], spread[:, half:]], axis=2)
+        send_ref[:, width // LANES * capacity :, :] = spread.astype(BF16)
+        copies[2].wait()
+        copies[3].wait()
+        query = jnp.dot(feats_ref[...], w_query_ref[...], preferred_element_type=F32)
+        placed = jnp.dot(place, query.astype(BF16), preferred_element_type=F32).astype(BF16)
+        for head in range(width // LANES):
+            send_ref[:, head * capacity : (head + 1) * capacity, :] = placed[
+                :, head * LANES : (head + 1) * LANES
+            ].reshape(region_count, capacity, LANES)
+        leaving = pltpu.make_async_copy(send_ref, send_hbm, left)
+        leaving.start()
+        leaving.wait()
 
 
 def count_kernel(neighbor_count, received_ref, logcount_ref, low_ref, digit_ref):
@@ -302,22 +298,30 @@
             name=name,
         )(*pieces)
 
+    def pack(early_turn, *begun):
+        anywhere = pl.BlockSpec(memory_space=pl.ANY)
+        return pl.pallas_call(
+            functools.partial(pack_kernel, region_count, capacity, early_turn),
+            out_shape=jax.ShapeDtypeStruct(payload, BF16),
+            in_specs=[anywhere] * (4 + len(begun)),
+            out_specs=anywhere,
+            scratch_shapes=[
+                pltpu.VMEM((query_count, width), BF16),
+                pltpu.VMEM((1, query_count), jnp.int32),
+                pltpu.VMEM((neighbor_count, query_count), jnp.int32),
+                pltpu.VMEM((width, width), BF16),
+                pltpu.VMEM(payload, BF16),
+                pltpu.SemaphoreType.DMA((4,)),
+                pltpu.SemaphoreType.DMA,
+            ],
+            input_output_aliases={4: 0} if begun else {},
+            compiler_params=params(56),
+            name="pack_early" if early_turn else "pack_late",
+        )(query_feats, region_row, neighbors.T, w_query, *begun)
+
+    begun, latents = lax.optimization_barrier((pack(True), latents))
     opposite = fetch(latents, 4)
-    send = pl.pallas_call(
-        functools.partial(pack_kernel, region_count, capacity),
-        out_shape=jax.ShapeDtypeStruct(payload, BF16),
-        in_specs=[pl.BlockSpec(memory_space=pl.ANY)] * 4,
-        out_specs=VMEM,
-        scratch_shapes=[
-            pltpu.VMEM((query_count, width), BF16),
-            pltpu.VMEM((1, query_count), jnp.int32),
-            pltpu.VMEM((neighbor_count, query_count), jnp.int32),
-            pltpu.VMEM((width, width), BF16),
-            pltpu.SemaphoreType.DMA((4,)),
-        ],
-        compiler_params=params(56),
-        name="pack",
-    )(query_feats, region_row, neighbors.T, w_query)
+    send = pack(False, begun)
     received = lax.all_to_all(send, "region", split_axis=0, concat_axis=0, tiled=True)
     near = join([latents, opposite], 10**11, "join_near")
     pick = pl.pallas_call(

time: 53.3 us -> 51.8 us (0.972)
  starting transfers between devices: 21.9 us -> 20.1 us
  blocking collectives: 13.2 us -> 14.2 us
  waiting for transfers between devices: 5.45 us -> 4.82 us
    ppermute x4, starting transfers between devices: 11.6 us -> 9.72 us  [fetch(): return lax.ppermute(table, 'shard', pairs)]
    all_to_all x1, blocking collectives: 13.2 us -> 14.2 us  [on_device(): lax.all_to_all(mixed, 'region', split_axis=0, concat_axis=0, tiled=True)]
    all_to_all x1, waiting for transfers between devices: 5.44 us -> 4.81 us  [on_device(): lax.all_to_all(send, 'region', split_axis=0, concat_axis=0, tiled=True)]
    pallas_call x1 -> x2, Pallas kernels: 2.59 us -> 2.69 us  [pack(): pl.pallas_call(functools.partial(pack_kernel, region_count, capacity, ear...]
  transfers between devices with their start and end apart: 7 -> 7, of which waited for: 1 -> 1; matrix products, arithmetic and copies ran while one was open for 0% -> 0% of each run, Pallas kernels for 13% -> 9%
where the time goes in v4:
time: 51.8 us; the launch traced here: 51.6 us
  starting transfers between devices  20.1 us (39%)
  blocking collectives  14.2 us (27%)
  Pallas kernels  12.3 us (24%)
  waiting for transfers between devices  4.82 us (9%)
    all_to_all x1, blocking collectives, on_device(): lax.all_to_all(mixed, 'region', split_axis=0, concat_axis=0, tiled=True)  14.2 us
    ppermute x4, starting transfers between devices, fetch(): return lax.ppermute(table, 'shard', pairs)  9.72 us
    all_to_all x1, starting transfers between devices, on_device(): lax.all_to_all(send, 'region', split_axis=0, concat_axis=0, tiled=True)  6.77 us
    all_to_all x1, waiting for transfers between devices, on_device(): lax.all_to_all(send, 'region', split_axis=0, concat_axis=0, tiled=True)  4.81 us
    ppermute x2, starting transfers between devices, swap(): lax.ppermute(table, 'shard', [(place, place ^ 1) for place in range(shard...  3.57 us
    pallas_call x1, Pallas kernels, on_device(): pl.pallas_call(finish_kernel, out_shape=jax.ShapeDtypeStruct((query_count...  2.76 us
    pallas_call x2, Pallas kernels, pack(): pl.pallas_call(functools.partial(pack_kernel, region_count, capacity, ear...  2.69 us
    pallas_call x1, Pallas kernels, on_device(): pl.pallas_call(functools.partial(attend_kernel, False, latents.shape[0]),...  2.36 us
  transfers between devices with their start and end apart: 7, of which 1 were waited for; matrix products, arithmetic and copies ran while one was open for 0% of the time, Pallas kernels for 9%

profile of v4, /device:TPU:1, one launch (start us, length us, event | category | flops | bytes accessed | tf_op | source)
XLA Modules:
  0.0 51.6 jit_solution(227961511199685694)
XLA Ops:
  0.0 0.0 copy-start.8
  0.0 2.6 %pack_early.1.refs_4_ = bf16[16,144,128]{2,1,0:T(8,128)(2,1)} custom-call(bf16[256,512]{1,0:T(8,128)(2,1)} %feats_ref.1, s32[1,256]{1,0:T(1,128)} %bitcast.5, s32[64,256]{1,0:T(8,128)} %bitcast.9, bf16[512,512]{1,0:T(8,128)(2,1)} %refs_3_.3), custom_call_target="tpu_custom_call" | custom-call | tf_op jit(solution)/shard_map/pack_early/pallas_call | solution.py:303
  2.7 5.2 %collective-permute-start = (bf16[64,512]{1,0:T(8,128)(2,1)}, bf16[64,512]{1,0:T(8,128)(2,1)S(1)}, u32[]{:S(2)}, u32[]{:S(2)}) collective-permute-start(bf16[64,512]{1,0:T(8,128)(2,1)} %refs_0_.4), channel_id=1, source_target_pairs={{8,0},{9,1},{10,2},{11,3},{12,4},{13,5},{14,6},{15,7},{0,8},{1,9},... | collective-permute-start | bytes 196616 | tf_op jit(solution)/shard_map/ppermute | solution.py:284
  7.9 6.8 %all-to-all-start = ((bf16[16,144,128]{2,1,0:T(8,128)(2,1)}), bf16[16,144,128]{2,1,0:T(8,128)(2,1)S(1)}, u32[]{:S(2)}, u32[]{:S(2)}) async-start(bf16[16,144,128]{2,1,0:T(8,128)(2,1)} %pack_late.1), calls=%async_computation | async-start | bytes 1179648 | tf_op jit(solution)/shard_map/all_to_all | solution.py:325
  14.7 0.0 copy-start.6
  14.7 0.0 collective-permute-done.refs_1_
  14.7 0.0 copy-done.8
  14.8 1.3 %collective-permute-start.4 = (bf16[128,512]{1,0:T(8,128)(2,1)S(1)}, bf16[128,512]{1,0:T(8,128)(2,1)S(1)}, u32[]{:S(2)}, u32[]{:S(2)}) collective-permute-start(bf16[128,512]{1,0:T(8,128)(2,1)S(1)} %join_near.1.after_ref.table_ref), channel_id=1, source_target_pairs={{0,1},{1,0},{2,3},{3,2},{4,5},{5,4},{6,7},{7,6},{8,9},{9,8},{10,11... | collective-permute-start | bytes 393224 | tf_op jit(solution)/shard_map/ppermute | solution.py:287
  16.1 1.2 %collective-permute-start.3 = (bf16[128,512]{1,0:T(8,128)(2,1)S(1)}, bf16[128,512]{1,0:T(8,128)(2,1)S(1)}, u32[]{:S(2)}, u32[]{:S(2)}) collective-permute-start(bf16[128,512]{1,0:T(8,128)(2,1)S(1)} %join_near.1.after_ref.table_ref), channel_id=1, source_target_pairs={{4,0},{13,1},{6,2},{15,3},{8,4},{1,5},{10,6},{3,7},{12,8},{5,9},{1... | collective-permute-start | bytes 393224 | tf_op jit(solution)/shard_map/ppermute | solution.py:284
  17.3 3.3 %collective-permute-start.2 = (bf16[128,512]{1,0:T(8,128)(2,1)S(1)}, bf16[128,512]{1,0:T(8,128)(2,1)S(1)}, u32[]{:S(2)}, u32[]{:S(2)}) collective-permute-start(bf16[128,512]{1,0:T(8,128)(2,1)S(1)} %join_near.1.after_ref.table_ref), channel_id=1, source_target_pairs={{14,0},{15,1},{0,2},{1,3},{2,4},{3,5},{4,6},{5,7},{6,8},{7,9},{8,1... | collective-permute-start | bytes 393224 | tf_op jit(solution)/shard_map/ppermute | solution.py:284
  20.6 0.0 collective-permute-start.1
  20.6 0.0 copy-done.6
  20.6 0.3 pick.1.pick_ref
  20.9 0.0 copy-start.3
  20.9 0.0 copy-start.4
  20.9 4.8 %all-to-all-done.received_ref = bf16[16,144,128]{2,1,0:T(8,128)(2,1)S(1)} async-done(((bf16[16,144,128]{2,1,0:T(8,128)(2,1)}), bf16[16,144,128]{2,1,0:T(8,128)(2,1)S(1)}, u32[]{:S(2)}, u32[]{:S(2)}) %all-to-all-start) | async-done | bytes 589856 | tf_op jit(solution)/shard_map/all_to_all | solution.py:325
  25.7 2.0 %count.1.logcount_ref = f32[8,2,64,512]{3,2,1,0:T(8,128)S(1)} custom-call(bf16[16,144,128]{2,1,0:T(8,128)(2,1)S(1)} %all-to-all-done.received_ref), custom_call_target="tpu_custom_call" | custom-call | tf_op jit(solution)/shard_map/count/pallas_call | solution.py:337
  27.7 0.0 collective-permute-done.3.refs_2_
  27.7 0.0 collective-permute-done.2.refs_1_
  27.7 0.0 collective-permute-done.1.refs_0_
  27.8 2.3 %collective-permute-start.5 = (bf16[384,512]{1,0:T(8,128)(2,1)S(1)}, bf16[384,512]{1,0:T(8,128)(2,1)S(1)}, u32[]{:S(2)}, u32[]{:S(2)}) collective-permute-start(bf16[384,512]{1,0:T(8,128)(2,1)S(1)} %join_more.1.table_more_ref), channel_id=1, source_target_pairs={{0,1},{1,0},{2,3},{3,2},{4,5},{5,4},{6,7},{7,6},{8,9},{9,8},{10,11... | collective-permute-start | bytes 1179656 | tf_op jit(solution)/shard_map/ppermute | solution.py:287
  30.0 0.0 copy-done.3
  30.0 0.0 copy-done.4
  30.0 2.2 %attend_near.1 = (f32[16,128,128]{2,1,0:T(8,128)S(1)}, f32[16,8,128]{2,1,0:T(8,128)S(1)}) custom-call(bf16[16,144,128]{2,1,0:T(8,128)(2,1)S(1)} %all-to-all-done.received_ref, f32[8,2,64,512]{3,2,1,0:T(8,128)S(1)} %count.1.logcount_ref, bf16[128,512]{1,0:T(8,128)(2,1)S(1)} %join_near.1.after_ref.table_ref, bf16[384,512]{1,0:T(8,128)(2,1)S(1)} %join_more.1.table_more_ref, ...), custom_call_target="tpu_custom_call" | custom-call | flops 10000000000 | tf_op jit(solution)/shard_map/attend_near/pallas_call | solution.py:360
  32.2 0.0 collective-permute-done.4.table_ref
  32.2 0.0 collective-permute-done.5.table_more_ref
  32.2 0.0 copy-start
  32.2 0.0 copy-start.1
  32.3 0.0 copy-start.2
  32.3 0.0 copy-start.5
  32.3 0.0 copy-start.7
  32.3 2.4 %attend_far.1 = bf16[16,32,512]{2,1,0:T(8,128)(2,1)S(1)} custom-call(bf16[16,144,128]{2,1,0:T(8,128)(2,1)S(1)} %all-to-all-done.received_ref, f32[8,2,64,512]{3,2,1,0:T(8,128)S(1)} %count.1.logcount_ref, bf16[128,512]{1,0:T(8,128)(2,1)S(1)} %collective-permute-done.4.table_ref, bf16[384,512]{1,0:T(8,128)(2,1)S(1)} %collective-permute-done.5.table_more_ref, ...), custom_call_target="tpu_custom_call" | custom-call | tf_op jit(solution)/shard_map/attend_far/pallas_call | solution.py:373
  34.7 14.2 %all_to_all.10 = bf16[16,32,512]{2,1,0:T(8,128)(2,1)S(1)} all-to-all(bf16[16,32,512]{2,1,0:T(8,128)(2,1)S(1)} %attend_far.1), channel_id=1, replica_groups=mesh['region'=16,'shard'=16] {'region'}, dimensions={0} | all-to-all | bytes 1048576 | tf_op jit(solution)/shard_map/all_to_all | solution.py:382
  48.8 0.0 copy-done
  48.8 0.0 copy-done.1
  48.8 0.0 copy-done.2
  48.8 0.0 copy-done.5
  48.8 0.0 copy-done.7
  48.9 2.8 %finish.1 = bf16[256,512]{1,0:T(8,128)(2,1)} custom-call(bf16[256,512]{1,0:T(8,128)(2,1)S(1)} %copy-done, bf16[256,512]{1,0:T(8,128)(2,1)S(1)} %pick.1.pick_ref, bf16[512,512]{1,0:T(8,128)(2,1)S(1)} %bitcast.4, bf16[512,512]{1,0:T(8,128)(2,1)S(1)} %copy-done.5, f32[1,512]{1,0:T(1,128)S(1)} %bitcast.8, bf16[512,2048]{1,0:T(8,128)(2,1)S(1)} %copy-done.1, ...), custom_call_target="tpu_custom_call" | custom-call | tf_op jit(solution)/shard_map/finish/pallas_call | solution.py:385
  (3 shorter events, 0.1 us)
Async XLA Ops:
  0.0 14.7 %copy-start.8 = (bf16[64,512]{1,0:T(8,128)(2,1)S(1)}, bf16[64,512]{1,0:T(8,128)(2,1)}, u32[]{:S(2)}) copy-start(bf16[64,512]{1,0:T(8,128)(2,1)} %refs_0_.4) | copy-start | bytes 196612
  2.7 12.1 %collective-permute-start = (bf16[64,512]{1,0:T(8,128)(2,1)}, bf16[64,512]{1,0:T(8,128)(2,1)S(1)}, u32[]{:S(2)}, u32[]{:S(2)}) collective-permute-start(bf16[64,512]{1,0:T(8,128)(2,1)} %refs_0_.4), channel_id=1, source_target_pairs={{8,0},{9,1},{10,2},{11,3},{12,4},{13,5},{14,6},{15,7},{0,8},{1,9},... | collective-permute-start | bytes 196616 | tf_op jit(solution)/shard_map/ppermute | solution.py:284
  7.9 17.8 %all-to-all-start = ((bf16[16,144,128]{2,1,0:T(8,128)(2,1)}), bf16[16,144,128]{2,1,0:T(8,128)(2,1)S(1)}, u32[]{:S(2)}, u32[]{:S(2)}) async-start(bf16[16,144,128]{2,1,0:T(8,128)(2,1)} %pack_late.1), calls=%async_computation | async-start | bytes 1179648 | tf_op jit(solution)/shard_map/all_to_all | solution.py:325
  14.7 5.9 %copy-start.6 = (s32[256,1]{0,1:T(1,128)S(1)}, s32[256,1]{0,1:T(1,128)}, u32[]{:S(2)}) copy-start(s32[256,1]{0,1:T(1,128)} %param.12) | copy-start | bytes 3076
  14.8 17.5 %collective-permute-start.4 = (bf16[128,512]{1,0:T(8,128)(2,1)S(1)}, bf16[128,512]{1,0:T(8,128)(2,1)S(1)}, u32[]{:S(2)}, u32[]{:S(2)}) collective-permute-start(bf16[128,512]{1,0:T(8,128)(2,1)S(1)} %join_near.1.after_ref.table_ref), channel_id=1, source_target_pairs={{0,1},{1,0},{2,3},{3,2},{4,5},{5,4},{6,7},{7,6},{8,9},{9,8},{10,11... | collective-permute-start | bytes 393224 | tf_op jit(solution)/shard_map/ppermute | solution.py:287
  16.1 11.6 %collective-permute-start.3 = (bf16[128,512]{1,0:T(8,128)(2,1)S(1)}, bf16[128,512]{1,0:T(8,128)(2,1)S(1)}, u32[]{:S(2)}, u32[]{:S(2)}) collective-permute-start(bf16[128,512]{1,0:T(8,128)(2,1)S(1)} %join_near.1.after_ref.table_ref), channel_id=1, source_target_pairs={{4,0},{13,1},{6,2},{15,3},{8,4},{1,5},{10,6},{3,7},{12,8},{5,9},{1... | collective-permute-start | bytes 393224 | tf_op jit(solution)/shard_map/ppermute | solution.py:284
  17.3 10.5 %collective-permute-start.2 = (bf16[128,512]{1,0:T(8,128)(2,1)S(1)}, bf16[128,512]{1,0:T(8,128)(2,1)S(1)}, u32[]{:S(2)}, u32[]{:S(2)}) collective-permute-start(bf16[128,512]{1,0:T(8,128)(2,1)S(1)} %join_near.1.after_ref.table_ref), channel_id=1, source_target_pairs={{14,0},{15,1},{0,2},{1,3},{2,4},{3,5},{4,6},{5,7},{6,8},{7,9},{8,1... | collective-permute-start | bytes 393224 | tf_op jit(solution)/shard_map/ppermute | solution.py:284
  20.6 7.2 %collective-permute-start.1 = (bf16[128,512]{1,0:T(8,128)(2,1)S(1)}, bf16[128,512]{1,0:T(8,128)(2,1)S(1)}, u32[]{:S(2)}, u32[]{:S(2)}) collective-permute-start(bf16[128,512]{1,0:T(8,128)(2,1)S(1)} %join_near.1.after_ref.table_ref), channel_id=1, source_target_pairs={{2,0},{3,1},{4,2},{5,3},{6,4},{7,5},{8,6},{9,7},{10,8},{11,9},{12,... | collective-permute-start | bytes 393224 | tf_op jit(solution)/shard_map/ppermute | solution.py:284
  20.9 9.2 %copy-start.3 = (bf16[512,512]{1,0:T(8,128)(2,1)S(1)}, bf16[512,512]{1,0:T(8,128)(2,1)}, u32[]{:S(2)}) copy-start(bf16[512,512]{1,0:T(8,128)(2,1)} %w_key_ref.3) | copy-start | bytes 1572868
  20.9 9.2 %copy-start.4 = (bf16[512,512]{1,0:T(8,128)(2,1)S(1)}, bf16[512,512]{1,0:T(8,128)(2,1)}, u32[]{:S(2)}) copy-start(bf16[512,512]{1,0:T(8,128)(2,1)} %w_value_ref.3) | copy-start | bytes 1572868
  27.8 4.4 %collective-permute-start.5 = (bf16[384,512]{1,0:T(8,128)(2,1)S(1)}, bf16[384,512]{1,0:T(8,128)(2,1)S(1)}, u32[]{:S(2)}, u32[]{:S(2)}) collective-permute-start(bf16[384,512]{1,0:T(8,128)(2,1)S(1)} %join_more.1.table_more_ref), channel_id=1, source_target_pairs={{0,1},{1,0},{2,3},{3,2},{4,5},{5,4},{6,7},{7,6},{8,9},{9,8},{10,11... | collective-permute-start | bytes 1179656 | tf_op jit(solution)/shard_map/ppermute | solution.py:287
  32.2 16.6 %copy-start = (bf16[256,512]{1,0:T(8,128)(2,1)S(1)}, bf16[256,512]{1,0:T(8,128)(2,1)}, u32[]{:S(2)}) copy-start(bf16[256,512]{1,0:T(8,128)(2,1)} %feats_ref.1) | copy-start | bytes 786436
  32.2 16.6 %copy-start.1 = (bf16[512,2048]{1,0:T(8,128)(2,1)S(1)}, bf16[512,2048]{1,0:T(8,128)(2,1)}, u32[]{:S(2)}) copy-start(bf16[512,2048]{1,0:T(8,128)(2,1)} %w_up_ref.1) | copy-start | bytes 6291460
  32.3 16.6 %copy-start.2 = (bf16[2048,512]{1,0:T(8,128)(2,1)S(1)}, bf16[2048,512]{1,0:T(8,128)(2,1)}, u32[]{:S(2)}) copy-start(bf16[2048,512]{1,0:T(8,128)(2,1)} %w_down_ref.1) | copy-start | bytes 6291460
  32.3 16.6 %copy-start.5 = (bf16[512,512]{1,0:T(8,128)(2,1)S(1)}, bf16[512,512]{1,0:T(8,128)(2,1)}, u32[]{:S(2)}) copy-start(bf16[512,512]{1,0:T(8,128)(2,1)} %w_out_ref.1) | copy-start | bytes 1572868
  32.3 16.6 %copy-start.7 = (f32[512]{0:T(512)S(1)}, f32[512]{0:T(512)}, u32[]{:S(2)}) copy-start(f32[512]{0:T(512)} %param.19) | copy-start | bytes 6148

commit v5 on v4

--- a/solution.py
+++ b/solution.py
@@ -134,7 +134,6 @@
     received_ref,
     logcount_ref,
     table_ref,
-    table_more_ref,
     w_key_ref,
     w_value_ref,
     *refs,
@@ -152,12 +151,12 @@
     chip, core = place // 2, place % 2
     if not first_part:
         core = 1 - core
-    skip = 2 + 4 * core
-    for step, offset in enumerate((0, 4, 1, 5, 7, 3, skip, skip + 4)):
-        origin = lax.rem(chip + offset, chips)
+    turn = 1 - 2 * (chip % 2)
+    steps = (0, 3 * turn, 1, 1 - 3 * turn, -1, -1 - 3 * turn, 2 * turn, 5 * turn)
+    for step, offset in enumerate(steps):
+        origin = lax.rem(chip + offset + chips, chips)
         target = pl.ds(pl.multiple_of(origin * rows_held, rows_held), rows_held)
-        ref, row = (table_ref, step) if step < 2 else (table_more_ref, step - 2)
-        token_ref[target, :] = ref[row * rows_held : (row + 1) * rows_held, :]
+        token_ref[target, :] = table_ref[step * rows_held : (step + 1) * rows_held, :]
     tokens = token_ref[...]
     key_ref[...] = jnp.dot(tokens, w_key_ref[...], preferred_element_type=F32).astype(BF16)
     value_ref[...] = lax.dot_general(
@@ -274,10 +273,10 @@
     region_row = query_region.reshape(1, query_count)
     payload = (region_count, width // LANES * capacity + capacity // 2, LANES)
 
-    def fetch(table, chip_offset, other_offset=None):
-        steps = (chip_offset, chip_offset if other_offset is None else other_offset)
+    def fetch(table, even_step, odd_step):
+        steps = (even_step, odd_step)
         pairs = [
-            ((chip + steps[core]) % chips * 2 + core, chip * 2 + core)
+            ((chip + steps[chip % 2]) % chips * 2 + core, chip * 2 + core)
             for chip in range(chips)
             for core in range(2)
         ]
@@ -320,10 +319,10 @@
         )(query_feats, region_row, neighbors.T, w_query, *begun)
 
     begun, latents = lax.optimization_barrier((pack(True), latents))
-    opposite = fetch(latents, 4)
+    opposite = fetch(latents, 3, -3)
     send = pack(False, begun)
     received = lax.all_to_all(send, "region", split_axis=0, concat_axis=0, tiled=True)
-    near = join([latents, opposite], 10**11, "join_near")
+    pair = join([latents, opposite], 10**11, "join_pair")
     pick = pl.pallas_call(
         functools.partial(pick_kernel, region_count, capacity),
         out_shape=jax.ShapeDtypeStruct((query_count, slot_count), BF16),
@@ -332,7 +331,7 @@
         compiler_params=params(4),
         cost_estimate=pl.CostEstimate(flops=10**10, bytes_accessed=0, transcendentals=0),
         name="pick",
-    )(region_row, near)
+    )(region_row, pair)
     received, pick = lax.optimization_barrier((received, pick))
     logcount = pl.pallas_call(
         functools.partial(count_kernel, neighbor_count),
@@ -346,11 +345,10 @@
         compiler_params=params(8),
         name="count",
     )(received)
-    arrivals = [fetch(near, 1), fetch(near, -1), fetch(near, 2, -2)]
+    arrivals = [fetch(pair, 1, 1), fetch(pair, -1, -1), fetch(pair, 2, -2)]
     arrivals, logcount = lax.optimization_barrier((arrivals, logcount))
-    near_more = join(arrivals, 0, "join_more")
+    near = join([pair, *arrivals], 0, "join_near")
     far = swap(near)
-    far_more = swap(near_more)
     scratch = [
         pltpu.VMEM((table_rows, width), BF16),
         pltpu.VMEM((table_rows, width), BF16),
@@ -363,22 +361,22 @@
             jax.ShapeDtypeStruct((groups, width // HEADS, LANES), F32),
             jax.ShapeDtypeStruct((groups, 8, LANES), F32),
         ],
-        in_specs=[VMEM] * 6,
+        in_specs=[VMEM] * 5,
         out_specs=[VMEM] * 2,
         scratch_shapes=scratch,
         compiler_params=params(16),
         cost_estimate=pl.CostEstimate(flops=10**10, bytes_accessed=0, transcendentals=0),
         name="attend_near",
-    )(received, logcount, near, near_more, w_key, w_value)
+    )(received, logcount, near, w_key, w_value)
     mixed = pl.pallas_call(
         functools.partial(attend_kernel, False, latents.shape[0]),
         out_shape=jax.ShapeDtypeStruct((region_count, capacity, width), BF16),
-        in_specs=[VMEM] * 8,
+        in_specs=[VMEM] * 7,
         out_specs=VMEM,
         scratch_shapes=scratch,
         compiler_params=params(16),
         name="attend_far",
-    )(received, logcount, far, far_more, w_key, w_value, *sums)
+    )(received, logcount, far, w_key, w_value, *sums)
     returned = lax.all_to_all(
         mixed, "region", split_axis=0, concat_axis=0, tiled=True
     ).reshape(slot_count, width)

time: 51.8 us -> 50.3 us (0.971)
  waiting for transfers between devices: 4.82 us -> 2.16 us
  blocking collectives: 14.2 us -> 15.2 us
    all_to_all x1, waiting for transfers between devices: 4.81 us -> 2.15 us  [on_device(): lax.all_to_all(send, 'region', split_axis=0, concat_axis=0, tiled=True)]
    ppermute x4, starting transfers between devices: 9.72 us -> 11.1 us  [fetch(): return lax.ppermute(table, 'shard', pairs)]
    ppermute x2 -> x1, starting transfers between devices: 3.57 us -> 2.25 us  [swap(): lax.ppermute(table, 'shard', [(place, place ^ 1) for place in range(shard...]
    all_to_all x1, blocking collectives: 14.2 us -> 15.2 us  [on_device(): lax.all_to_all(mixed, 'region', split_axis=0, concat_axis=0, tiled=True)]
  transfers between devices with their start and end apart: 7 -> 6, of which waited for: 1 -> 1; matrix products, arithmetic and copies ran while one was open for 0% -> 0% of each run, Pallas kernels for 9% -> 9%
where the time goes in v5:
time: 50.3 us; the launch traced here: 50.1 us
  starting transfers between devices  20.2 us (40%)
  blocking collectives  15.2 us (30%)
  Pallas kernels  12.3 us (24%)
  waiting for transfers between devices  2.16 us (4%)
    all_to_all x1, blocking collectives, on_device(): lax.all_to_all(mixed, 'region', split_axis=0, concat_axis=0, tiled=True)  15.2 us
    ppermute x4, starting transfers between devices, fetch(): return lax.ppermute(table, 'shard', pairs)  11.1 us
    all_to_all x1, starting transfers between devices, on_device(): lax.all_to_all(send, 'region', split_axis=0, concat_axis=0, tiled=True)  6.77 us
    pallas_call x1, Pallas kernels, on_device(): pl.pallas_call(finish_kernel, out_shape=jax.ShapeDtypeStruct((query_count...  2.76 us
    pallas_call x2, Pallas kernels, pack(): pl.pallas_call(functools.partial(pack_kernel, region_count, capacity, ear...  2.67 us
    pallas_call x1, Pallas kernels, on_device(): pl.pallas_call(functools.partial(attend_kernel, False, latents.shape[0]),...  2.36 us
    ppermute x1, starting transfers between devices, swap(): lax.ppermute(table, 'shard', [(place, place ^ 1) for place in range(shard...  2.25 us
    pallas_call x1, Pallas kernels, on_device(): pl.pallas_call(functools.partial(attend_kernel, True, latents.shape[0]),...  2.16 us
  transfers between devices with their start and end apart: 6, of which 1 were waited for; matrix products, arithmetic and copies ran while one was open for 0% of the time, Pallas kernels for 9%

profile of v5, /device:TPU:1, one launch (start us, length us, event | category | flops | bytes accessed | tf_op | source)
XLA Modules:
  0.0 50.1 jit_solution(2920673586543768533)
XLA Ops:
  0.0 0.0 copy-start.8
  0.0 2.6 %pack_early.1.refs_4_ = bf16[16,144,128]{2,1,0:T(8,128)(2,1)} custom-call(bf16[256,512]{1,0:T(8,128)(2,1)} %feats_ref.1, s32[1,256]{1,0:T(1,128)} %bitcast.5, s32[64,256]{1,0:T(8,128)} %bitcast.9, bf16[512,512]{1,0:T(8,128)(2,1)} %refs_3_.3), custom_call_target="tpu_custom_call" | custom-call | tf_op jit(solution)/shard_map/pack_early/pallas_call | solution.py:302
  2.6 2.7 %collective-permute-start = (bf16[64,512]{1,0:T(8,128)(2,1)}, bf16[64,512]{1,0:T(8,128)(2,1)S(1)}, u32[]{:S(2)}, u32[]{:S(2)}) collective-permute-start(bf16[64,512]{1,0:T(8,128)(2,1)} %refs_0_.4), channel_id=1, source_target_pairs={{6,0},{7,1},{12,2},{13,3},{10,4},{11,5},{0,6},{1,7},{14,8},{15,9},... | collective-permute-start | bytes 196616 | tf_op jit(solution)/shard_map/ppermute | solution.py:283
  5.4 6.8 %all-to-all-start = ((bf16[16,144,128]{2,1,0:T(8,128)(2,1)}), bf16[16,144,128]{2,1,0:T(8,128)(2,1)S(1)}, u32[]{:S(2)}, u32[]{:S(2)}) async-start(bf16[16,144,128]{2,1,0:T(8,128)(2,1)} %pack_late.1), calls=%async_computation | async-start | bytes 1179648 | tf_op jit(solution)/shard_map/all_to_all | solution.py:324
  12.1 0.0 copy-start.6
  12.2 0.0 collective-permute-done.refs_1_
  12.2 0.0 copy-done.8
  12.2 5.8 %collective-permute-start.3 = (bf16[128,512]{1,0:T(8,128)(2,1)S(1)}, bf16[128,512]{1,0:T(8,128)(2,1)S(1)}, u32[]{:S(2)}, u32[]{:S(2)}) collective-permute-start(bf16[128,512]{1,0:T(8,128)(2,1)S(1)} %join_pair.1.after_ref.refs_0_), channel_id=1, source_target_pairs={{4,0},{5,1},{14,2},{15,3},{8,4},{9,5},{2,6},{3,7},{12,8},{13,9},{6... | collective-permute-start | bytes 393224 | tf_op jit(solution)/shard_map/ppermute | solution.py:283
  18.0 0.0 collective-permute-start.2
  18.0 2.7 %collective-permute-start.1 = (bf16[128,512]{1,0:T(8,128)(2,1)S(1)}, bf16[128,512]{1,0:T(8,128)(2,1)S(1)}, u32[]{:S(2)}, u32[]{:S(2)}) collective-permute-start(bf16[128,512]{1,0:T(8,128)(2,1)S(1)} %join_pair.1.after_ref.refs_0_), channel_id=1, source_target_pairs={{2,0},{3,1},{4,2},{5,3},{6,4},{7,5},{8,6},{9,7},{10,8},{11,9},{12,... | collective-permute-start | bytes 393224 | tf_op jit(solution)/shard_map/ppermute | solution.py:283
  20.7 0.0 copy-done.6
  20.7 0.3 pick.1.pick_ref
  21.0 0.0 copy-start.3
  21.0 0.0 copy-start.4
  21.0 2.1 %all-to-all-done.received_ref = bf16[16,144,128]{2,1,0:T(8,128)(2,1)S(1)} async-done(((bf16[16,144,128]{2,1,0:T(8,128)(2,1)}), bf16[16,144,128]{2,1,0:T(8,128)(2,1)S(1)}, u32[]{:S(2)}, u32[]{:S(2)}) %all-to-all-start) | async-done | bytes 589856 | tf_op jit(solution)/shard_map/all_to_all | solution.py:324
  23.1 2.0 %count.1.logcount_ref = f32[8,2,64,512]{3,2,1,0:T(8,128)S(1)} custom-call(bf16[16,144,128]{2,1,0:T(8,128)(2,1)S(1)} %all-to-all-done.received_ref), custom_call_target="tpu_custom_call" | custom-call | tf_op jit(solution)/shard_map/count/pallas_call | solution.py:336
  25.2 0.0 collective-permute-done.3.refs_3_
  25.2 0.0 collective-permute-done.2.refs_2_
  25.2 0.0 collective-permute-done.1.refs_1_
  25.2 2.3 %collective-permute-start.4 = (bf16[512,512]{1,0:T(8,128)(2,1)S(1)}, bf16[512,512]{1,0:T(8,128)(2,1)S(1)}, u32[]{:S(2)}, u32[]{:S(2)}) collective-permute-start(bf16[512,512]{1,0:T(8,128)(2,1)S(1)} %join_near.1.table_ref), channel_id=1, source_target_pairs={{0,1},{1,0},{2,3},{3,2},{4,5},{5,4},{6,7},{7,6},{8,9},{9,8},{10,11... | collective-permute-start | bytes 1572872 | tf_op jit(solution)/shard_map/ppermute | solution.py:286
  27.5 0.0 copy-done.3
  27.5 0.0 copy-done.4
  27.5 2.2 %attend_near.1 = (f32[16,128,128]{2,1,0:T(8,128)S(1)}, f32[16,8,128]{2,1,0:T(8,128)S(1)}) custom-call(bf16[16,144,128]{2,1,0:T(8,128)(2,1)S(1)} %all-to-all-done.received_ref, f32[8,2,64,512]{3,2,1,0:T(8,128)S(1)} %count.1.logcount_ref, bf16[512,512]{1,0:T(8,128)(2,1)S(1)} %join_near.1.table_ref, bf16[512,512]{1,0:T(8,128)(2,1)S(1)} %copy-done.3, ...), custom_call_target="tpu_custom_call" | custom-call | flops 10000000000 | tf_op jit(solution)/shard_map/attend_near/pallas_call | solution.py:358
  29.7 0.0 collective-permute-done.4.table_ref
  29.7 0.0 copy-start
  29.7 0.0 copy-start.1
  29.7 0.0 copy-start.2
  29.7 0.0 copy-start.5
  29.7 0.0 copy-start.7
  29.7 2.4 %attend_far.1 = bf16[16,32,512]{2,1,0:T(8,128)(2,1)S(1)} custom-call(bf16[16,144,128]{2,1,0:T(8,128)(2,1)S(1)} %all-to-all-done.received_ref, f32[8,2,64,512]{3,2,1,0:T(8,128)S(1)} %count.1.logcount_ref, bf16[512,512]{1,0:T(8,128)(2,1)S(1)} %collective-permute-done.4.table_ref, bf16[512,512]{1,0:T(8,128)(2,1)S(1)} %copy-done.3, ...), custom_call_target="tpu_custom_call" | custom-call | tf_op jit(solution)/shard_map/attend_far/pallas_call | solution.py:371
  32.1 15.2 %all_to_all.10 = bf16[16,32,512]{2,1,0:T(8,128)(2,1)S(1)} all-to-all(bf16[16,32,512]{2,1,0:T(8,128)(2,1)S(1)} %attend_far.1), channel_id=1, replica_groups=mesh['region'=16,'shard'=16] {'region'}, dimensions={0} | all-to-all | bytes 1048576 | tf_op jit(solution)/shard_map/all_to_all | solution.py:380
  47.3 0.0 copy-done
  47.3 0.0 copy-done.1
  47.3 0.0 copy-done.2
  47.3 0.0 copy-done.5
  47.3 0.0 copy-done.7
  47.3 2.8 %finish.1 = bf16[256,512]{1,0:T(8,128)(2,1)} custom-call(bf16[256,512]{1,0:T(8,128)(2,1)S(1)} %copy-done, bf16[256,512]{1,0:T(8,128)(2,1)S(1)} %pick.1.pick_ref, bf16[512,512]{1,0:T(8,128)(2,1)S(1)} %bitcast.4, bf16[512,512]{1,0:T(8,128)(2,1)S(1)} %copy-done.5, f32[1,512]{1,0:T(1,128)S(1)} %bitcast.8, bf16[512,2048]{1,0:T(8,128)(2,1)S(1)} %copy-done.1, ...), custom_call_target="tpu_custom_call" | custom-call | tf_op jit(solution)/shard_map/finish/pallas_call | solution.py:383
  (3 shorter events, 0.1 us)
Async XLA Ops:
  0.0 12.2 %copy-start.8 = (bf16[64,512]{1,0:T(8,128)(2,1)S(1)}, bf16[64,512]{1,0:T(8,128)(2,1)}, u32[]{:S(2)}) copy-start(bf16[64,512]{1,0:T(8,128)(2,1)} %refs_0_.4) | copy-start | bytes 196612
  2.6 9.5 %collective-permute-start = (bf16[64,512]{1,0:T(8,128)(2,1)}, bf16[64,512]{1,0:T(8,128)(2,1)S(1)}, u32[]{:S(2)}, u32[]{:S(2)}) collective-permute-start(bf16[64,512]{1,0:T(8,128)(2,1)} %refs_0_.4), channel_id=1, source_target_pairs={{6,0},{7,1},{12,2},{13,3},{10,4},{11,5},{0,6},{1,7},{14,8},{15,9},... | collective-permute-start | bytes 196616 | tf_op jit(solution)/shard_map/ppermute | solution.py:283
  5.4 17.8 %all-to-all-start = ((bf16[16,144,128]{2,1,0:T(8,128)(2,1)}), bf16[16,144,128]{2,1,0:T(8,128)(2,1)S(1)}, u32[]{:S(2)}, u32[]{:S(2)}) async-start(bf16[16,144,128]{2,1,0:T(8,128)(2,1)} %pack_late.1), calls=%async_computation | async-start | bytes 1179648 | tf_op jit(solution)/shard_map/all_to_all | solution.py:324
  12.1 8.5 %copy-start.6 = (s32[256,1]{0,1:T(1,128)S(1)}, s32[256,1]{0,1:T(1,128)}, u32[]{:S(2)}) copy-start(s32[256,1]{0,1:T(1,128)} %param.12) | copy-start | bytes 3076
  12.2 13.0 %collective-permute-start.3 = (bf16[128,512]{1,0:T(8,128)(2,1)S(1)}, bf16[128,512]{1,0:T(8,128)(2,1)S(1)}, u32[]{:S(2)}, u32[]{:S(2)}) collective-permute-start(bf16[128,512]{1,0:T(8,128)(2,1)S(1)} %join_pair.1.after_ref.refs_0_), channel_id=1, source_target_pairs={{4,0},{5,1},{14,2},{15,3},{8,4},{9,5},{2,6},{3,7},{12,8},{13,9},{6... | collective-permute-start | bytes 393224 | tf_op jit(solution)/shard_map/ppermute | solution.py:283
  18.0 7.2 %collective-permute-start.2 = (bf16[128,512]{1,0:T(8,128)(2,1)S(1)}, bf16[128,512]{1,0:T(8,128)(2,1)S(1)}, u32[]{:S(2)}, u32[]{:S(2)}) collective-permute-start(bf16[128,512]{1,0:T(8,128)(2,1)S(1)} %join_pair.1.after_ref.refs_0_), channel_id=1, source_target_pairs={{14,0},{15,1},{0,2},{1,3},{2,4},{3,5},{4,6},{5,7},{6,8},{7,9},{8,1... | collective-permute-start | bytes 393224 | tf_op jit(solution)/shard_map/ppermute | solution.py:283
  18.0 7.2 %collective-permute-start.1 = (bf16[128,512]{1,0:T(8,128)(2,1)S(1)}, bf16[128,512]{1,0:T(8,128)(2,1)S(1)}, u32[]{:S(2)}, u32[]{:S(2)}) collective-permute-start(bf16[128,512]{1,0:T(8,128)(2,1)S(1)} %join_pair.1.after_ref.refs_0_), channel_id=1, source_target_pairs={{2,0},{3,1},{4,2},{5,3},{6,4},{7,5},{8,6},{9,7},{10,8},{11,9},{12,... | collective-permute-start | bytes 393224 | tf_op jit(solution)/shard_map/ppermute | solution.py:283
  21.0 6.5 %copy-start.3 = (bf16[512,512]{1,0:T(8,128)(2,1)S(1)}, bf16[512,512]{1,0:T(8,128)(2,1)}, u32[]{:S(2)}) copy-start(bf16[512,512]{1,0:T(8,128)(2,1)} %w_key_ref.3) | copy-start | bytes 1572868
  21.0 6.5 %copy-start.4 = (bf16[512,512]{1,0:T(8,128)(2,1)S(1)}, bf16[512,512]{1,0:T(8,128)(2,1)}, u32[]{:S(2)}) copy-start(bf16[512,512]{1,0:T(8,128)(2,1)} %w_value_ref.3) | copy-start | bytes 1572868
  25.2 4.4 %collective-permute-start.4 = (bf16[512,512]{1,0:T(8,128)(2,1)S(1)}, bf16[512,512]{1,0:T(8,128)(2,1)S(1)}, u32[]{:S(2)}, u32[]{:S(2)}) collective-permute-start(bf16[512,512]{1,0:T(8,128)(2,1)S(1)} %join_near.1.table_ref), channel_id=1, source_target_pairs={{0,1},{1,0},{2,3},{3,2},{4,5},{5,4},{6,7},{7,6},{8,9},{9,8},{10,11... | collective-permute-start | bytes 1572872 | tf_op jit(solution)/shard_map/ppermute | solution.py:286
  29.7 17.6 %copy-start = (bf16[256,512]{1,0:T(8,128)(2,1)S(1)}, bf16[256,512]{1,0:T(8,128)(2,1)}, u32[]{:S(2)}) copy-start(bf16[256,512]{1,0:T(8,128)(2,1)} %feats_ref.1) | copy-start | bytes 786436
  29.7 17.6 %copy-start.1 = (bf16[512,2048]{1,0:T(8,128)(2,1)S(1)}, bf16[512,2048]{1,0:T(8,128)(2,1)}, u32[]{:S(2)}) copy-start(bf16[512,2048]{1,0:T(8,128)(2,1)} %w_up_ref.1) | copy-start | bytes 6291460
  29.7 17.6 %copy-start.2 = (bf16[2048,512]{1,0:T(8,128)(2,1)S(1)}, bf16[2048,512]{1,0:T(8,128)(2,1)}, u32[]{:S(2)}) copy-start(bf16[2048,512]{1,0:T(8,128)(2,1)} %w_down_ref.1) | copy-start | bytes 6291460
  29.7 17.6 %copy-start.5 = (bf16[512,512]{1,0:T(8,128)(2,1)S(1)}, bf16[512,512]{1,0:T(8,128)(2,1)}, u32[]{:S(2)}) copy-start(bf16[512,512]{1,0:T(8,128)(2,1)} %w_out_ref.1) | copy-start | bytes 1572868
  29.7 17.6 %copy-start.7 = (f32[512]{0:T(512)S(1)}, f32[512]{0:T(512)}, u32[]{:S(2)}) copy-start(f32[512]{0:T(512)} %param.19) | copy-start | bytes 6148

commit v6 on v5

--- a/solution.py
+++ b/solution.py
@@ -152,7 +152,7 @@
     if not first_part:
         core = 1 - core
     turn = 1 - 2 * (chip % 2)
-    steps = (0, 3 * turn, 1, 1 - 3 * turn, -1, -1 - 3 * turn, 2 * turn, 5 * turn)
+    steps = (0, 3 * turn, -1, -1 - 3 * turn, 1, 1 - 3 * turn, 2 * turn, 5 * turn)
     for step, offset in enumerate(steps):
         origin = lax.rem(chip + offset + chips, chips)
         target = pl.ds(pl.multiple_of(origin * rows_held, rows_held), rows_held)
@@ -345,7 +345,7 @@
         compiler_params=params(8),
         name="count",
     )(received)
-    arrivals = [fetch(pair, 1, 1), fetch(pair, -1, -1), fetch(pair, 2, -2)]
+    arrivals = [fetch(pair, -1, -1), fetch(pair, 1, 1), fetch(pair, 2, -2)]
     arrivals, logcount = lax.optimization_barrier((arrivals, logcount))
     near = join([pair, *arrivals], 0, "join_near")
     far = swap(near)

time: 50.3 us -> 50.3 us (level)
  waiting for transfers between devices: 2.16 us -> 3.37 us
  starting transfers between devices: 20.2 us -> 19 us
    ppermute x4, starting transfers between devices: 11.1 us -> 9.94 us  [fetch(): return lax.ppermute(table, 'shard', pairs)]
    all_to_all x1, waiting for transfers between devices: 2.15 us -> 3.36 us  [on_device(): lax.all_to_all(send, 'region', split_axis=0, concat_axis=0, tiled=True)]
where the time goes in v6:
time: 50.3 us; the launch traced here: 50.1 us
  starting transfers between devices  19 us (38%)
  blocking collectives  15.2 us (30%)
  Pallas kernels  12.3 us (24%)
  waiting for transfers between devices  3.37 us (7%)
    all_to_all x1, blocking collectives, on_device(): lax.all_to_all(mixed, 'region', split_axis=0, concat_axis=0, tiled=True)  15.2 us
    ppermute x4, starting transfers between devices, fetch(): return lax.ppermute(table, 'shard', pairs)  9.94 us
    all_to_all x1, starting transfers between devices, on_device(): lax.all_to_all(send, 'region', split_axis=0, concat_axis=0, tiled=True)  6.77 us
    all_to_all x1, waiting for transfers between devices, on_device(): lax.all_to_all(send, 'region', split_axis=0, concat_axis=0, tiled=True)  3.36 us
    pallas_call x1, Pallas kernels, on_device(): pl.pallas_call(finish_kernel, out_shape=jax.ShapeDtypeStruct((query_count...  2.76 us
    pallas_call x2, Pallas kernels, pack(): pl.pallas_call(functools.partial(pack_kernel, region_count, capacity, ear...  2.67 us
    pallas_call x1, Pallas kernels, on_device(): pl.pallas_call(functools.partial(attend_kernel, False, latents.shape[0]),...  2.36 us
    ppermute x1, starting transfers between devices, swap(): lax.ppermute(table, 'shard', [(place, place ^ 1) for place in range(shard...  2.25 us
  transfers between devices with their start and end apart: 6, of which 1 were waited for; matrix products, arithmetic and copies ran while one was open for 0% of the time, Pallas kernels for 9%

profile of v6, /device:TPU:1, one launch (start us, length us, event | category | flops | bytes accessed | tf_op | source)
XLA Modules:
  0.0 50.1 jit_solution(6476329294785958171)
XLA Ops:
  0.0 0.0 copy-start.8
  0.0 2.6 %pack_early.1.refs_4_ = bf16[16,144,128]{2,1,0:T(8,128)(2,1)} custom-call(bf16[256,512]{1,0:T(8,128)(2,1)} %feats_ref.1, s32[1,256]{1,0:T(1,128)} %bitcast.5, s32[64,256]{1,0:T(8,128)} %bitcast.9, bf16[512,512]{1,0:T(8,128)(2,1)} %refs_3_.3), custom_call_target="tpu_custom_call" | custom-call | tf_op jit(solution)/shard_map/pack_early/pallas_call | solution.py:302
  2.6 2.7 %collective-permute-start = (bf16[64,512]{1,0:T(8,128)(2,1)}, bf16[64,512]{1,0:T(8,128)(2,1)S(1)}, u32[]{:S(2)}, u32[]{:S(2)}) collective-permute-start(bf16[64,512]{1,0:T(8,128)(2,1)} %refs_0_.4), channel_id=1, source_target_pairs={{6,0},{7,1},{12,2},{13,3},{10,4},{11,5},{0,6},{1,7},{14,8},{15,9},... | collective-permute-start | bytes 196616 | tf_op jit(solution)/shard_map/ppermute | solution.py:283
  5.4 6.8 %all-to-all-start = ((bf16[16,144,128]{2,1,0:T(8,128)(2,1)}), bf16[16,144,128]{2,1,0:T(8,128)(2,1)S(1)}, u32[]{:S(2)}, u32[]{:S(2)}) async-start(bf16[16,144,128]{2,1,0:T(8,128)(2,1)} %pack_late.1), calls=%async_computation | async-start | bytes 1179648 | tf_op jit(solution)/shard_map/all_to_all | solution.py:324
  12.1 0.0 copy-start.6
  12.2 0.0 collective-permute-done.refs_1_
  12.2 0.0 copy-done.8
  12.2 5.8 %collective-permute-start.3 = (bf16[128,512]{1,0:T(8,128)(2,1)S(1)}, bf16[128,512]{1,0:T(8,128)(2,1)S(1)}, u32[]{:S(2)}, u32[]{:S(2)}) collective-permute-start(bf16[128,512]{1,0:T(8,128)(2,1)S(1)} %join_pair.1.after_ref.refs_0_), channel_id=1, source_target_pairs={{4,0},{5,1},{14,2},{15,3},{8,4},{9,5},{2,6},{3,7},{12,8},{13,9},{6... | collective-permute-start | bytes 393224 | tf_op jit(solution)/shard_map/ppermute | solution.py:283
  18.0 0.0 collective-permute-start.2
  18.0 1.5 %collective-permute-start.1 = (bf16[128,512]{1,0:T(8,128)(2,1)S(1)}, bf16[128,512]{1,0:T(8,128)(2,1)S(1)}, u32[]{:S(2)}, u32[]{:S(2)}) collective-permute-start(bf16[128,512]{1,0:T(8,128)(2,1)S(1)} %join_pair.1.after_ref.refs_0_), channel_id=1, source_target_pairs={{14,0},{15,1},{0,2},{1,3},{2,4},{3,5},{4,6},{5,7},{6,8},{7,9},{8,1... | collective-permute-start | bytes 393224 | tf_op jit(solution)/shard_map/ppermute | solution.py:283
  19.5 0.0 copy-done.6
  19.5 0.3 pick.1.pick_ref
  19.7 0.0 copy-start.3
  19.8 0.0 copy-start.4
  19.8 3.4 %all-to-all-done.received_ref = bf16[16,144,128]{2,1,0:T(8,128)(2,1)S(1)} async-done(((bf16[16,144,128]{2,1,0:T(8,128)(2,1)}), bf16[16,144,128]{2,1,0:T(8,128)(2,1)S(1)}, u32[]{:S(2)}, u32[]{:S(2)}) %all-to-all-start) | async-done | bytes 589856 | tf_op jit(solution)/shard_map/all_to_all | solution.py:324
  23.1 2.0 %count.1.logcount_ref = f32[8,2,64,512]{3,2,1,0:T(8,128)S(1)} custom-call(bf16[16,144,128]{2,1,0:T(8,128)(2,1)S(1)} %all-to-all-done.received_ref), custom_call_target="tpu_custom_call" | custom-call | tf_op jit(solution)/shard_map/count/pallas_call | solution.py:336
  25.2 0.0 collective-permute-done.3.refs_3_
  25.2 0.0 collective-permute-done.2.refs_2_
  25.2 0.0 collective-permute-done.1.refs_1_
  25.2 2.3 %collective-permute-start.4 = (bf16[512,512]{1,0:T(8,128)(2,1)S(1)}, bf16[512,512]{1,0:T(8,128)(2,1)S(1)}, u32[]{:S(2)}, u32[]{:S(2)}) collective-permute-start(bf16[512,512]{1,0:T(8,128)(2,1)S(1)} %join_near.1.table_ref), channel_id=1, source_target_pairs={{0,1},{1,0},{2,3},{3,2},{4,5},{5,4},{6,7},{7,6},{8,9},{9,8},{10,11... | collective-permute-start | bytes 1572872 | tf_op jit(solution)/shard_map/ppermute | solution.py:286
  27.5 0.0 copy-done.3
  27.5 0.0 copy-done.4
  27.5 2.2 %attend_near.1 = (f32[16,128,128]{2,1,0:T(8,128)S(1)}, f32[16,8,128]{2,1,0:T(8,128)S(1)}) custom-call(bf16[16,144,128]{2,1,0:T(8,128)(2,1)S(1)} %all-to-all-done.received_ref, f32[8,2,64,512]{3,2,1,0:T(8,128)S(1)} %count.1.logcount_ref, bf16[512,512]{1,0:T(8,128)(2,1)S(1)} %join_near.1.table_ref, bf16[512,512]{1,0:T(8,128)(2,1)S(1)} %copy-done.3, ...), custom_call_target="tpu_custom_call" | custom-call | flops 10000000000 | tf_op jit(solution)/shard_map/attend_near/pallas_call | solution.py:358
  29.7 0.0 collective-permute-done.4.table_ref
  29.7 0.0 copy-start
  29.7 0.0 copy-start.1
  29.7 0.0 copy-start.2
  29.7 0.0 copy-start.5
  29.7 0.0 copy-start.7
  29.7 2.4 %attend_far.1 = bf16[16,32,512]{2,1,0:T(8,128)(2,1)S(1)} custom-call(bf16[16,144,128]{2,1,0:T(8,128)(2,1)S(1)} %all-to-all-done.received_ref, f32[8,2,64,512]{3,2,1,0:T(8,128)S(1)} %count.1.logcount_ref, bf16[512,512]{1,0:T(8,128)(2,1)S(1)} %collective-permute-done.4.table_ref, bf16[512,512]{1,0:T(8,128)(2,1)S(1)} %copy-done.3, ...), custom_call_target="tpu_custom_call" | custom-call | tf_op jit(solution)/shard_map/attend_far/pallas_call | solution.py:371
  32.1 15.2 %all_to_all.10 = bf16[16,32,512]{2,1,0:T(8,128)(2,1)S(1)} all-to-all(bf16[16,32,512]{2,1,0:T(8,128)(2,1)S(1)} %attend_far.1), channel_id=1, replica_groups=mesh['region'=16,'shard'=16] {'region'}, dimensions={0} | all-to-all | bytes 1048576 | tf_op jit(solution)/shard_map/all_to_all | solution.py:380
  47.3 0.0 copy-done
  47.3 0.0 copy-done.1
  47.3 0.0 copy-done.2
  47.3 0.0 copy-done.5
  47.3 0.0 copy-done.7
  47.3 2.8 %finish.1 = bf16[256,512]{1,0:T(8,128)(2,1)} custom-call(bf16[256,512]{1,0:T(8,128)(2,1)S(1)} %copy-done, bf16[256,512]{1,0:T(8,128)(2,1)S(1)} %pick.1.pick_ref, bf16[512,512]{1,0:T(8,128)(2,1)S(1)} %bitcast.4, bf16[512,512]{1,0:T(8,128)(2,1)S(1)} %copy-done.5, f32[1,512]{1,0:T(1,128)S(1)} %bitcast.8, bf16[512,2048]{1,0:T(8,128)(2,1)S(1)} %copy-done.1, ...), custom_call_target="tpu_custom_call" | custom-call | tf_op jit(solution)/shard_map/finish/pallas_call | solution.py:383
  (3 shorter events, 0.1 us)
Async XLA Ops:
  0.0 12.2 %copy-start.8 = (bf16[64,512]{1,0:T(8,128)(2,1)S(1)}, bf16[64,512]{1,0:T(8,128)(2,1)}, u32[]{:S(2)}) copy-start(bf16[64,512]{1,0:T(8,128)(2,1)} %refs_0_.4) | copy-start | bytes 196612
  2.6 9.5 %collective-permute-start = (bf16[64,512]{1,0:T(8,128)(2,1)}, bf16[64,512]{1,0:T(8,128)(2,1)S(1)}, u32[]{:S(2)}, u32[]{:S(2)}) collective-permute-start(bf16[64,512]{1,0:T(8,128)(2,1)} %refs_0_.4), channel_id=1, source_target_pairs={{6,0},{7,1},{12,2},{13,3},{10,4},{11,5},{0,6},{1,7},{14,8},{15,9},... | collective-permute-start | bytes 196616 | tf_op jit(solution)/shard_map/ppermute | solution.py:283
  5.4 17.8 %all-to-all-start = ((bf16[16,144,128]{2,1,0:T(8,128)(2,1)}), bf16[16,144,128]{2,1,0:T(8,128)(2,1)S(1)}, u32[]{:S(2)}, u32[]{:S(2)}) async-start(bf16[16,144,128]{2,1,0:T(8,128)(2,1)} %pack_late.1), calls=%async_computation | async-start | bytes 1179648 | tf_op jit(solution)/shard_map/all_to_all | solution.py:324
  12.1 7.3 %copy-start.6 = (s32[256,1]{0,1:T(1,128)S(1)}, s32[256,1]{0,1:T(1,128)}, u32[]{:S(2)}) copy-start(s32[256,1]{0,1:T(1,128)} %param.12) | copy-start | bytes 3076
  12.2 13.0 %collective-permute-start.3 = (bf16[128,512]{1,0:T(8,128)(2,1)S(1)}, bf16[128,512]{1,0:T(8,128)(2,1)S(1)}, u32[]{:S(2)}, u32[]{:S(2)}) collective-permute-start(bf16[128,512]{1,0:T(8,128)(2,1)S(1)} %join_pair.1.after_ref.refs_0_), channel_id=1, source_target_pairs={{4,0},{5,1},{14,2},{15,3},{8,4},{9,5},{2,6},{3,7},{12,8},{13,9},{6... | collective-permute-start | bytes 393224 | tf_op jit(solution)/shard_map/ppermute | solution.py:283
  18.0 7.2 %collective-permute-start.2 = (bf16[128,512]{1,0:T(8,128)(2,1)S(1)}, bf16[128,512]{1,0:T(8,128)(2,1)S(1)}, u32[]{:S(2)}, u32[]{:S(2)}) collective-permute-start(bf16[128,512]{1,0:T(8,128)(2,1)S(1)} %join_pair.1.after_ref.refs_0_), channel_id=1, source_target_pairs={{2,0},{3,1},{4,2},{5,3},{6,4},{7,5},{8,6},{9,7},{10,8},{11,9},{12,... | collective-permute-start | bytes 393224 | tf_op jit(solution)/shard_map/ppermute | solution.py:283
  18.0 7.2 %collective-permute-start.1 = (bf16[128,512]{1,0:T(8,128)(2,1)S(1)}, bf16[128,512]{1,0:T(8,128)(2,1)S(1)}, u32[]{:S(2)}, u32[]{:S(2)}) collective-permute-start(bf16[128,512]{1,0:T(8,128)(2,1)S(1)} %join_pair.1.after_ref.refs_0_), channel_id=1, source_target_pairs={{14,0},{15,1},{0,2},{1,3},{2,4},{3,5},{4,6},{5,7},{6,8},{7,9},{8,1... | collective-permute-start | bytes 393224 | tf_op jit(solution)/shard_map/ppermute | solution.py:283
  19.7 7.7 %copy-start.3 = (bf16[512,512]{1,0:T(8,128)(2,1)S(1)}, bf16[512,512]{1,0:T(8,128)(2,1)}, u32[]{:S(2)}) copy-start(bf16[512,512]{1,0:T(8,128)(2,1)} %w_key_ref.3) | copy-start | bytes 1572868
  19.8 7.7 %copy-start.4 = (bf16[512,512]{1,0:T(8,128)(2,1)S(1)}, bf16[512,512]{1,0:T(8,128)(2,1)}, u32[]{:S(2)}) copy-start(bf16[512,512]{1,0:T(8,128)(2,1)} %w_value_ref.3) | copy-start | bytes 1572868
  25.2 4.4 %collective-permute-start.4 = (bf16[512,512]{1,0:T(8,128)(2,1)S(1)}, bf16[512,512]{1,0:T(8,128)(2,1)S(1)}, u32[]{:S(2)}, u32[]{:S(2)}) collective-permute-start(bf16[512,512]{1,0:T(8,128)(2,1)S(1)} %join_near.1.table_ref), channel_id=1, source_target_pairs={{0,1},{1,0},{2,3},{3,2},{4,5},{5,4},{6,7},{7,6},{8,9},{9,8},{10,11... | collective-permute-start | bytes 1572872 | tf_op jit(solution)/shard_map/ppermute | solution.py:286
  29.7 17.6 %copy-start = (bf16[256,512]{1,0:T(8,128)(2,1)S(1)}, bf16[256,512]{1,0:T(8,128)(2,1)}, u32[]{:S(2)}) copy-start(bf16[256,512]{1,0:T(8,128)(2,1)} %feats_ref.1) | copy-start | bytes 786436
  29.7 17.6 %copy-start.1 = (bf16[512,2048]{1,0:T(8,128)(2,1)S(1)}, bf16[512,2048]{1,0:T(8,128)(2,1)}, u32[]{:S(2)}) copy-start(bf16[512,2048]{1,0:T(8,128)(2,1)} %w_up_ref.1) | copy-start | bytes 6291460
  29.7 17.6 %copy-start.2 = (bf16[2048,512]{1,0:T(8,128)(2,1)S(1)}, bf16[2048,512]{1,0:T(8,128)(2,1)}, u32[]{:S(2)}) copy-start(bf16[2048,512]{1,0:T(8,128)(2,1)} %w_down_ref.1) | copy-start | bytes 6291460
  29.7 17.6 %copy-start.5 = (bf16[512,512]{1,0:T(8,128)(2,1)S(1)}, bf16[512,512]{1,0:T(8,128)(2,1)}, u32[]{:S(2)}) copy-start(bf16[512,512]{1,0:T(8,128)(2,1)} %w_out_ref.1) | copy-start | bytes 1572868
  29.7 17.6 %copy-start.7 = (f32[512]{0:T(512)S(1)}, f32[512]{0:T(512)}, u32[]{:S(2)}) copy-start(f32[512]{0:T(512)} %param.19) | copy-start | bytes 6148

commit v7 on v5

--- a/solution.py
+++ b/solution.py
@@ -41,7 +41,7 @@
             pltpu.make_async_copy(source, target, arrived.at[number])
             for number, (source, target) in enumerate(zip(sources, targets))
         ]
-        for copy in copies:
+        for copy in reversed(copies):
             copy.start()
         slot_count = region_count * capacity
         rows, width = feats_ref.shape

time: 50.3 us -> 50.8 us (level)
    all_to_all x1, blocking collectives: 15.2 us -> 15.7 us  [on_device(): lax.all_to_all(mixed, 'region', split_axis=0, concat_axis=0, tiled=True)]
where the time goes in v7:
time: 50.8 us; the launch traced here: 50.6 us
  starting transfers between devices  20.4 us (40%)
  blocking collectives  15.7 us (31%)
  Pallas kernels  12.5 us (25%)
  waiting for transfers between devices  1.66 us (3%)
    all_to_all x1, blocking collectives, on_device(): lax.all_to_all(mixed, 'region', split_axis=0, concat_axis=0, tiled=True)  15.7 us
    ppermute x4, starting transfers between devices, fetch(): return lax.ppermute(table, 'shard', pairs)  11.4 us
    all_to_all x1, starting transfers between devices, on_device(): lax.all_to_all(send, 'region', split_axis=0, concat_axis=0, tiled=True)  6.77 us
    pallas_call x2, Pallas kernels, pack(): pl.pallas_call(functools.partial(pack_kernel, region_count, capacity, ear...  2.91 us
    pallas_call x1, Pallas kernels, on_device(): pl.pallas_call(finish_kernel, out_shape=jax.ShapeDtypeStruct((query_count...  2.75 us
    pallas_call x1, Pallas kernels, on_device(): pl.pallas_call(functools.partial(attend_kernel, False, latents.shape[0]),...  2.36 us
    ppermute x1, starting transfers between devices, swap(): lax.ppermute(table, 'shard', [(place, place ^ 1) for place in range(shard...  2.25 us
    pallas_call x1, Pallas kernels, on_device(): pl.pallas_call(functools.partial(attend_kernel, True, latents.shape[0]),...  2.16 us
  transfers between devices with their start and end apart: 6, of which 1 were waited for; matrix products, arithmetic and copies ran while one was open for 0% of the time, Pallas kernels for 9%

profile of v7, /device:TPU:1, one launch (start us, length us, event | category | flops | bytes accessed | tf_op | source)
XLA Modules:
  0.0 50.6 jit_solution(15541059761844237448)
XLA Ops:
  0.0 0.0 copy-start.8
  0.0 2.9 %pack_early.1.refs_4_ = bf16[16,144,128]{2,1,0:T(8,128)(2,1)} custom-call(bf16[256,512]{1,0:T(8,128)(2,1)} %feats_ref.1, s32[1,256]{1,0:T(1,128)} %bitcast.5, s32[64,256]{1,0:T(8,128)} %bitcast.9, bf16[512,512]{1,0:T(8,128)(2,1)} %refs_3_.3), custom_call_target="tpu_custom_call" | custom-call | tf_op jit(solution)/shard_map/pack_early/pallas_call | solution.py:302
  2.9 2.4 %collective-permute-start = (bf16[64,512]{1,0:T(8,128)(2,1)}, bf16[64,512]{1,0:T(8,128)(2,1)S(1)}, u32[]{:S(2)}, u32[]{:S(2)}) collective-permute-start(bf16[64,512]{1,0:T(8,128)(2,1)} %refs_0_.4), channel_id=1, source_target_pairs={{6,0},{7,1},{12,2},{13,3},{10,4},{11,5},{0,6},{1,7},{14,8},{15,9},... | collective-permute-start | bytes 196616 | tf_op jit(solution)/shard_map/ppermute | solution.py:283
  5.4 6.8 %all-to-all-start = ((bf16[16,144,128]{2,1,0:T(8,128)(2,1)}), bf16[16,144,128]{2,1,0:T(8,128)(2,1)S(1)}, u32[]{:S(2)}, u32[]{:S(2)}) async-start(bf16[16,144,128]{2,1,0:T(8,128)(2,1)} %pack_late.1), calls=%async_computation | async-start | bytes 1179648 | tf_op jit(solution)/shard_map/all_to_all | solution.py:324
  12.1 0.0 copy-start.6
  12.2 0.0 collective-permute-done.refs_1_
  12.2 0.0 copy-done.8
  12.2 6.3 %collective-permute-start.3 = (bf16[128,512]{1,0:T(8,128)(2,1)S(1)}, bf16[128,512]{1,0:T(8,128)(2,1)S(1)}, u32[]{:S(2)}, u32[]{:S(2)}) collective-permute-start(bf16[128,512]{1,0:T(8,128)(2,1)S(1)} %join_pair.1.after_ref.refs_0_), channel_id=1, source_target_pairs={{4,0},{5,1},{14,2},{15,3},{8,4},{9,5},{2,6},{3,7},{12,8},{13,9},{6... | collective-permute-start | bytes 393224 | tf_op jit(solution)/shard_map/ppermute | solution.py:283
  18.5 0.0 collective-permute-start.2
  18.5 2.7 %collective-permute-start.1 = (bf16[128,512]{1,0:T(8,128)(2,1)S(1)}, bf16[128,512]{1,0:T(8,128)(2,1)S(1)}, u32[]{:S(2)}, u32[]{:S(2)}) collective-permute-start(bf16[128,512]{1,0:T(8,128)(2,1)S(1)} %join_pair.1.after_ref.refs_0_), channel_id=1, source_target_pairs={{2,0},{3,1},{4,2},{5,3},{6,4},{7,5},{8,6},{9,7},{10,8},{11,9},{12,... | collective-permute-start | bytes 393224 | tf_op jit(solution)/shard_map/ppermute | solution.py:283
  21.2 0.0 copy-done.6
  21.2 0.3 pick.1.pick_ref
  21.5 0.0 copy-start.3
  21.5 0.0 copy-start.4
  21.5 1.7 %all-to-all-done.received_ref = bf16[16,144,128]{2,1,0:T(8,128)(2,1)S(1)} async-done(((bf16[16,144,128]{2,1,0:T(8,128)(2,1)}), bf16[16,144,128]{2,1,0:T(8,128)(2,1)S(1)}, u32[]{:S(2)}, u32[]{:S(2)}) %all-to-all-start) | async-done | bytes 589856 | tf_op jit(solution)/shard_map/all_to_all | solution.py:324
  23.1 2.0 %count.1.logcount_ref = f32[8,2,64,512]{3,2,1,0:T(8,128)S(1)} custom-call(bf16[16,144,128]{2,1,0:T(8,128)(2,1)S(1)} %all-to-all-done.received_ref), custom_call_target="tpu_custom_call" | custom-call | tf_op jit(solution)/shard_map/count/pallas_call | solution.py:336
  25.2 0.0 collective-permute-done.3.refs_3_
  25.2 0.0 collective-permute-done.2.refs_2_
  25.2 0.0 collective-permute-done.1.refs_1_
  25.2 2.3 %collective-permute-start.4 = (bf16[512,512]{1,0:T(8,128)(2,1)S(1)}, bf16[512,512]{1,0:T(8,128)(2,1)S(1)}, u32[]{:S(2)}, u32[]{:S(2)}) collective-permute-start(bf16[512,512]{1,0:T(8,128)(2,1)S(1)} %join_near.1.table_ref), channel_id=1, source_target_pairs={{0,1},{1,0},{2,3},{3,2},{4,5},{5,4},{6,7},{7,6},{8,9},{9,8},{10,11... | collective-permute-start | bytes 1572872 | tf_op jit(solution)/shard_map/ppermute | solution.py:286
  27.5 0.0 copy-done.3
  27.5 0.0 copy-done.4
  27.5 2.2 %attend_near.1 = (f32[16,128,128]{2,1,0:T(8,128)S(1)}, f32[16,8,128]{2,1,0:T(8,128)S(1)}) custom-call(bf16[16,144,128]{2,1,0:T(8,128)(2,1)S(1)} %all-to-all-done.received_ref, f32[8,2,64,512]{3,2,1,0:T(8,128)S(1)} %count.1.logcount_ref, bf16[512,512]{1,0:T(8,128)(2,1)S(1)} %join_near.1.table_ref, bf16[512,512]{1,0:T(8,128)(2,1)S(1)} %copy-done.3, ...), custom_call_target="tpu_custom_call" | custom-call | flops 10000000000 | tf_op jit(solution)/shard_map/attend_near/pallas_call | solution.py:358
  29.7 0.0 collective-permute-done.4.table_ref
  29.7 0.0 copy-start
  29.7 0.0 copy-start.1
  29.7 0.0 copy-start.2
  29.7 0.0 copy-start.5
  29.7 0.0 copy-start.7
  29.7 2.4 %attend_far.1 = bf16[16,32,512]{2,1,0:T(8,128)(2,1)S(1)} custom-call(bf16[16,144,128]{2,1,0:T(8,128)(2,1)S(1)} %all-to-all-done.received_ref, f32[8,2,64,512]{3,2,1,0:T(8,128)S(1)} %count.1.logcount_ref, bf16[512,512]{1,0:T(8,128)(2,1)S(1)} %collective-permute-done.4.table_ref, bf16[512,512]{1,0:T(8,128)(2,1)S(1)} %copy-done.3, ...), custom_call_target="tpu_custom_call" | custom-call | tf_op jit(solution)/shard_map/attend_far/pallas_call | solution.py:371
  32.1 15.7 %all_to_all.10 = bf16[16,32,512]{2,1,0:T(8,128)(2,1)S(1)} all-to-all(bf16[16,32,512]{2,1,0:T(8,128)(2,1)S(1)} %attend_far.1), channel_id=1, replica_groups=mesh['region'=16,'shard'=16] {'region'}, dimensions={0} | all-to-all | bytes 1048576 | tf_op jit(solution)/shard_map/all_to_all | solution.py:380
  47.8 0.0 copy-done
  47.8 0.0 copy-done.1
  47.8 0.0 copy-done.2
  47.8 0.0 copy-done.5
  47.8 0.0 copy-done.7
  47.8 2.7 %finish.1 = bf16[256,512]{1,0:T(8,128)(2,1)} custom-call(bf16[256,512]{1,0:T(8,128)(2,1)S(1)} %copy-done, bf16[256,512]{1,0:T(8,128)(2,1)S(1)} %pick.1.pick_ref, bf16[512,512]{1,0:T(8,128)(2,1)S(1)} %bitcast.4, bf16[512,512]{1,0:T(8,128)(2,1)S(1)} %copy-done.5, f32[1,512]{1,0:T(1,128)S(1)} %bitcast.8, bf16[512,2048]{1,0:T(8,128)(2,1)S(1)} %copy-done.1, ...), custom_call_target="tpu_custom_call" | custom-call | tf_op jit(solution)/shard_map/finish/pallas_call | solution.py:383
  (3 shorter events, 0.1 us)
Async XLA Ops:
  0.0 12.2 %copy-start.8 = (bf16[64,512]{1,0:T(8,128)(2,1)S(1)}, bf16[64,512]{1,0:T(8,128)(2,1)}, u32[]{:S(2)}) copy-start(bf16[64,512]{1,0:T(8,128)(2,1)} %refs_0_.4) | copy-start | bytes 196612
  2.9 9.3 %collective-permute-start = (bf16[64,512]{1,0:T(8,128)(2,1)}, bf16[64,512]{1,0:T(8,128)(2,1)S(1)}, u32[]{:S(2)}, u32[]{:S(2)}) collective-permute-start(bf16[64,512]{1,0:T(8,128)(2,1)} %refs_0_.4), channel_id=1, source_target_pairs={{6,0},{7,1},{12,2},{13,3},{10,4},{11,5},{0,6},{1,7},{14,8},{15,9},... | collective-permute-start | bytes 196616 | tf_op jit(solution)/shard_map/ppermute | solution.py:283
  5.4 17.8 %all-to-all-start = ((bf16[16,144,128]{2,1,0:T(8,128)(2,1)}), bf16[16,144,128]{2,1,0:T(8,128)(2,1)S(1)}, u32[]{:S(2)}, u32[]{:S(2)}) async-start(bf16[16,144,128]{2,1,0:T(8,128)(2,1)} %pack_late.1), calls=%async_computation | async-start | bytes 1179648 | tf_op jit(solution)/shard_map/all_to_all | solution.py:324
  12.1 9.0 %copy-start.6 = (s32[256,1]{0,1:T(1,128)S(1)}, s32[256,1]{0,1:T(1,128)}, u32[]{:S(2)}) copy-start(s32[256,1]{0,1:T(1,128)} %param.12) | copy-start | bytes 3076
  12.2 13.0 %collective-permute-start.3 = (bf16[128,512]{1,0:T(8,128)(2,1)S(1)}, bf16[128,512]{1,0:T(8,128)(2,1)S(1)}, u32[]{:S(2)}, u32[]{:S(2)}) collective-permute-start(bf16[128,512]{1,0:T(8,128)(2,1)S(1)} %join_pair.1.after_ref.refs_0_), channel_id=1, source_target_pairs={{4,0},{5,1},{14,2},{15,3},{8,4},{9,5},{2,6},{3,7},{12,8},{13,9},{6... | collective-permute-start | bytes 393224 | tf_op jit(solution)/shard_map/ppermute | solution.py:283
  18.5 6.7 %collective-permute-start.2 = (bf16[128,512]{1,0:T(8,128)(2,1)S(1)}, bf16[128,512]{1,0:T(8,128)(2,1)S(1)}, u32[]{:S(2)}, u32[]{:S(2)}) collective-permute-start(bf16[128,512]{1,0:T(8,128)(2,1)S(1)} %join_pair.1.after_ref.refs_0_), channel_id=1, source_target_pairs={{14,0},{15,1},{0,2},{1,3},{2,4},{3,5},{4,6},{5,7},{6,8},{7,9},{8,1... | collective-permute-start | bytes 393224 | tf_op jit(solution)/shard_map/ppermute | solution.py:283
  18.5 6.7 %collective-permute-start.1 = (bf16[128,512]{1,0:T(8,128)(2,1)S(1)}, bf16[128,512]{1,0:T(8,128)(2,1)S(1)}, u32[]{:S(2)}, u32[]{:S(2)}) collective-permute-start(bf16[128,512]{1,0:T(8,128)(2,1)S(1)} %join_pair.1.after_ref.refs_0_), channel_id=1, source_target_pairs={{2,0},{3,1},{4,2},{5,3},{6,4},{7,5},{8,6},{9,7},{10,8},{11,9},{12,... | collective-permute-start | bytes 393224 | tf_op jit(solution)/shard_map/ppermute | solution.py:283
  21.5 6.0 %copy-start.3 = (bf16[512,512]{1,0:T(8,128)(2,1)S(1)}, bf16[512,512]{1,0:T(8,128)(2,1)}, u32[]{:S(2)}) copy-start(bf16[512,512]{1,0:T(8,128)(2,1)} %w_key_ref.3) | copy-start | bytes 1572868
  21.5 6.0 %copy-start.4 = (bf16[512,512]{1,0:T(8,128)(2,1)S(1)}, bf16[512,512]{1,0:T(8,128)(2,1)}, u32[]{:S(2)}) copy-start(bf16[512,512]{1,0:T(8,128)(2,1)} %w_value_ref.3) | copy-start | bytes 1572868
  25.2 4.4 %collective-permute-start.4 = (bf16[512,512]{1,0:T(8,128)(2,1)S(1)}, bf16[512,512]{1,0:T(8,128)(2,1)S(1)}, u32[]{:S(2)}, u32[]{:S(2)}) collective-permute-start(bf16[512,512]{1,0:T(8,128)(2,1)S(1)} %join_near.1.table_ref), channel_id=1, source_target_pairs={{0,1},{1,0},{2,3},{3,2},{4,5},{5,4},{6,7},{7,6},{8,9},{9,8},{10,11... | collective-permute-start | bytes 1572872 | tf_op jit(solution)/shard_map/ppermute | solution.py:286
  29.7 18.1 %copy-start = (bf16[256,512]{1,0:T(8,128)(2,1)S(1)}, bf16[256,512]{1,0:T(8,128)(2,1)}, u32[]{:S(2)}) copy-start(bf16[256,512]{1,0:T(8,128)(2,1)} %feats_ref.1) | copy-start | bytes 786436
  29.7 18.1 %copy-start.1 = (bf16[512,2048]{1,0:T(8,128)(2,1)S(1)}, bf16[512,2048]{1,0:T(8,128)(2,1)}, u32[]{:S(2)}) copy-start(bf16[512,2048]{1,0:T(8,128)(2,1)} %w_up_ref.1) | copy-start | bytes 6291460
  29.7 18.1 %copy-start.2 = (bf16[2048,512]{1,0:T(8,128)(2,1)S(1)}, bf16[2048,512]{1,0:T(8,128)(2,1)}, u32[]{:S(2)}) copy-start(bf16[2048,512]{1,0:T(8,128)(2,1)} %w_down_ref.1) | copy-start | bytes 6291460
  29.7 18.1 %copy-start.5 = (bf16[512,512]{1,0:T(8,128)(2,1)S(1)}, bf16[512,512]{1,0:T(8,128)(2,1)}, u32[]{:S(2)}) copy-start(bf16[512,512]{1,0:T(8,128)(2,1)} %w_out_ref.1) | copy-start | bytes 1572868
  29.7 18.1 %copy-start.7 = (f32[512]{0:T(512)S(1)}, f32[512]{0:T(512)}, u32[]{:S(2)}) copy-start(f32[512]{0:T(512)} %param.19) | copy-start | bytes 6148
